TPU v7x, 32 devices: a whole 2x2x4 slice. The times are simulated.
32 devices in a mesh: seq: 8 (over z, y), ch: 4 (over x, core).
Axes of the slice: x: 2, y: 2, z: 4, core: 2. Of those that a mesh axis runs over, the one named last changes fastest.
Arguments:
- stream: bfloat16 [2048, 1536], P('seq'), may hold values from -6 to 6
- doc_bounds: int32 [2], replicated, may hold values from 1 to 2047, as said below
- norm_gains: float32 [2, 1536], replicated, may hold values from 0.5 to 1.5
- w_in: bfloat16 [1536, 2, 3072], P(None, None, 'ch'), may hold values from -0.15625 to 0.15625
- chan_vectors: float32 [7, 3072], P(None, 'ch'), may hold values from -7 to 2
- decay_logs: float32 [16, 3072], P(None, 'ch'), may hold values from -14 to 4
- w_x: bfloat16 [3072, 128], P('ch'), may hold values from -0.109375 to 0.109375
- small_gains: float32 [128], replicated, may hold values from 0.5 to 1.5
- w_dt: bfloat16 [96, 3072], P(None, 'ch'), may hold values from -0.625 to 0.625
- w_out: bfloat16 [3072, 1536], P('ch'), may hold values from -0.0546875 to 0.0546875
- w_gate_up: bfloat16 [1536, 2, 4096], P(None, None, 'ch'), may hold values from -0.15625 to 0.15625
- w_down: bfloat16 [4096, 1536], P('ch'), may hold values from -0.09375 to 0.09375
- cotangent: bfloat16 [2048, 1536], P('seq'), may hold values from -6 to 6
Outputs:
- out: bfloat16 [2048, 1536], P('seq')
- stream_grad: float32 [2048, 1536], P('seq')
- norm_gains_grad: float32 [2, 1536], P(None, 'seq')
- w_in_grad: float32 [1536, 2, 3072], P('seq', None, 'ch')
- chan_vectors_grad: float32 [7, 3072], P(None, ('ch', 'seq'))
- decay_logs_grad: float32 [16, 3072], P(None, ('ch', 'seq'))
- w_x_grad: float32 [3072, 128], P(('ch', 'seq'))
- small_gains_grad: float32 [128], P('seq')
- w_dt_grad: float32 [96, 3072], P(None, ('ch', 'seq'))
- w_out_grad: float32 [3072, 1536], P(('ch', 'seq'))
- w_gate_up_grad: float32 [1536, 2, 4096], P('seq', None, 'ch')
- w_down_grad: float32 [4096, 1536], P(('ch', 'seq'))
- stream_rms: float32 [3], replicated
Inputs may be any that keep to these rules, and one draw needn't show every extreme that they name: doc_bounds[0] lies among the first 256 tokens and doc_bounds[1] among the last 256, so the second document runs from the first index of seq to the last.
All inputs are finite; a program needn't handle non-finite values.
Results may differ from a plain program's by a relative error of at most 0.022.
Values may be sent and summed in bfloat16 or wider, within the bound.
A program may use at most 192 MiB of HBM per device.

v0:
```python
import functools
import math

import jax
import jax.numpy as jnp
from jax import lax
from jax.experimental import pallas as pl
from jax.experimental.pallas import tpu as pltpu
from jax.sharding import PartitionSpec as P

f32 = jnp.float32
bf16 = jnp.bfloat16
LOG2E = math.log2(math.e)
LN2 = math.log(2.0)
RESET = 1e30
UNROLL = 8
LANES = 256
VMEM = pl.BlockSpec(memory_space=pltpu.VMEM)


def shape_of(*dims, dtype=f32):
    return jax.ShapeDtypeStruct(dims, dtype)


def cost(us):
    return pl.CostEstimate(flops=int(us * 1e9), bytes_accessed=int(us * 1e6), transcendentals=0)


def widened(column, width):
    return jnp.concatenate([column] * (width // 128), 1)


def folded(values):
    total = values[:, :128]
    for part in range(1, values.shape[1] // 128):
        total = total + values[:, part * 128 : (part + 1) * 128]
    return total


def ahead_end_kernel(step, drive, into, rate, end):
    tokens, width = step.shape
    rates = rate[...]

    def body(index, state):
        first = pl.multiple_of(index * UNROLL, UNROLL)
        steps = step[pl.ds(first, UNROLL), :]
        drives = drive[pl.ds(first, UNROLL), :]
        for k in range(UNROLL):
            decay = jnp.exp2(steps[k : k + 1] * rates)
            state = decay * state + widened(into[first + k], width) * drives[k : k + 1]
        return state

    end[...] = lax.fori_loop(0, tokens // UNROLL, body, jnp.zeros_like(rates))


def ahead_kernel(step, drive, into, out_of, rate, start, scanned, before, end):
    tokens, width = step.shape
    rates = rate[...]

    def body(index, state):
        first = pl.multiple_of(index * UNROLL, UNROLL)
        steps = step[pl.ds(first, UNROLL), :]
        drives = drive[pl.ds(first, UNROLL), :]
        rows = []
        for k in range(UNROLL):
            before[first + k] = state
            decay = jnp.exp2(steps[k : k + 1] * rates)
            state = decay * state + widened(into[first + k], width) * drives[k : k + 1]
            rows.append(
                jnp.sum(widened(out_of[first + k], width) * state, axis=0, keepdims=True)
            )
        scanned[pl.ds(first, UNROLL), :] = jnp.concatenate(rows, 0)
        return state

    end[...] = lax.fori_loop(0, tokens // UNROLL, body, start[...])


def back_end_kernel(step, grad, out_of, rate, end):
    tokens, width = step.shape
    rates = rate[...]

    def body(index, carried):
        first = pl.multiple_of(tokens - UNROLL - index * UNROLL, UNROLL)
        steps = step[pl.ds(first, UNROLL), :]
        grads = grad[pl.ds(first, UNROLL), :]
        for k in reversed(range(UNROLL)):
            decay = jnp.exp2(steps[k : k + 1] * rates)
            carried = decay * (widened(out_of[first + k], width) * grads[k : k + 1] + carried)
        return carried

    end[...] = lax.fori_loop(0, tokens // UNROLL, body, jnp.zeros_like(rates))


def back_kernel(
    step, drive, grad, into, out_of, rate, before, end, start,
    decay_rows, push_rows, into_wide, out_wide, rate_sum,
):
    tokens, width = step.shape
    rates = rate[...]

    @pl.when(pl.program_id(0) == 0)
    def _():
        into_wide[...] = jnp.zeros_like(into_wide)
        out_wide[...] = jnp.zeros_like(out_wide)

    def body(index, carry):
        carried, state, total = carry
        first = pl.multiple_of(tokens - UNROLL - index * UNROLL, UNROLL)
        steps = step[pl.ds(first, UNROLL), :]
        drives = drive[pl.ds(first, UNROLL), :]
        grads = grad[pl.ds(first, UNROLL), :]
        decay_list, push_list = [None] * UNROLL, [None] * UNROLL
        for k in reversed(range(UNROLL)):
            place = first + k
            grad_row = grads[k : k + 1]
            decay = jnp.exp2(steps[k : k + 1] * rates)
            adjoint = widened(out_of[place], width) * grad_row + carried
            carried = decay * adjoint
            out_wide[place] = out_wide[place] + folded(state * grad_row)
            into_wide[place] = into_wide[place] + folded(adjoint * drives[k : k + 1])
            state = before[place]
            share = carried * state
            total = total + share * steps[k : k + 1]
            decay_list[k] = jnp.sum(share * rates, axis=0, keepdims=True)
            push_list[k] = jnp.sum(widened(into[place], width) * adjoint, axis=0, keepdims=True)
        decay_rows[pl.ds(first, UNROLL), :] = jnp.concatenate(decay_list, 0)
        push_rows[pl.ds(first, UNROLL), :] = jnp.concatenate(push_list, 0)
        return (carried, state, total)

    _, _, total = lax.fori_loop(
        0, tokens // UNROLL, body, (start[...], end[...], jnp.zeros_like(rates))
    )
    rate_sum[...] = total


def scan_specs(tokens, states):
    return (
        pl.BlockSpec((tokens, LANES), lambda j: (0, j)),
        pl.BlockSpec((states, LANES), lambda j: (0, j)),
        pl.BlockSpec((tokens, states, 128), lambda j: (0, 0, 0)),
        pl.BlockSpec((tokens, states, LANES), lambda j: (0, 0, j)),
    )


def scan_call(kernel, name, us, channels, in_specs, out_specs, out_shape):
    return pl.pallas_call(
        kernel,
        grid=(channels // LANES,),
        in_specs=in_specs,
        out_specs=out_specs,
        out_shape=out_shape,
        compiler_params=pltpu.CompilerParams(vmem_limit_bytes=48 * 2**20),
        cost_estimate=cost(us),
        name=name,
    )


def ahead_end(step, drive, into, rate):
    (tokens, channels), states = step.shape, rate.shape[0]
    row, st, col, _ = scan_specs(tokens, states)
    return scan_call(
        ahead_end_kernel, "ahead_end", 5, channels, [row, row, col, st], st,
        shape_of(states, channels),
    )(step, drive, into, rate)


def ahead(step, drive, into, out_of, rate, start):
    (tokens, channels), states = step.shape, rate.shape[0]
    row, st, col, hist = scan_specs(tokens, states)
    return scan_call(
        ahead_kernel, "ahead", 10, channels, [row, row, col, col, st, st], [row, hist, st],
        [shape_of(tokens, channels), shape_of(tokens, states, channels), shape_of(states, channels)],
    )(step, drive, into, out_of, rate, start)


def back_end(step, grad, out_of, rate, ties=()):
    (tokens, channels), states = step.shape, rate.shape[0]
    row, st, col, _ = scan_specs(tokens, states)
    return scan_call(
        tied(back_end_kernel, 4, len(ties)), "back_end", 5, channels,
        [row, row, col, st] + [ANY] * len(ties), st, shape_of(states, channels),
    )(step, grad, out_of, rate, *ties)


def back(step, drive, grad, into, out_of, rate, before, end, start):
    (tokens, channels), states = step.shape, rate.shape[0]
    row, st, col, hist = scan_specs(tokens, states)
    wide = shape_of(tokens, states, 128)
    rows = shape_of(tokens, channels)
    return scan_call(
        back_kernel, "back", 16, channels,
        [row, row, row, col, col, st, hist, st, st], [row, row, col, col, st],
        [rows, rows, wide, wide, shape_of(states, channels)],
    )(step, drive, grad, into, out_of, rate, before, end, start)


ANY = pl.BlockSpec(memory_space=pl.ANY)


def tied(kernel, ins, ties):
    def body(*refs):
        return kernel(*refs[:ins], *refs[ins + ties :])

    return body


def met(axis, partners):
    barrier = pltpu.get_barrier_semaphore()
    for partner in partners:
        pl.semaphore_signal(
            barrier, inc=1, device_id={axis: partner}, device_id_type=pl.DeviceIdType.MESH
        )
    pl.semaphore_wait(barrier, len(partners))


def sent(source, target, sends, receives, slot, axis, partner):
    copy = pltpu.make_async_remote_copy(
        src_ref=source,
        dst_ref=target,
        send_sem=sends.at[slot],
        recv_sem=receives.at[slot],
        device_id={axis: partner},
        device_id_type=pl.DeviceIdType.MESH,
    )
    copy.start()
    return copy


def bits_of(count):
    return [1 << k for k in range(count.bit_length() - 1)]


def flipped(me, bit):
    mine = lax.rem(me // bit, 2)
    return mine, me + bit - 2 * bit * mine


def exchange_params(ident):
    return pltpu.CompilerParams(
        collective_id=ident, has_side_effects=True, vmem_limit_bytes=32 * 2**20
    )


def small_sum_kernel(axis, bits, value, total, moving, landed, sends, receives):
    me = lax.axis_index(axis)
    met(axis, [flipped(me, bit)[1] for bit in bits])
    moving[0] = value[...]
    for k, bit in enumerate(bits):
        _, partner = flipped(me, bit)
        copy = sent(moving.at[k], landed.at[k], sends, receives, k, axis, partner)
        copy.wait()
        if k + 1 < len(bits):
            moving[k + 1] = moving[k] + landed[k]
        else:
            total[...] = moving[k] + landed[k]


def small_sum(value, axis, count, ident, name, ties=()):
    bits = bits_of(count)
    slots = pltpu.VMEM((len(bits),) + value.shape, f32)
    return pl.pallas_call(
        tied(functools.partial(small_sum_kernel, axis, bits), 1, len(ties)),
        out_shape=shape_of(*value.shape),
        in_specs=[VMEM] + [ANY] * len(ties),
        out_specs=VMEM,
        scratch_shapes=[slots, slots] + [pltpu.SemaphoreType.DMA((len(bits),))] * 2,
        compiler_params=exchange_params(ident),
        cost_estimate=cost(7),
        name=name,
    )(value, *ties)


def four_sum_kernel(value, total, first, second, moving, sends, receives):
    me = lax.axis_index("ch")
    low, across = flipped(me, 1)
    high, along = flipped(me, 2)
    met("ch", [across, along])
    sent(value.at[:, 1 - low], first, sends, receives, 0, "ch", across).wait()
    moving[...] = (
        value[1 - high, low].astype(f32) + first[1 - high].astype(f32)
    ).astype(bf16)
    copy = sent(moving, second, sends, receives, 1, "ch", along)
    kept = value[high, low].astype(f32) + first[high].astype(f32)
    copy.wait()
    total[high, low] = (kept + second[...].astype(f32)).astype(bf16)
    sent(total.at[high, low], total.at[high, low], sends, receives, 2, "ch", along).wait()
    sent(total.at[:, low], total.at[:, low], sends, receives, 3, "ch", across).wait()


def four_sum(value, ident, name, ties=()):
    rows, columns = value.shape
    part = rows // 4
    result = pl.pallas_call(
        tied(four_sum_kernel, 1, len(ties)),
        out_shape=shape_of(2, 2, part, columns, dtype=bf16),
        in_specs=[VMEM] + [ANY] * len(ties),
        out_specs=VMEM,
        scratch_shapes=[
            pltpu.VMEM((2, part, columns), bf16),
            pltpu.VMEM((part, columns), bf16),
            pltpu.VMEM((part, columns), bf16),
            pltpu.SemaphoreType.DMA((4,)),
            pltpu.SemaphoreType.DMA((4,)),
        ],
        compiler_params=exchange_params(ident),
        cost_estimate=cost(14),
        name=name,
    )(value.reshape(2, 2, part, columns), *ties)
    return result.reshape(rows, columns)


def chain_kernel(forward, bits, state, steps, rate, arriving, moving, landed, sends, receives):
    me = lax.axis_index("seq")
    states = state.shape[0]
    met("seq", [flipped(me, bit)[1] for bit in bits])
    rates = rate[...]
    all_state, all_steps = state[...], steps[...]
    mine_state, mine_steps = jnp.zeros_like(all_state), jnp.zeros_like(all_steps)
    for k, bit in enumerate(bits):
        mine, partner = flipped(me, bit)
        moving[k, :states] = all_state
        moving[k, states:] = all_steps
        sent(moving.at[k], landed.at[k], sends, receives, k, "seq", partner).wait()
        other_state, other_steps = landed[k, :states], landed[k, states:]
        earlier = (mine == 1) if forward else (mine == 0)
        through = jnp.exp2(rates * mine_steps[:1])
        mine_state = jnp.where(earlier, mine_state + through * other_state, mine_state)
        mine_steps = jnp.where(earlier, mine_steps + other_steps, mine_steps)
        after = jnp.exp2(rates * all_steps[:1]) * other_state + all_state
        ahead_of = jnp.exp2(rates * other_steps[:1]) * all_state + other_state
        all_state = jnp.where(earlier, after, ahead_of)
        all_steps = all_steps + other_steps
    arriving[...] = mine_state


def chain(state, step_total, rate, forward, count, ident, name):
    bits = bits_of(count)
    states, channels = state.shape
    slots = pltpu.VMEM((len(bits), states + 8, channels), f32)
    return pl.pallas_call(
        functools.partial(chain_kernel, forward, bits),
        out_shape=shape_of(states, channels),
        in_specs=[VMEM] * 3,
        out_specs=VMEM,
        scratch_shapes=[slots, slots] + [pltpu.SemaphoreType.DMA((len(bits),))] * 2,
        compiler_params=exchange_params(ident),
        cost_estimate=cost(14),
        name=name,
    )(state, step_total, rate)


def last_sums_kernel(bits, parts, flat, own, flat_total, *rest):
    me = lax.axis_index("seq")
    levels = len(bits)
    works, rest = rest[:levels], rest[levels:]
    lows, rest = rest[:levels], rest[levels:]
    lands, rest = rest[:levels], rest[levels:]
    moving, landed, sends, receives, flat_sends, flat_receives = rest
    met("seq", [flipped(me, bit)[1] for bit in bits])
    moving[0] = flat[...]
    for k, bit in enumerate(bits):
        mine, partner = flipped(me, bit)
        source = parts if k == 0 else works[k - 1]
        lows[k][...] = source[:, 1 - mine].astype(bf16)
        copy = sent(lows[k], lands[k], sends, receives, k, "seq", partner)
        flat_copy = sent(moving.at[k], landed.at[k], flat_sends, flat_receives, k, "seq", partner)
        copy.wait()
        summed = source[:, mine] + lands[k][...].astype(f32)
        if k + 1 < levels:
            works[k][...] = summed.reshape(works[k].shape)
        else:
            own[...] = summed.reshape(own.shape)
        flat_copy.wait()
        if k + 1 < levels:
            moving[k + 1] = moving[k] + landed[k]
        else:
            flat_total[...] = moving[k] + landed[k]


def last_sums(parts, flat, count, ident, name, ties=()):
    bits = bits_of(count)
    levels = len(bits)
    rows, columns = parts.shape[0] // count, parts.shape[1]
    halves = [count >> (k + 1) for k in range(levels)]
    works = [pltpu.VMEM((max(half // 2, 1), 2 if half > 1 else 1, rows, columns), f32) for half in halves]
    lows = [pltpu.VMEM((half, rows, columns), bf16) for half in halves]
    slots = pltpu.VMEM((levels,) + flat.shape, f32)
    sems = [pltpu.SemaphoreType.DMA((levels,))] * 4
    return pl.pallas_call(
        tied(functools.partial(last_sums_kernel, bits), 2, len(ties)),
        out_shape=[shape_of(rows, columns), shape_of(*flat.shape)],
        in_specs=[VMEM] * 2 + [ANY] * len(ties),
        out_specs=[VMEM] * 2,
        scratch_shapes=works + lows + lows + [slots, slots] + sems,
        compiler_params=exchange_params(ident),
        cost_estimate=cost(20),
        name=name,
    )(parts.reshape(count // 2, 2, rows, columns), flat, *ties)


def swapped(value, bit, count):
    return lax.ppermute(value, "seq", [(s, s ^ bit) for s in range(count)])


def side(columns, mine, count):
    rows, width = columns.shape
    part = width // count
    blocks = [columns[:, k * part : (k + 1) * part] for k in range(count)]
    return jnp.where(
        mine == 0, jnp.concatenate(blocks[::2], 1), jnp.concatenate(blocks[1::2], 1)
    )


class Scattered:
    def __init__(self, half, count):
        self.count = count
        self.bits = bits_of(count)[1:]
        self.held = half
        self.left = count // 2
        self.step = 0

    def go(self):
        bit = self.bits[self.step]
        self.step += 1
        self.left //= 2
        rows = self.held.reshape(-1, self.held.shape[-1]).shape[0] // (2 * self.left)
        held = self.held.reshape(self.left, 2, rows, self.held.shape[-1])
        mine = (lax.axis_index("seq") // bit) % 2
        self.away = lax.dynamic_index_in_dim(held, 1 - mine, 1, keepdims=False).astype(bf16)
        self.kept = lax.dynamic_index_in_dim(held, mine, 1, keepdims=False)
        self.came = swapped(self.away, bit, self.count)
        self.held = self.kept.astype(f32) + self.came.astype(f32)
        return self.away

    def rest(self):
        while self.step < len(self.bits):
            self.go()
        return self.held.reshape(-1, self.held.shape[-1])


def paired(own_left, own_right, came_left, came_right, count):
    half = jnp.dot(own_left.T, own_right, preferred_element_type=f32) + jnp.dot(
        came_left.T, came_right, preferred_element_type=f32
    )
    return Scattered(half, count)


CHUNK = 32


def sigmoid(values):
    return 1.0 / (1.0 + jnp.exp(-values))


def softplus(values):
    return jnp.maximum(values, 0.0) + jnp.log1p(jnp.exp(-jnp.abs(values)))


def row_doc(places, bounds):
    return (places >= bounds[0]).astype(jnp.int32) + (places >= bounds[1]).astype(jnp.int32)


def tap_mask(places, bounds, offset):
    source = places - offset
    same = row_doc(source, bounds) == row_doc(places, bounds)
    return jnp.where((source >= 0) & same, 1.0, 0.0)


def mean_square(values):
    return jnp.mean(values * values, axis=-1, keepdims=True)


def three_norms(raw, gains, rank, states):
    low, mid, high = raw[:, :rank], raw[:, rank : rank + states], raw[:, rank + states :]
    low_scale = lax.rsqrt(mean_square(low) + 1e-06)
    mid_scale = lax.rsqrt(jnp.maximum(mean_square(mid), 0.1))
    high_scale = lax.rsqrt(jnp.maximum(mean_square(high), 0.1))
    return (
        low * low_scale * gains[:, :rank],
        mid * mid_scale * gains[:, rank : rank + states],
        high * high_scale * gains[:, rank + states :],
    )


def widen(values, wide, first, count):
    states = values.shape[1]
    eye = (
        lax.broadcasted_iota(jnp.int32, (states, states), 0)
        == lax.broadcasted_iota(jnp.int32, (states, states), 1)
    ).astype(f32)
    spread = jnp.sum(values[:, None, :] * eye[None], axis=-1, keepdims=True)
    wide[pl.ds(first, count)] = jnp.broadcast_to(spread, (count, states, 128))


def greeted(axis_partners):
    barrier = pltpu.get_barrier_semaphore()
    for axis, partner in axis_partners:
        pl.semaphore_signal(
            barrier, inc=1, device_id={axis: partner}, device_id_type=pl.DeviceIdType.MESH
        )
    pl.semaphore_wait(barrier, len(axis_partners))


def chained(forward, bits, state, steps, rates, moving, landed, sends, receives, base):
    me = lax.axis_index("seq")
    states = state.shape[0]
    all_state, all_steps = state, steps
    mine_state, mine_steps = jnp.zeros_like(all_state), jnp.zeros_like(all_steps)
    for k, bit in enumerate(bits):
        mine, partner = flipped(me, bit)
        moving[k, :states] = all_state
        moving[k, states:] = all_steps
        sent(moving.at[k], landed.at[k], sends, receives, base + k, "seq", partner).wait()
        other_state, other_steps = landed[k, :states], landed[k, states:]
        earlier = (mine == 1) if forward else (mine == 0)
        through = jnp.exp2(rates * mine_steps[:1])
        mine_state = jnp.where(earlier, mine_state + through * other_state, mine_state)
        mine_steps = jnp.where(earlier, mine_steps + other_steps, mine_steps)
        after = jnp.exp2(rates * all_steps[:1]) * other_state + all_state
        ahead_of = jnp.exp2(rates * other_steps[:1]) * all_state + other_state
        all_state = jnp.where(earlier, after, ahead_of)
        all_steps = all_steps + other_steps
    return mine_state


def forward_kernel(
    bits, bounds, proj, chan, logs, w_x, gains, w_dt, w_out,
    halo, pre_out, low_out, raw_out, step_pre_out, into, out_of, scan_out, gated_out, last_state,
    mixer, hist_out,
    extended, raw_move, raw_land, step, drive, starts, moving, landed, part, first_land,
    second_move, second_land, hist, sends, receives, hist_sem,
):
    tokens, channels = proj.shape[1:]
    rank, states = w_dt.shape[0], logs.shape[0]
    chunks = tokens // CHUNK
    ch_me, me = lax.axis_index("ch"), lax.axis_index("seq")
    seq_count = 1 << len(bits)
    low, across = flipped(ch_me, 1)
    high, along = flipped(ch_me, 2)
    following, previous = lax.rem(me + 1, seq_count), lax.rem(me + seq_count - 1, seq_count)
    greeted(
        [("ch", across), ("ch", along), ("seq", following), ("seq", previous)]
        + [("seq", flipped(me, bit)[1]) for bit in bits]
    )
    halo_copy = sent(
        proj.at[0, pl.ds(tokens - 16, 16)], halo, sends, receives, 0, "seq", following
    )
    rates = -jnp.exp(logs[...]) * LOG2E
    halo_copy.wait()
    extended[0:16] = halo[...].astype(f32)

    def spread(index, _):
        first = pl.multiple_of(index * CHUNK, CHUNK)
        extended[pl.ds(first + 16, CHUNK)] = proj[0, pl.ds(first, CHUNK)].astype(f32)
        return 0

    lax.fori_loop(0, chunks, spread, 0)

    def convolved(index, _):
        first = pl.multiple_of(index * CHUNK, CHUNK)
        places = me * tokens + first + lax.broadcasted_iota(jnp.int32, (CHUNK, 128), 0)
        window = extended[pl.ds(first, CHUNK + 16)]
        summed = chan[4:5]
        for k in range(4):
            mask = widened(tap_mask(places, bounds, 3 - k), channels)
            summed = summed + chan[k : k + 1] * window[13 + k : 13 + k + CHUNK] * mask
        pre_out[pl.ds(first, CHUNK)] = summed
        low_out[pl.ds(first, CHUNK)] = (summed * sigmoid(summed)).astype(bf16)
        return 0

    lax.fori_loop(0, chunks, convolved, 0)
    raw_move[0] = jnp.dot(low_out[...], w_x[...], preferred_element_type=f32)
    sent(raw_move.at[0], raw_land.at[0], sends, receives, 1, "ch", across).wait()
    raw_move[1] = raw_move[0] + raw_land[0]
    sent(raw_move.at[1], raw_land.at[1], sends, receives, 2, "ch", along).wait()

    def stepped(index, total):
        first = pl.multiple_of(index * CHUNK, CHUNK)
        rows = pl.ds(first, CHUNK)
        raw = raw_move[1, rows] + raw_land[1, rows]
        raw_out[rows] = raw
        step_norm, input_norm, output_norm = three_norms(raw, gains[...], rank, states)
        widen(input_norm, into, first, CHUNK)
        widen(output_norm, out_of, first, CHUNK)
        pre = (
            jnp.dot(step_norm.astype(bf16), w_dt[...], preferred_element_type=f32) + chan[5:6]
        )
        step_pre_out[rows] = pre
        size = softplus(pre)
        drive[rows] = size * low_out[rows].astype(f32)
        places = me * tokens + first + lax.broadcasted_iota(jnp.int32, (CHUNK, 128), 0)
        resets = jnp.where((places == bounds[0]) | (places == bounds[1]), RESET, 0.0)
        size = size + widened(resets, channels)
        step[rows] = size
        return total + jnp.sum(size, axis=0, keepdims=True)

    total = lax.fori_loop(0, chunks, stepped, jnp.zeros((1, channels), f32))
    blocks = [slice(j, j + LANES) for j in range(0, channels, LANES)]
    for lanes in blocks:
        block_rates = rates[:, lanes]

        def ended(index, state, lanes=lanes, block_rates=block_rates):
            first = pl.multiple_of(index * UNROLL, UNROLL)
            steps, drives = step[pl.ds(first, UNROLL), lanes], drive[pl.ds(first, UNROLL), lanes]
            for k in range(UNROLL):
                decay = jnp.exp2(steps[k : k + 1] * block_rates)
                state = decay * state + widened(into[first + k], LANES) * drives[k : k + 1]
            return state

        starts[:, lanes] = lax.fori_loop(
            0, tokens // UNROLL, ended, jnp.zeros((states, LANES), f32)
        )
    starts[...] = chained(
        True, bits, starts[...], jnp.broadcast_to(total, (8, channels)), rates, moving, landed,
        sends, receives, 7,
    )
    hist_copies = []
    for number, lanes in enumerate(blocks):
        block_rates = rates[:, lanes]
        skip = chan[6:7, lanes]

        def walked(index, state, lanes=lanes, block_rates=block_rates, skip=skip):
            first = pl.multiple_of(index * UNROLL, UNROLL)
            steps, drives = step[pl.ds(first, UNROLL), lanes], drive[pl.ds(first, UNROLL), lanes]
            rows = []
            for k in range(UNROLL):
                hist[first + k, :, lanes] = state
                decay = jnp.exp2(steps[k : k + 1] * block_rates)
                state = decay * state + widened(into[first + k], LANES) * drives[k : k + 1]
                rows.append(
                    jnp.sum(widened(out_of[first + k], LANES) * state, axis=0, keepdims=True)
                )
            scan_out[pl.ds(first, UNROLL), lanes] = jnp.concatenate(rows, 0)
            return state

        last_state[:, lanes] = lax.fori_loop(0, tokens // UNROLL, walked, starts[:, lanes])
        copy = pltpu.make_async_copy(
            hist.at[:, :, lanes], hist_out.at[:, :, lanes], hist_sem.at[number]
        )
        copy.start()
        hist_copies.append(copy)

    def gate(index, _):
        first = pl.multiple_of(index * CHUNK, CHUNK)
        rows = pl.ds(first, CHUNK)
        scanned = scan_out[rows] + chan[6:7] * low_out[rows].astype(f32)
        scan_out[rows] = scanned
        gate_pre = proj[1, rows].astype(f32)
        gated_out[rows] = (scanned * gate_pre * sigmoid(gate_pre)).astype(bf16)
        return 0

    lax.fori_loop(0, chunks, gate, 0)
    quarter = tokens // 4
    width = w_out.shape[1]

    def mixed(index, _):
        first = pl.multiple_of(index * 512, 512)
        product = jnp.dot(
            gated_out[...], w_out[:, pl.ds(first, 512)], preferred_element_type=f32
        ).astype(bf16)
        for k in range(4):
            part[k // 2, k % 2, :, pl.ds(first, 512)] = product[k * quarter : (k + 1) * quarter]
        return 0

    lax.fori_loop(0, width // 512, mixed, 0)
    four_summed(
        part, mixer, first_land, second_land, second_move, sends, receives, 3, low, across, high,
        along,
    )
    for copy in hist_copies:
        copy.wait()


def four_summed(
    value, total, first, second, moving, sends, receives, base, low, across, high, along
):
    sent(value.at[:, 1 - low], first, sends, receives, base, "ch", across).wait()
    moving[...] = (
        value[1 - high, low].astype(f32) + first[1 - high].astype(f32)
    ).astype(bf16)
    copy = sent(moving, second, sends, receives, base + 1, "ch", along)
    kept = value[high, low].astype(f32) + first[high].astype(f32)
    copy.wait()
    total[high, low] = (kept + second[...].astype(f32)).astype(bf16)
    own = total.at[high, low]
    sent(own, own, sends, receives, base + 2, "ch", along).wait()
    both = total.at[:, low]
    sent(both, both, sends, receives, base + 3, "ch", across).wait()


def mixer_forward(bounds, proj, chan, logs, w_x, gains, w_dt, w_out, count, ident):
    bits = bits_of(count)
    _, tokens, channels = proj.shape
    states, rank, width = logs.shape[0], w_dt.shape[0], w_out.shape[1]
    quarter, narrow = tokens // 4, w_x.shape[1]
    rows = shape_of(tokens, channels)
    low_rows = shape_of(tokens, channels, dtype=bf16)
    wide = shape_of(tokens, states, 128)
    slots = pltpu.VMEM((len(bits), states + 8, channels), f32)
    raws = pltpu.VMEM((2, tokens, narrow), f32)
    out = pl.pallas_call(
        functools.partial(forward_kernel, bits),
        out_shape=[
            shape_of(16, channels, dtype=bf16), rows, low_rows, shape_of(tokens, narrow), rows,
            wide, wide, rows, low_rows, shape_of(states, channels),
            shape_of(2, 2, quarter, width, dtype=bf16), shape_of(tokens, states, channels),
        ],
        in_specs=[pl.BlockSpec(memory_space=pltpu.SMEM)] + [VMEM] * 7,
        out_specs=[VMEM] * 11 + [ANY],
        scratch_shapes=[
            pltpu.VMEM((tokens + 16, channels), f32), raws, raws,
            pltpu.VMEM((tokens, channels), f32), pltpu.VMEM((tokens, channels), f32),
            pltpu.VMEM((states, channels), f32), slots, slots,
            pltpu.VMEM((2, 2, quarter, width), bf16), pltpu.VMEM((2, quarter, width), bf16),
            pltpu.VMEM((quarter, width), bf16), pltpu.VMEM((quarter, width), bf16),
            pltpu.VMEM((tokens, states, channels), f32),
            pltpu.SemaphoreType.DMA((7 + len(bits),)), pltpu.SemaphoreType.DMA((7 + len(bits),)),
            pltpu.SemaphoreType.DMA((channels // LANES,)),
        ],
        compiler_params=pltpu.CompilerParams(
            collective_id=ident, has_side_effects=True, vmem_limit_bytes=56 * 2**20
        ),
        cost_estimate=cost(6),
        name="mixer_forward",
    )(bounds, proj, chan, logs, w_x, gains, w_dt, w_out)
    out = list(out)
    out[10] = out[10].reshape(tokens, width)
    return out


def passed_along(value, axis, steps):
    count = lax.axis_size(axis)
    leading, last = (max(0, -steps), min(count, count - steps))
    return lax.ppermute(value, axis, [(source, source + steps) for source in range(leading, last)])


def rms_gain(values, gain_row):
    return values * lax.rsqrt(jnp.mean(values * values, axis=-1, keepdims=True) + 1e-06) * gain_row


def rms_floor(values, gain_row):
    return (
        values
        * lax.rsqrt(jnp.maximum(jnp.mean(values * values, axis=-1, keepdims=True), 0.1))
        * gain_row
    )


def norm_three(raw_proj, gains_small, step_rank):
    state_width = (raw_proj.shape[1] - step_rank) // 2
    step_norm = rms_gain(raw_proj[:, :step_rank], gains_small[:step_rank])
    input_norm = rms_floor(
        raw_proj[:, step_rank : step_rank + state_width],
        gains_small[step_rank : step_rank + state_width],
    )
    output_norm = rms_floor(
        raw_proj[:, step_rank + state_width :], gains_small[step_rank + state_width :]
    )
    return (step_norm, input_norm, output_norm)


def doc_number(places, bounds):
    return (places >= bounds[0]).astype(jnp.int32) + (places >= bounds[1]).astype(jnp.int32)


def conv_masks(places, bounds):
    own_doc = doc_number(places, bounds)
    mask_rows = []
    for offset in range(4):
        source = places - (3 - offset)
        mask_rows.append(((source >= 0) & (doc_number(source, bounds) == own_doc)).astype(f32))
    return jnp.stack(mask_rows, 0)


def conv_silu(extended, kernel, tap_masks):
    length = tap_masks.shape[1]
    summed = kernel[4]
    for offset in range(4):
        summed = (
            summed
            + kernel[offset] * extended[offset : offset + length] * tap_masks[offset][:, None]
        )
    return jax.nn.silu(summed)


def gating(scan_out, gate_pre):
    return scan_out * jax.nn.silu(gate_pre)


def swiglu(gate_up):
    return jax.nn.silu(gate_up[:, 0]) * gate_up[:, 1]


def local(
    seq_count,
    ch_count,
    stream,
    doc_bounds,
    norm_gains,
    w_in,
    chan_vectors,
    decay_logs,
    w_x,
    small_gains,
    w_dt,
    w_out,
    w_gate_up,
    w_down,
    cotangent,
):
    tok_rows, width = stream.shape
    step_rank = w_dt.shape[0]
    states, channels = decay_logs.shape
    first_row = lax.axis_index("seq") * tok_rows
    places = first_row + jnp.arange(tok_rows, dtype=jnp.int32)
    tap_masks = conv_masks(places, doc_bounds)
    resets = ((places == doc_bounds[0]) | (places == doc_bounds[1])).astype(f32) * RESET

    stream_in = stream.astype(f32)
    normed_one, norm_one_back = jax.vjp(rms_gain, stream_in, norm_gains[0])
    normed_low = normed_one.astype(bf16)
    in_proj = jnp.einsum("td,dke->kte", normed_low, w_in, preferred_element_type=f32).astype(bf16)
    (
        halo, pre_conv, conv_low, raw_proj, step_pre, into, out_of, scan_out, gated_low,
        last_state, mixer_low, before,
    ) = mixer_forward(
        doc_bounds, in_proj, chan_vectors, decay_logs, w_x, small_gains[None], w_dt, w_out,
        seq_count, 1,
    )
    gate_pre = in_proj[1].astype(f32)
    extended = jnp.concatenate([halo[13:], in_proj[0]], 0).astype(f32)
    _, conv_back = jax.vjp(
        functools.partial(conv_silu, tap_masks=tap_masks), extended, chan_vectors[:5]
    )
    conv_used = conv_low.astype(f32)
    (step_norm, input_norm, output_norm), norm_three_back = jax.vjp(
        functools.partial(norm_three, step_rank=step_rank), raw_proj, small_gains
    )
    step_low = step_norm.astype(bf16)
    step_size = jax.nn.softplus(step_pre)
    step_reset = step_size + resets[:, None]
    decay_rate = -jnp.exp(decay_logs)
    rate_two = decay_rate * LOG2E
    drive_term = step_size * conv_used
    step_total = jnp.broadcast_to(jnp.sum(step_reset, axis=0)[None], (8, channels))
    _, gate_back = jax.vjp(gating, scan_out, gate_pre)
    mixer_out = mixer_low.astype(f32)
    middle = stream_in + mixer_out
    normed_two, norm_two_back = jax.vjp(rms_gain, middle, norm_gains[1])
    normed_two_low = normed_two.astype(bf16)
    gate_up = jnp.einsum("td,dkf->tkf", normed_two_low, w_gate_up, preferred_element_type=f32)
    hidden_act, act_back = jax.vjp(swiglu, gate_up)
    hidden_low = hidden_act.astype(bf16)

    grad_out = cotangent.astype(f32)
    mine = lax.axis_index("seq") % 2
    sides = functools.partial(side, count=seq_count)
    pair = functools.partial(swapped, bit=1, count=seq_count)
    one_own, one_came = sides(normed_low, mine), pair(sides(normed_low, 1 - mine))
    two_own, two_came = sides(normed_two_low, mine), pair(sides(normed_two_low, 1 - mine))
    gated_own, gated_came = sides(gated_low, mine), pair(sides(gated_low, 1 - mine))
    hidden_own, hidden_came = sides(hidden_low, mine), pair(sides(hidden_low, 1 - mine))
    cotangent_came = pair(cotangent)
    hidden_grad = jnp.einsum("td,fd->tf", cotangent, w_down, preferred_element_type=f32)
    (gate_up_grad,) = act_back(hidden_grad)
    gate_up_low = gate_up_grad.astype(bf16)
    normed_two_part = jnp.einsum(
        "tkf,dkf->td", gate_up_low, w_gate_up, preferred_element_type=f32
    )
    gate_up_flat = gate_up_low.reshape(tok_rows, -1)
    gate_up_came = pair(gate_up_flat)
    down_sum = paired(hidden_own, cotangent, hidden_came, cotangent_came, seq_count)
    down_away = down_sum.go()
    normed_two_grad = four_sum(
        normed_two_part.astype(bf16), 3, "normed_two_sum", ties=[down_away]
    ).astype(f32)
    gate_up_sum = paired(two_own, gate_up_flat, two_came, gate_up_came, seq_count)
    gate_up_away = gate_up_sum.go()
    middle_part, gain_two_grad = norm_two_back(normed_two_grad)
    middle_grad = grad_out + middle_part
    middle_low = middle_grad.astype(bf16)
    middle_came = pair(middle_low)
    gated_grad = jnp.einsum("td,ed->te", middle_low, w_out, preferred_element_type=f32)
    scan_grad, gate_pre_grad = gate_back(gated_grad)
    gate_pre_low = gate_pre_grad.astype(bf16)
    gate_pre_came = pair(gate_pre_low)

    left_total = back_end(
        step_reset, scan_grad, out_of, rate_two, ties=[gate_up_away, gate_pre_low]
    )
    returning = chain(left_total, step_total, rate_two, False, seq_count, 4, "chain_back")
    decay_rows, push_rows, into_wide, out_wide, rate_sum = back(
        step_reset, drive_term, scan_grad, into, out_of, rate_two, before, last_state, returning
    )

    out_sum = paired(gated_own, middle_low, gated_came, middle_came, seq_count)
    out_away = out_sum.go()
    gate_in_sum = paired(one_own, gate_pre_low, one_came, gate_pre_came, seq_count)
    gate_in_away = gate_in_sum.go()
    gate_up_next = gate_up_sum.go()
    down_next = down_sum.go()
    step_grads = LN2 * decay_rows + push_rows * conv_used
    conv_total = push_rows * step_size + chan_vectors[6] * scan_grad
    skip_grad = jnp.sum(scan_grad * conv_used, axis=0)
    step_pre_low = (step_grads * jax.nn.sigmoid(step_pre)).astype(bf16)
    bias_grad = jnp.sum(step_pre_low.astype(f32), axis=0)
    step_norm_part = jnp.einsum("te,re->tr", step_pre_low, w_dt, preferred_element_type=f32)
    norm_grads = small_sum(
        jnp.concatenate(
            [step_norm_part, jnp.sum(into_wide, axis=-1), jnp.sum(out_wide, axis=-1)], 1
        ),
        "ch",
        ch_count,
        6,
        "norm_grads_sum",
        ties=[out_away, gate_in_away, gate_up_next, down_next],
    )
    raw_grad, small_grad = norm_three_back(
        (
            norm_grads[:, :step_rank],
            norm_grads[:, step_rank : step_rank + states],
            norm_grads[:, step_rank + states :],
        )
    )
    raw_low = raw_grad.astype(bf16)
    conv_total = conv_total + jnp.einsum("tk,ek->te", raw_low, w_x, preferred_element_type=f32)
    extended_grad, kernel_grad = conv_back(conv_total)
    edge_grad = passed_along(extended_grad[:3], "seq", -1)
    conv_in_grad = extended_grad[3:].at[tok_rows - 3 :].add(edge_grad)
    conv_in_low = conv_in_grad.astype(bf16)
    conv_in_came = pair(conv_in_low)
    out_next = out_sum.go()
    gate_in_next = gate_in_sum.go()
    normed_one_part = jnp.einsum(
        "tke,dke->td",
        jnp.stack([conv_in_low, gate_pre_low], 1),
        w_in,
        preferred_element_type=f32,
    )
    normed_one_grad = four_sum(
        normed_one_part.astype(bf16), 7, "normed_one_sum", ties=[out_next, gate_in_next]
    ).astype(f32)
    conv_in_sum = paired(one_own, conv_in_low, one_came, conv_in_came, seq_count)
    conv_in_away = conv_in_sum.go()

    feed_part = jnp.dot(hidden_low, w_down, preferred_element_type=f32)
    feed_out = four_sum(feed_part.astype(bf16), 5, "feed_sum", ties=[conv_in_away]).astype(f32)
    result = middle + feed_out
    squares = jnp.stack(
        [jnp.sum(result * result), jnp.sum(mixer_out * mixer_out), jnp.sum(feed_out * feed_out)]
    )
    out_rows_all = result.astype(bf16)
    stream_part, gain_one_grad = norm_one_back(normed_one_grad)
    stream_grad = middle_grad + stream_part

    grad_x = jnp.dot(conv_low.T, raw_low, preferred_element_type=f32)
    grad_dt = jnp.dot(step_pre_low.T, step_low, preferred_element_type=f32)
    small_rows = jnp.concatenate(
        [rate_sum * decay_rate, kernel_grad, bias_grad[None], skip_grad[None]], 0
    )
    narrow = step_rank + grad_x.shape[1] + small_rows.shape[0]
    padding = -narrow % 128
    columns_all = jnp.concatenate(
        [grad_x, grad_dt, small_rows.T, jnp.zeros((channels, padding), f32)], 1
    )

    def as_row(values):
        return jnp.pad(values, (0, width - values.shape[0]))[None]

    flat = jnp.concatenate(
        [
            gain_one_grad[None],
            gain_two_grad[None],
            as_row(small_grad),
            as_row(squares),
            jnp.zeros((4, width), f32),
        ],
        0,
    )
    conv_in_next = conv_in_sum.go()
    own, flat_total = last_sums(
        columns_all, flat, seq_count, 8, "last_sums", ties=[conv_in_next]
    )
    conv_in_part, gate_in_part = conv_in_sum.rest(), gate_in_sum.rest()
    out_part, gate_up_part, down_part = out_sum.rest(), gate_up_sum.rest(), down_sum.rest()
    at = grad_x.shape[1]
    x_part = own[:, :at]
    dt_part = own[:, at : at + step_rank].T
    at += step_rank
    decay_out = own[:, at : at + states].T
    at += states
    chan_part = own[:, at : at + 7].T
    me = lax.axis_index("seq")
    gains_part = lax.dynamic_slice_in_dim(
        flat_total[:2], me * (width // seq_count), width // seq_count, 1
    )
    small_width = small_gains.shape[0] // seq_count
    small_part = lax.dynamic_slice_in_dim(flat_total[2], me * small_width, small_width, 0)
    rms_values = jnp.sqrt(flat_total[3, :3] / (tok_rows * seq_count * width))
    in_part = jnp.stack([conv_in_part, gate_in_part], 1)
    return (
        out_rows_all,
        stream_grad,
        gains_part,
        in_part,
        chan_part,
        decay_out,
        x_part,
        small_part,
        dt_part,
        out_part,
        gate_up_part.reshape(gate_up_part.shape[0], 2, -1),
        down_part,
        rms_values,
    )


def solution(mesh):
    in_specs = (
        P("seq", None),
        P(),
        P(),
        P(None, None, "ch"),
        P(None, "ch"),
        P(None, "ch"),
        P("ch", None),
        P(),
        P(None, "ch"),
        P("ch", None),
        P(None, None, "ch"),
        P("ch", None),
        P("seq", None),
    )
    out_specs = (
        P("seq", None),
        P("seq", None),
        P(None, "seq"),
        P("seq", None, "ch"),
        P(None, ("ch", "seq")),
        P(None, ("ch", "seq")),
        P(("ch", "seq"), None),
        P("seq"),
        P(None, ("ch", "seq")),
        P(("ch", "seq"), None),
        P("seq", None, "ch"),
        P(("ch", "seq"), None),
        P(),
    )
    return jax.shard_map(
        functools.partial(local, mesh.shape["seq"], mesh.shape["ch"]),
        mesh=mesh,
        in_specs=in_specs,
        out_specs=out_specs,
        check_vma=False,
    )
```

profile of v0, /device:TPU:0, one launch (start us, length us, event | category | flops | bytes accessed | tf_op | source)
XLA Modules:
  0.0 446.7 jit_solution(3073535476371635456)
XLA Ops:
  0.7 3.0 collective-permute-start.1
  7.3 4.9 %fusion.36.proj = bf16[2,256,768]{2,1,0:T(8,128)(2,1)} fusion(bf16[1536,2,768]{2,1,0:T(2,128)(2,1)} %param.18, bf16[256,1536]{1,0:T(8,128)(2,1)S(1)} %fusion.24), kind=kOutput, calls=%fused_computation.58 | convolution fusion | flops 1208352768 | bytes 6291456 | tf_op jit(solution)/shard_map/td,dke->kte/dot_general | solution.py:822
  12.2 65.2 %mixer_forward.1 = (bf16[16,768]{1,0:T(8,128)(2,1)}, f32[256,768]{1,0:T(8,128)}, bf16[256,768]{1,0:T(8,128)(2,1)}, f32[256,128]{1,0:T(8,128)}, f32[256,768]{1,0:...) custom-call(s32[2]{0:T(128)} %bounds.1, ...), custom_call_target="tpu_custom_call" | custom-call | flops 6000000000 | bytes 6000000 | tf_op jit(solution)/shard_map/mixer_forward/pallas_call | solution.py:701
  79.3 5.0 %fusion.2 = f32[256,2,1024]{2,0,1:T(8,128)S(1)} fusion(bf16[1536,2,1024]{2,1,0:T(2,128)(2,1)} %param.25, bf16[256,1536]{1,0:T(8,128)(2,1)S(1)} %multiply_convert_fusion), kind=kOutput, calls=%fused_computation.2 | convolution fusion | flops 1610612736 | bytes 9175040 | tf_op jit(solution)/shard_map/td,dkf->tkf/dot_general | solution.py:851
  99.6 6.3 %fusion.14 = bf16[256,1536]{1,0:T(8,128)(2,1)} fusion(bf16[256,2,1024]{2,0,1:T(8,128)(2,1)} %add_convert_fusion, bf16[1536,2,1024]{2,1,0:T(2,128)(2,1)} %param.25), kind=kOutput, calls=%fused_computation.20 | convolution fusion | flops 1611005952 | bytes 8126464 | tf_op jit(solution)/shard_map/tkf,dkf->td/dot_general | solution.py:867
  114.9 3.0 convolution_convert_fusion
  136.2 15.8 %normed_two_sum.1 = bf16[2,2,64,1536]{3,2,1,0:T(8,128)(2,1)S(1)} custom-call(bf16[2,2,64,1536]{3,2,1,0:T(8,128)(2,1)S(1)} %bitcast.196, bf16[2,128,1536]{2,1,0:T(8,128)(2,1)} %fusion.56.refs_1_), custom_call_target="tpu_custom_call" | custom-call | flops 14000000000 | bytes 14000000 | tf_op jit(solution)/shard_map/normed_two_sum/pallas_call | solution.py:293
  155.6 3.0 fusion.46
  158.7 3.5 fusion.75
  162.9 3.5 fusion.72
  177.0 26.1 %chain_back.1.start = f32[16,768]{1,0:T(8,128)S(1)} custom-call(f32[16,768]{1,0:T(8,128)S(1)} %back_end.1.state, f32[8,768]{1,0:T(8,128)S(1)} %broadcast_in_dim.68.steps, f32[16,768]{1,0:T(8,128)S(1)} %fusion.80.refs_3_.rate), custom_call_target="tpu_custom_call" | custom-call | flops 14000000000 | bytes 14000000 | tf_op jit(solution)/shard_map/chain_back/pallas_call | solution.py:340
  203.1 15.2 %back.1 = (f32[256,768]{1,0:T(8,128)S(1)}, f32[256,768]{1,0:T(8,128)S(1)}, f32[256,16,128]{2,1,0:T(8,128)S(1)}, f32[256,16,128]{2,1,0:T(8,128)}, f32[16,768]{1,0:T(8,128)S(1)}) custom-call(f32[256,768]{1,0:T(8,128)S(1)} %get-tuple-element.131.refs_0_.step, f32[256,768]{1,0:T(8,128)S(1)} %get-tuple-element.149.drive, ...), custom_call_target="tpu_custom_call" | custom-call | flops 16000000000 | bytes 16000000 | tf_op jit(solution)/shard_map/back/pallas_call | solution.py:190
  231.9 3.2 collective-permute-start.19
  235.1 50.0 %collective-permute-done.13 = bf16[2,192,768]{2,1,0:T(8,128)(2,1)S(1)} collective-permute-done((bf16[2,192,768]{2,1,0:T(8,128)(2,1)S(1)}, bf16[2,192,768]{2,1,0:T(8,128)(2,1)S(1)}, u32[]{:S(2)}, u32[]{:S(2)}) %collective-permute-start.13) | collective-permute-done | bytes 589856 | tf_op jit(solution)/shard_map/ppermute | solution.py:402
  285.3 9.5 %collective-permute-done.12 = bf16[2,96,1536]{2,1,0:T(8,128)(2,1)S(1)} collective-permute-done((bf16[2,96,1536]{2,1,0:T(8,128)(2,1)S(1)}, bf16[2,96,1536]{2,1,0:T(8,128)(2,1)S(1)}, u32[]{:S(2)}, u32[]{:S(2)}) %collective-permute-start.12) | collective-permute-done | bytes 589856 | tf_op jit(solution)/shard_map/ppermute | solution.py:402
  296.5 16.0 %collective-permute-done.16 = bf16[1,192,768]{2,1,0:T(8,128)(2,1)S(1)} collective-permute-done((bf16[1,192,768]{2,1,0:T(8,128)(2,1)S(1)}, bf16[1,192,768]{2,1,0:T(8,128)(2,1)S(1)}, u32[]{:S(2)}, u32[]{:S(2)}) %collective-permute-start.16) | collective-permute-done | bytes 294944 | tf_op jit(solution)/shard_map/ppermute | solution.py:402
  320.4 7.1 %norm_grads_sum.1 = f32[256,128]{1,0:T(8,128)S(1)} custom-call(f32[256,128]{1,0:T(8,128)S(1)} %pad_maximum_fusion.9.refs_0_, bf16[2,96,1536]{2,1,0:T(8,128)(2,1)S(1)} %fusion.63.refs_1_, bf16[2,192,768]{2,1,0:T(8,128)(2,1)S(1)} %fusion.64.refs_2_, bf16[1,192,2048]{2,1,0:T(8,128)(2,1)S(1)} %dynamic-slice_convert_fusion.refs_3_, ...), custom_call_target="tpu_custom_call" | custom-call | flops 7000000000 | bytes 7000000 | tf_op jit(solution)/shard_map/norm_grads_sum/pallas_call | solution.py:261
  341.1 14.5 %collective-permute-start.11 = (bf16[256,768]{1,0:T(8,128)(2,1)S(1)}, bf16[256,768]{1,0:T(8,128)(2,1)S(1)}, u32[]{:S(2)}, u32[]{:S(2)}) collective-permute-start(bf16[256,768]{1,0:T(8,128)(2,1)S(1)} %scatter-add.4), channel_id=1, source_target_pairs={{0,4},{4,0},{8,12},{12,8},{16,20},{20,16},{24,28},{28,24},{1,5},{5... | collective-permute-start | bytes 1179656 | tf_op jit(solution)/shard_map/ppermute | solution.py:402
  355.6 3.9 fusion.17
  359.5 16.7 %normed_one_sum.1 = bf16[2,2,64,1536]{3,2,1,0:T(8,128)(2,1)S(1)} custom-call(bf16[2,2,64,1536]{3,2,1,0:T(8,128)(2,1)S(1)} %bitcast.197, bf16[1,96,1536]{2,1,0:T(8,128)(2,1)S(1)} %dynamic-slice_convert_fusion.4.refs_1_, bf16[1,192,768]{2,1,0:T(8,128)(2,1)S(1)} %dynamic-slice_convert_fusion.3.refs_2_), custom_call_target="tpu_custom_call" | custom-call | flops 14000000000 | bytes 14000000 | tf_op jit(solution)/shard_map/normed_one_sum/pallas_call | solution.py:293
  382.3 15.7 %feed_sum.1 = bf16[2,2,64,1536]{3,2,1,0:T(8,128)(2,1)S(1)} custom-call(bf16[2,2,64,1536]{3,2,1,0:T(8,128)(2,1)S(1)} %bitcast.195, bf16[2,192,768]{2,1,0:T(8,128)(2,1)S(1)} %fusion.65.refs_1_), custom_call_target="tpu_custom_call" | custom-call | flops 14000000000 | bytes 14000000 | tf_op jit(solution)/shard_map/feed_sum/pallas_call | solution.py:293
  406.3 3.0 convert_add_fusion.1
  409.4 3.4 reshape_reshape.3
  414.3 24.1 %last_sums.1 = (f32[96,256]{1,0:T(8,128)S(1)}, f32[8,1536]{1,0:T(8,128)S(1)}) custom-call(f32[4,2,96,256]{3,2,1,0:T(8,128)S(1)} %bitcast.194, f32[8,1536]{1,0:T(8,128)S(1)} %concatenate.61.refs_1_, bf16[1,192,768]{2,1,0:T(8,128)(2,1)S(1)} %dynamic-slice_convert_fusion.2.refs_2_), custom_call_target="tpu_custom_call" | custom-call | flops 20000000000 | bytes 20000000 | tf_op jit(solution)/shard_map/last_sums/pallas_call | solution.py:389
  (419 shorter events, 122.0 us)
Async XLA Ops:
  0.6 83.7 %copy-start = (bf16[1024,1536]{1,0:T(8,128)(2,1)S(1)}, bf16[1024,1536]{1,0:T(8,128)(2,1)}, u32[]{:S(2)}) copy-start(bf16[1024,1536]{1,0:T(8,128)(2,1)} %param.26) | copy-start | bytes 9437188
  0.7 132.0 %collective-permute-start.1 = (bf16[256,1536]{1,0:T(8,128)(2,1)}, bf16[256,1536]{1,0:T(8,128)(2,1)}, u32[]{:S(2)}, u32[]{:S(2)}) collective-permute-start(bf16[256,1536]{1,0:T(8,128)(2,1)} %param.27), channel_id=1, source_target_pairs={{0,4},{4,0},{8,12},{12,8},{16,20},{20,16},{24,28},{28,24},{1,5},{5... | collective-permute-start | bytes 2359304 | tf_op jit(solution)/shard_map/ppermute | solution.py:402
  12.2 65.2 %copy-start.12 = (bf16[256,1536]{1,0:T(8,128)(2,1)S(1)}, bf16[256,1536]{1,0:T(8,128)(2,1)}, u32[]{:S(2)}) copy-start(bf16[256,1536]{1,0:T(8,128)(2,1)} %param.15) | copy-start | bytes 2359300
  86.8 45.7 %collective-permute-start = (bf16[256,512]{1,0:T(8,128)(2,1)}, bf16[256,512]{1,0:T(8,128)(2,1)}, u32[]{:S(2)}, u32[]{:S(2)}) collective-permute-start(bf16[256,512]{1,0:T(8,128)(2,1)} %broadcast_select_fusion.3), channel_id=1, source_target_pairs={{0,4},{4,0},{8,12},{12,8},{16,20},{20,16},{24,28},{28,24},{1,5},{5... | collective-permute-start | bytes 786440 | tf_op jit(solution)/shard_map/ppermute | solution.py:402
  88.8 77.6 %collective-permute-start.2 = (bf16[256,768]{1,0:T(8,128)(2,1)}, bf16[256,768]{1,0:T(8,128)(2,1)}, u32[]{:S(2)}, u32[]{:S(2)}) collective-permute-start(bf16[256,768]{1,0:T(8,128)(2,1)} %broadcast_select_fusion.1), channel_id=1, source_target_pairs={{0,4},{4,0},{8,12},{12,8},{16,20},{20,16},{24,28},{28,24},{1,5},{5... | collective-permute-start | bytes 1179656 | tf_op jit(solution)/shard_map/ppermute | solution.py:402
  94.5 73.9 %collective-permute-start.3 = (bf16[256,2048]{0,1:T(8,128)(2,1)}, bf16[256,2048]{0,1:T(8,128)(2,1)}, u32[]{:S(2)}, u32[]{:S(2)}) collective-permute-start(bf16[256,2048]{0,1:T(8,128)(2,1)} %bitcast.208), channel_id=1, source_target_pairs={{0,4},{4,0},{8,12},{12,8},{16,20},{20,16},{24,28},{28,24},{1,5},{5... | collective-permute-start | bytes 3145736 | tf_op jit(solution)/shard_map/ppermute | solution.py:402
  97.6 130.7 %collective-permute-start.4 = (bf16[256,384]{1,0:T(8,128)(2,1)}, bf16[256,384]{1,0:T(8,128)(2,1)}, u32[]{:S(2)}, u32[]{:S(2)}) collective-permute-start(bf16[256,384]{1,0:T(8,128)(2,1)} %broadcast_select_fusion.4), channel_id=1, source_target_pairs={{0,4},{4,0},{8,12},{12,8},{16,20},{20,16},{24,28},{28,24},{1,5},{5... | collective-permute-start | bytes 589832 | tf_op jit(solution)/shard_map/ppermute | solution.py:402
  132.5 90.9 %collective-permute-start.6 = (bf16[256,768]{1,0:T(8,128)(2,1)}, bf16[256,768]{1,0:T(8,128)(2,1)}, u32[]{:S(2)}, u32[]{:S(2)}) collective-permute-start(bf16[256,768]{1,0:T(8,128)(2,1)} %broadcast_select_fusion), channel_id=1, source_target_pairs={{0,4},{4,0},{8,12},{12,8},{16,20},{20,16},{24,28},{28,24},{1,5},{5... | collective-permute-start | bytes 1179656 | tf_op jit(solution)/shard_map/ppermute | solution.py:402
  135.5 94.9 %collective-permute-start.9 = (bf16[2,128,1536]{2,1,0:T(8,128)(2,1)}, bf16[2,128,1536]{2,1,0:T(8,128)(2,1)}, u32[]{:S(2)}, u32[]{:S(2)}) collective-permute-start(bf16[2,128,1536]{2,1,0:T(8,128)(2,1)} %fusion.56.refs_1_), channel_id=1, source_target_pairs={{0,8},{4,12},{8,0},{12,4},{16,24},{20,28},{24,16},{28,20},{1,9},{5... | collective-permute-start | bytes 2359304 | tf_op jit(solution)/shard_map/ppermute | solution.py:402
  158.6 44.5 %copy-start.8 = (f32[256,768]{1,0:T(8,128)}, f32[256,768]{1,0:T(8,128)S(1)}, u32[]{:S(2)}) copy-start(f32[256,768]{1,0:T(8,128)S(1)} %get-tuple-element.129.refs_1_.grad) | copy-start | bytes 2359300
  166.4 61.9 %collective-permute-start.5 = (bf16[256,1536]{1,0:T(8,128)(2,1)}, bf16[256,1536]{1,0:T(8,128)(2,1)}, u32[]{:S(2)}, u32[]{:S(2)}) collective-permute-start(bf16[256,1536]{1,0:T(8,128)(2,1)} %fusion.97), channel_id=1, source_target_pairs={{0,4},{4,0},{8,12},{12,8},{16,20},{20,16},{24,28},{28,24},{1,5},{5... | collective-permute-start | bytes 2359304 | tf_op jit(solution)/shard_map/ppermute | solution.py:402
  168.4 55.2 %collective-permute-start.7 = (bf16[256,768]{1,0:T(8,128)(2,1)}, bf16[256,768]{1,0:T(8,128)(2,1)}, u32[]{:S(2)}, u32[]{:S(2)}) collective-permute-start(bf16[256,768]{1,0:T(8,128)(2,1)} %get-tuple-element.136.refs_5_), channel_id=1, source_target_pairs={{0,4},{4,0},{8,12},{12,8},{16,20},{20,16},{24,28},{28,24},{1,5},{5... | collective-permute-start | bytes 1179656 | tf_op jit(solution)/shard_map/ppermute | solution.py:402
  223.5 93.2 %collective-permute-start.8 = (bf16[2,192,2048]{2,1,0:T(8,128)(2,1)S(1)}, bf16[2,192,2048]{2,1,0:T(8,128)(2,1)S(1)}, u32[]{:S(2)}, u32[]{:S(2)}) collective-permute-start(bf16[2,192,2048]{2,1,0:T(8,128)(2,1)S(1)} %copy-done.3), channel_id=1, source_target_pairs={{0,8},{4,12},{8,0},{12,4},{16,24},{20,28},{24,16},{28,20},{1,9},{5... | collective-permute-start | bytes 4718600 | tf_op jit(solution)/shard_map/ppermute | solution.py:402
  226.2 58.9 %collective-permute-start.13 = (bf16[2,192,768]{2,1,0:T(8,128)(2,1)S(1)}, bf16[2,192,768]{2,1,0:T(8,128)(2,1)S(1)}, u32[]{:S(2)}, u32[]{:S(2)}) collective-permute-start(bf16[2,192,768]{2,1,0:T(8,128)(2,1)S(1)} %fusion.64.refs_2_), channel_id=1, source_target_pairs={{0,8},{4,12},{8,0},{12,4},{16,24},{20,28},{24,16},{28,20},{1,9},{5... | collective-permute-start | bytes 1769480 | tf_op jit(solution)/shard_map/ppermute | solution.py:402
  230.3 64.6 %collective-permute-start.12 = (bf16[2,96,1536]{2,1,0:T(8,128)(2,1)S(1)}, bf16[2,96,1536]{2,1,0:T(8,128)(2,1)S(1)}, u32[]{:S(2)}, u32[]{:S(2)}) collective-permute-start(bf16[2,96,1536]{2,1,0:T(8,128)(2,1)S(1)} %fusion.63.refs_1_), channel_id=1, source_target_pairs={{0,8},{4,12},{8,0},{12,4},{16,24},{20,28},{24,16},{28,20},{1,9},{5... | collective-permute-start | bytes 1769480 | tf_op jit(solution)/shard_map/ppermute | solution.py:402
  231.9 63.6 %collective-permute-start.19 = (bf16[1,128,1536]{2,1,0:T(8,128)(2,1)S(1)}, bf16[1,128,1536]{2,1,0:T(8,128)(2,1)S(1)}, u32[]{:S(2)}, u32[]{:S(2)}) collective-permute-start(bf16[1,128,1536]{2,1,0:T(8,128)(2,1)S(1)} %dynamic-slice_convert_fusion.1.refs_4_), channel_id=1, source_target_pairs={{0,16},{4,20},{8,24},{12,28},{16,0},{20,4},{24,8},{28,12},{1,17},{... | collective-permute-start | bytes 1179656 | tf_op jit(solution)/shard_map/ppermute | solution.py:402
  285.1 31.5 %slice-start = ((s8[6291456]{0:T(1024)(128)(4,1)}), s8[4194304]{0:T(1024)(128)(4,1)S(1)}, s32[]{:S(2)}) async-start(s8[6291456]{0:T(1024)(128)(4,1)} %bitcast.199), calls=%async_computation | async-start | bytes 8388608
  285.3 27.2 %collective-permute-start.16 = (bf16[1,192,768]{2,1,0:T(8,128)(2,1)S(1)}, bf16[1,192,768]{2,1,0:T(8,128)(2,1)S(1)}, u32[]{:S(2)}, u32[]{:S(2)}) collective-permute-start(bf16[1,192,768]{2,1,0:T(8,128)(2,1)S(1)} %dynamic-slice_convert_fusion.3.refs_2_), channel_id=1, source_target_pairs={{0,16},{4,20},{8,24},{12,28},{16,0},{20,4},{24,8},{28,12},{1,17},{... | collective-permute-start | bytes 884744 | tf_op jit(solution)/shard_map/ppermute | solution.py:402
  295.0 20.8 %collective-permute-start.17 = (bf16[1,96,1536]{2,1,0:T(8,128)(2,1)S(1)}, bf16[1,96,1536]{2,1,0:T(8,128)(2,1)S(1)}, u32[]{:S(2)}, u32[]{:S(2)}) collective-permute-start(bf16[1,96,1536]{2,1,0:T(8,128)(2,1)S(1)} %dynamic-slice_convert_fusion.4.refs_1_), channel_id=1, source_target_pairs={{0,16},{4,20},{8,24},{12,28},{16,0},{20,4},{24,8},{28,12},{1,17},{... | collective-permute-start | bytes 884744 | tf_op jit(solution)/shard_map/ppermute | solution.py:402
  320.3 86.0 %collective-permute-start.18 = (bf16[1,192,2048]{2,1,0:T(8,128)(2,1)S(1)}, bf16[1,192,2048]{2,1,0:T(8,128)(2,1)}, u32[]{:S(2)}, u32[]{:S(2)}) collective-permute-start(bf16[1,192,2048]{2,1,0:T(8,128)(2,1)S(1)} %dynamic-slice_convert_fusion.refs_3_), channel_id=1, source_target_pairs={{0,16},{4,20},{8,24},{12,28},{16,0},{20,4},{24,8},{28,12},{1,17},{... | collective-permute-start | bytes 2359304 | tf_op jit(solution)/shard_map/ppermute | solution.py:402
  334.1 5.8 %collective-permute-start.10 = (f32[3,768]{1,0:T(4,128)}, f32[3,768]{1,0:T(4,128)S(1)}, u32[]{:S(2)}, u32[]{:S(2)}) collective-permute-start(f32[3,768]{1,0:T(4,128)} %pad_add_fusion.2), channel_id=1, source_target_pairs={{4,0},{8,4},{12,8},{16,12},{20,16},{24,20},{28,24},{5,1},{9,5},{13... | collective-permute-start | bytes 27656 | tf_op jit(solution)/shard_map/ppermute | solution.py:734
  341.1 35.2 %collective-permute-start.11 = (bf16[256,768]{1,0:T(8,128)(2,1)S(1)}, bf16[256,768]{1,0:T(8,128)(2,1)S(1)}, u32[]{:S(2)}, u32[]{:S(2)}) collective-permute-start(bf16[256,768]{1,0:T(8,128)(2,1)S(1)} %scatter-add.4), channel_id=1, source_target_pairs={{0,4},{4,0},{8,12},{12,8},{16,20},{20,16},{24,28},{28,24},{1,5},{5... | collective-permute-start | bytes 1179656 | tf_op jit(solution)/shard_map/ppermute | solution.py:402
  381.6 31.2 %collective-permute-start.14 = (bf16[2,192,768]{2,1,0:T(8,128)(2,1)S(1)}, bf16[2,192,768]{2,1,0:T(8,128)(2,1)S(1)}, u32[]{:S(2)}, u32[]{:S(2)}) collective-permute-start(bf16[2,192,768]{2,1,0:T(8,128)(2,1)S(1)} %fusion.65.refs_1_), channel_id=1, source_target_pairs={{0,8},{4,12},{8,0},{12,4},{16,24},{20,28},{24,16},{28,20},{1,9},{5... | collective-permute-start | bytes 1769480 | tf_op jit(solution)/shard_map/ppermute | solution.py:402
  414.2 28.8 %collective-permute-start.15 = (bf16[1,192,768]{2,1,0:T(8,128)(2,1)S(1)}, bf16[1,192,768]{2,1,0:T(8,128)(2,1)S(1)}, u32[]{:S(2)}, u32[]{:S(2)}) collective-permute-start(bf16[1,192,768]{2,1,0:T(8,128)(2,1)S(1)} %dynamic-slice_convert_fusion.2.refs_2_), channel_id=1, source_target_pairs={{0,16},{4,20},{8,24},{12,28},{16,0},{20,4},{24,8},{28,12},{1,17},{... | collective-permute-start | bytes 884744 | tf_op jit(solution)/shard_map/ppermute | solution.py:402
  (124 other events, 553.1 us)
where the time goes:
time: 455 us; the launch traced here: 447 us
  Pallas kernels  189 us (42%)
  waiting for transfers between devices  79 us (17%)
  matrix products  54.4 us (12%)
  other arithmetic  51 us (11%)
  local copies, waits for them, and re-layouts  38.2 us (8%)
  starting transfers between devices  32.2 us (7%)
    ppermute x19, waiting for transfers between devices, swapped(): return lax.ppermute(value, 'seq', [(s, s ^ bit) for s in range(count)])  77.8 us
    pallas_call x1, Pallas kernels, mixer_forward(): pl.pallas_call(functools.partial(forward_kernel, bits), out_shape=[shape_...  65.2 us
    pallas_call x3, Pallas kernels, four_sum(): pl.pallas_call(tied(four_sum_kernel, 1, len(ties)), out_shape=shape_of(2,...  48.2 us
    ppermute x19, starting transfers between devices, swapped(): return lax.ppermute(value, 'seq', [(s, s ^ bit) for s in range(count)])  30.9 us
    pallas_call x1, Pallas kernels, chain(): pl.pallas_call(functools.partial(chain_kernel, forward, bits), out_shape=...  26.1 us
    pallas_call x1, Pallas kernels, last_sums(): pl.pallas_call(tied(functools.partial(last_sums_kernel, bits), 2, len(tie...  24.1 us
    pallas_call x1, Pallas kernels, back(): scan_call(back_kernel, 'back', 16, channels, [row, row, row, col, col, st...  15.2 us
    dot_general x5, matrix products, paired(): jnp.dot(own_left.T, own_right, preferred_element_type=f32)  14 us
  transfers between devices with their start and end apart: 20, of which 5 were waited for; matrix products, arithmetic and copies ran while one was open for 28% of the time, Pallas kernels for 42%

commit v1 on v0

v1 whole, which is shorter than its diff:
```python
import functools
import math
import types

import jax
import jax.numpy as jnp
from jax import lax
from jax.experimental import pallas as pl
from jax.experimental.pallas import tpu as pltpu
from jax.sharding import PartitionSpec as P

f32 = jnp.float32
bf16 = jnp.bfloat16
LOG2E = math.log2(math.e)
LN2 = math.log(2.0)
RESET = 1e30
UNROLL = 8
LANES = 256
VMEM = pl.BlockSpec(memory_space=pltpu.VMEM)


def shape_of(*dims, dtype=f32):
    return jax.ShapeDtypeStruct(dims, dtype)


def cost(us):
    return pl.CostEstimate(flops=int(us * 1e9), bytes_accessed=int(us * 1e6), transcendentals=0)


def widened(column, width):
    return jnp.concatenate([column] * (width // 128), 1)


ANY = pl.BlockSpec(memory_space=pl.ANY)


def sent(source, target, sends, receives, slot, axis, partner):
    copy = pltpu.make_async_remote_copy(
        src_ref=source,
        dst_ref=target,
        send_sem=sends.at[slot],
        recv_sem=receives.at[slot],
        device_id={axis: partner},
        device_id_type=pl.DeviceIdType.MESH,
    )
    copy.start()
    return copy


def bits_of(count):
    return [1 << k for k in range(count.bit_length() - 1)]


def flipped(me, bit):
    mine = lax.rem(me // bit, 2)
    return mine, me + bit - 2 * bit * mine


CHUNK = 32


def sigmoid(values):
    return 1.0 / (1.0 + jnp.exp(-values))


def softplus(values):
    return jnp.maximum(values, 0.0) + jnp.log1p(jnp.exp(-jnp.abs(values)))


def row_doc(places, bounds):
    return (places >= bounds[0]).astype(jnp.int32) + (places >= bounds[1]).astype(jnp.int32)


def tap_mask(places, bounds, offset):
    source = places - offset
    same = row_doc(source, bounds) == row_doc(places, bounds)
    return jnp.where((source >= 0) & same, 1.0, 0.0)


def mean_square(values):
    return jnp.mean(values * values, axis=-1, keepdims=True)


def three_norms(raw, gains, rank, states):
    low, mid, high = raw[:, :rank], raw[:, rank : rank + states], raw[:, rank + states :]
    low_scale = lax.rsqrt(mean_square(low) + 1e-06)
    mid_scale = lax.rsqrt(jnp.maximum(mean_square(mid), 0.1))
    high_scale = lax.rsqrt(jnp.maximum(mean_square(high), 0.1))
    return (
        low * low_scale * gains[:, :rank],
        mid * mid_scale * gains[:, rank : rank + states],
        high * high_scale * gains[:, rank + states :],
    )


def widen(values, wide, first, count):
    states = values.shape[1]
    eye = (
        lax.broadcasted_iota(jnp.int32, (states, states), 0)
        == lax.broadcasted_iota(jnp.int32, (states, states), 1)
    ).astype(f32)
    spread = jnp.sum(values[:, None, :] * eye[None], axis=-1, keepdims=True)
    wide[pl.ds(first, count)] = jnp.broadcast_to(spread, (count, states, 128))


def greeted(axis_partners):
    barrier = pltpu.get_barrier_semaphore()
    for axis, partner in axis_partners:
        pl.semaphore_signal(
            barrier, inc=1, device_id={axis: partner}, device_id_type=pl.DeviceIdType.MESH
        )
    pl.semaphore_wait(barrier, len(axis_partners))


def chained(forward, bits, state, steps, rates, moving, landed, sends, receives, base):
    me = lax.axis_index("seq")
    states = state.shape[0]
    all_state, all_steps = state, steps
    mine_state, mine_steps = jnp.zeros_like(all_state), jnp.zeros_like(all_steps)
    for k, bit in enumerate(bits):
        mine, partner = flipped(me, bit)
        moving[k, :states] = all_state
        moving[k, states:] = all_steps
        sent(moving.at[k], landed.at[k], sends, receives, base + k, "seq", partner).wait()
        other_state, other_steps = landed[k, :states], landed[k, states:]
        earlier = (mine == 1) if forward else (mine == 0)
        through = jnp.exp2(rates * mine_steps[:1])
        mine_state = jnp.where(earlier, mine_state + through * other_state, mine_state)
        mine_steps = jnp.where(earlier, mine_steps + other_steps, mine_steps)
        after = jnp.exp2(rates * all_steps[:1]) * other_state + all_state
        ahead_of = jnp.exp2(rates * other_steps[:1]) * all_state + other_state
        all_state = jnp.where(earlier, after, ahead_of)
        all_steps = all_steps + other_steps
    return mine_state


def forward_kernel(
    bits, bounds, proj, chan, logs, w_x, gains, w_dt, w_out, one_in, cot,
    halo, pre_out, low_out, raw_out, step_pre_out, into, out_of, scan_out, gated_out, last_state,
    mixer, hist_out, one_came, cot_came,
    extended, raw_move, raw_land, step, drive, starts, moving, landed, part, first_land,
    second_move, second_land, hist, sends, receives, hist_sem, shared_sends, shared_receives,
):
    tokens, channels = low_out.shape
    rank, states = w_dt.shape[0], logs.shape[0]
    chunks = tokens // CHUNK
    ch_me, me = lax.axis_index("ch"), lax.axis_index("seq")
    seq_count = 1 << len(bits)
    low, across = flipped(ch_me, 1)
    high, along = flipped(ch_me, 2)
    following, previous = lax.rem(me + 1, seq_count), lax.rem(me + seq_count - 1, seq_count)
    greeted(
        [("ch", across), ("ch", along), ("seq", following), ("seq", previous)]
        + [("seq", flipped(me, bit)[1]) for bit in bits]
    )
    halo_copy = sent(
        proj.at[pl.ds(tokens - 16, 16), pl.ds(0, channels)], halo, sends, receives, 0, "seq",
        following,
    )
    mine, pair = flipped(me, bits[0])
    half = one_in.shape[0] // 2
    some = pl.ds(low * half, half)
    at = pl.ds(pl.multiple_of(low * (tokens // 2), tokens // 2), tokens // 2)
    shared = [
        (one_in.at[some, 1 - mine], one_came.at[some]),
        (cot.at[at], cot_came.at[at]),
    ]
    shared_copies = [
        sent(source, target, shared_sends, shared_receives, k, "seq", pair)
        for k, (source, target) in enumerate(shared)
    ]
    rates = -jnp.exp(logs[...]) * LOG2E
    halo_copy.wait()
    extended[0:16] = halo[...].astype(f32)

    def spread(index, _):
        first = pl.multiple_of(index * CHUNK, CHUNK)
        extended[pl.ds(first + 16, CHUNK)] = proj[pl.ds(first, CHUNK), :channels].astype(f32)
        return 0

    lax.fori_loop(0, chunks, spread, 0)

    def convolved(index, _):
        first = pl.multiple_of(index * CHUNK, CHUNK)
        places = me * tokens + first + lax.broadcasted_iota(jnp.int32, (CHUNK, 128), 0)
        window = extended[pl.ds(first, CHUNK + 16)]
        summed = chan[4:5]
        for k in range(4):
            mask = widened(tap_mask(places, bounds, 3 - k), channels)
            summed = summed + chan[k : k + 1] * window[13 + k : 13 + k + CHUNK] * mask
        pre_out[pl.ds(first, CHUNK)] = summed
        low_out[pl.ds(first, CHUNK)] = (summed * sigmoid(summed)).astype(bf16)
        return 0

    lax.fori_loop(0, chunks, convolved, 0)
    raw_move[0] = jnp.dot(low_out[...], w_x[...], preferred_element_type=f32)
    sent(raw_move.at[0], raw_land.at[0], sends, receives, 1, "ch", across).wait()
    raw_move[1] = raw_move[0] + raw_land[0]
    sent(raw_move.at[1], raw_land.at[1], sends, receives, 2, "ch", along).wait()

    def stepped(index, total):
        first = pl.multiple_of(index * CHUNK, CHUNK)
        rows = pl.ds(first, CHUNK)
        raw = raw_move[1, rows] + raw_land[1, rows]
        raw_out[rows] = raw
        step_norm, input_norm, output_norm = three_norms(raw, gains[...], rank, states)
        widen(input_norm, into, first, CHUNK)
        widen(output_norm, out_of, first, CHUNK)
        pre = (
            jnp.dot(step_norm.astype(bf16), w_dt[...], preferred_element_type=f32) + chan[5:6]
        )
        step_pre_out[rows] = pre
        size = softplus(pre)
        drive[rows] = size * low_out[rows].astype(f32)
        places = me * tokens + first + lax.broadcasted_iota(jnp.int32, (CHUNK, 128), 0)
        resets = jnp.where((places == bounds[0]) | (places == bounds[1]), RESET, 0.0)
        size = size + widened(resets, channels)
        step[rows] = size
        return total + jnp.sum(size, axis=0, keepdims=True)

    total = lax.fori_loop(0, chunks, stepped, jnp.zeros((1, channels), f32))
    blocks = [slice(j, j + LANES) for j in range(0, channels, LANES)]
    for lanes in blocks:
        block_rates = rates[:, lanes]

        def ended(index, state, lanes=lanes, block_rates=block_rates):
            first = pl.multiple_of(index * UNROLL, UNROLL)
            steps, drives = step[pl.ds(first, UNROLL), lanes], drive[pl.ds(first, UNROLL), lanes]
            for k in range(UNROLL):
                decay = jnp.exp2(steps[k : k + 1] * block_rates)
                state = decay * state + widened(into[first + k], LANES) * drives[k : k + 1]
            return state

        starts[:, lanes] = lax.fori_loop(
            0, tokens // UNROLL, ended, jnp.zeros((states, LANES), f32)
        )
    starts[...] = chained(
        True, bits, starts[...], jnp.broadcast_to(total, (8, channels)), rates, moving, landed,
        sends, receives, 7,
    )
    hist_copies = []
    for number, lanes in enumerate(blocks):
        block_rates = rates[:, lanes]
        skip = chan[6:7, lanes]

        def walked(index, state, lanes=lanes, block_rates=block_rates, skip=skip):
            first = pl.multiple_of(index * UNROLL, UNROLL)
            steps, drives = step[pl.ds(first, UNROLL), lanes], drive[pl.ds(first, UNROLL), lanes]
            rows = []
            for k in range(UNROLL):
                hist[first + k, :, lanes] = state
                decay = jnp.exp2(steps[k : k + 1] * block_rates)
                state = decay * state + widened(into[first + k], LANES) * drives[k : k + 1]
                rows.append(
                    jnp.sum(widened(out_of[first + k], LANES) * state, axis=0, keepdims=True)
                )
            scan_out[pl.ds(first, UNROLL), lanes] = jnp.concatenate(rows, 0)
            return state

        last_state[:, lanes] = lax.fori_loop(0, tokens // UNROLL, walked, starts[:, lanes])
        copy = pltpu.make_async_copy(
            hist.at[:, :, lanes], hist_out.at[:, :, lanes], hist_sem.at[number]
        )
        copy.start()
        hist_copies.append(copy)

    def gate(index, _):
        first = pl.multiple_of(index * CHUNK, CHUNK)
        rows = pl.ds(first, CHUNK)
        scanned = scan_out[rows] + chan[6:7] * low_out[rows].astype(f32)
        scan_out[rows] = scanned
        gate_pre = proj[rows, channels:].astype(f32)
        gated_out[rows] = (scanned * gate_pre * sigmoid(gate_pre)).astype(bf16)
        return 0

    lax.fori_loop(0, chunks, gate, 0)
    quarter = tokens // 4
    width = w_out.shape[1]
    for k, (_, target) in enumerate(shared):
        shared_copies[k].wait()
        shared_copies[k] = sent(
            target, target, shared_sends, shared_receives, 2 + k, "ch", across
        )

    def mixed(index, _):
        first = pl.multiple_of(index * 512, 512)
        product = jnp.dot(
            gated_out[...], w_out[:, pl.ds(first, 512)], preferred_element_type=f32
        ).astype(bf16)
        for k in range(4):
            part[k // 2, k % 2, :, pl.ds(first, 512)] = product[k * quarter : (k + 1) * quarter]
        return 0

    lax.fori_loop(0, width // 512, mixed, 0)
    four_summed(
        part, mixer, first_land, second_land, second_move, sends, receives, 3, low, across, high,
        along,
    )
    for copy in hist_copies + shared_copies:
        copy.wait()


def four_summed(
    value, total, first, second, moving, sends, receives, base, low, across, high, along
):
    sent(value.at[:, 1 - low], first, sends, receives, base, "ch", across).wait()
    moving[...] = (
        value[1 - high, low].astype(f32) + first[1 - high].astype(f32)
    ).astype(bf16)
    copy = sent(moving, second, sends, receives, base + 1, "ch", along)
    kept = value[high, low].astype(f32) + first[high].astype(f32)
    copy.wait()
    total[high, low] = (kept + second[...].astype(f32)).astype(bf16)
    own = total.at[high, low]
    sent(own, own, sends, receives, base + 2, "ch", along).wait()
    both = total.at[:, low]
    sent(both, both, sends, receives, base + 3, "ch", across).wait()


def mixer_forward(bounds, proj, chan, logs, w_x, gains, w_dt, w_out, one_in, cot, count, ident):
    bits = bits_of(count)
    tokens, channels = proj.shape[0], proj.shape[1] // 2
    states, rank, width = logs.shape[0], w_dt.shape[0], w_out.shape[1]
    quarter, narrow = tokens // 4, w_x.shape[1]
    rows = shape_of(tokens, channels)
    low_rows = shape_of(tokens, channels, dtype=bf16)
    wide = shape_of(tokens, states, 128)
    slots = pltpu.VMEM((len(bits), states + 8, channels), f32)
    raws = pltpu.VMEM((2, tokens, narrow), f32)
    out = pl.pallas_call(
        functools.partial(forward_kernel, bits),
        out_shape=[
            shape_of(16, channels, dtype=bf16), rows, low_rows, shape_of(tokens, narrow), rows,
            wide, wide, rows, low_rows, shape_of(states, channels),
            shape_of(2, 2, quarter, width, dtype=bf16), shape_of(tokens, states, channels),
            shape_of(one_in.shape[0], *one_in.shape[2:], dtype=bf16),
            shape_of(tokens, width, dtype=bf16),
        ],
        in_specs=[pl.BlockSpec(memory_space=pltpu.SMEM)] + [VMEM] * 7 + [ANY] * 2,
        out_specs=[VMEM] * 11 + [ANY] * 3,
        scratch_shapes=[
            pltpu.VMEM((tokens + 16, channels), f32), raws, raws,
            pltpu.VMEM((tokens, channels), f32), pltpu.VMEM((tokens, channels), f32),
            pltpu.VMEM((states, channels), f32), slots, slots,
            pltpu.VMEM((2, 2, quarter, width), bf16), pltpu.VMEM((2, quarter, width), bf16),
            pltpu.VMEM((quarter, width), bf16), pltpu.VMEM((quarter, width), bf16),
            pltpu.VMEM((tokens, states, channels), f32),
            pltpu.SemaphoreType.DMA((7 + len(bits),)), pltpu.SemaphoreType.DMA((7 + len(bits),)),
            pltpu.SemaphoreType.DMA((channels // LANES,)),
            pltpu.SemaphoreType.DMA((4,)), pltpu.SemaphoreType.DMA((4,)),
        ],
        compiler_params=pltpu.CompilerParams(
            collective_id=ident, has_side_effects=True, vmem_limit_bytes=56 * 2**20
        ),
        cost_estimate=cost(6),
        name="mixer_forward",
    )(bounds, proj, chan, logs, w_x, gains, w_dt, w_out, one_in, cot)
    return out


class Unit:
    def __init__(self, name, left, right, columns, refs, sends, receives, slot, bits, ready):
        self.name, self.left, self.right, self.columns = name, left, right, columns
        self.away, self.land, self.kept = refs
        self.sends, self.receives, self.slot, self.bits = sends, receives, slot, bits
        self.ready = ready
        self.stage = 0
        self.copy = None

    def next(self):
        stage, me = self.stage, lax.axis_index("seq")
        self.stage += 1
        left_over = stage == len(self.bits)
        if stage == 0:
            for wait in self.ready:
                wait()
            mine, partner = flipped(me, self.bits[0])
            self.make(1 - mine, self.away[0])
            self.copy = self.start(0, partner)
            self.make(mine, self.kept)
            return
        self.copy.wait()
        count = self.land[stage - 1].shape[0]
        rows = self.kept.shape[1]
        part = 32 if rows % 32 == 0 else rows
        parts = rows // part

        def total(index, at):
            return self.kept[index, at] + self.land[stage - 1][index, at].astype(f32)

        if left_over:

            def finish(step, _):
                at = pl.ds(pl.multiple_of(step * part, part), part)
                self.kept[0, at] = total(0, at)
                return 0

            lax.fori_loop(0, parts, finish, 0)
            return
        mine, partner = flipped(me, self.bits[stage])

        def send(step, _):
            index = lax.div(step, parts)
            at = pl.ds(pl.multiple_of(lax.rem(step, parts) * part, part), part)
            self.away[stage][index, at] = total(2 * index + 1 - mine, at).astype(bf16)
            return 0

        lax.fori_loop(0, (count // 2) * parts, send, 0)
        self.copy = self.start(stage, partner)

        def keep(step, _):
            index = lax.div(step, parts)
            at = pl.ds(pl.multiple_of(lax.rem(step, parts) * part, part), part)
            self.kept[index, at] = total(2 * index + mine, at)
            return 0

        lax.fori_loop(0, (count // 2) * parts, keep, 0)

    def start(self, stage, partner):
        return sent(
            self.away[stage], self.land[stage], self.sends, self.receives, self.slot + stage,
            "seq", partner,
        )

    def make(self, side, target):
        first, width = self.columns
        tile = 512 if width % 512 == 0 else 256
        tiles = width // tile

        def block(step, _):
            index = lax.div(step, tiles)
            column = pl.multiple_of(lax.rem(step, tiles) * tile, tile)
            product = jnp.dot(
                self.left[2 * index + side],
                self.right[:, pl.ds(first + column, tile)],
                preferred_element_type=f32,
            )
            target[index, :, pl.ds(column, tile)] = product.astype(target.dtype)
            return 0

        lax.fori_loop(0, target.shape[0] * tiles, block, 0)


def norm_back(values, scale, gains, grad, free=True):
    weighted = gains * grad
    result = scale * weighted
    inner = jnp.mean(values * weighted, axis=-1, keepdims=True)
    return result - jnp.where(free, 1.0, 0.0) * values * (scale * scale * scale) * inner, (
        grad * values * scale
    )


def silu_slope(values):
    part = sigmoid(values)
    return part * (1.0 + values * (1.0 - part))


def narrowed(wide, first, count):
    states = wide.shape[1]
    eye = (
        lax.broadcasted_iota(jnp.int32, (states, states), 0)
        == lax.broadcasted_iota(jnp.int32, (states, states), 1)
    ).astype(f32)
    sums = jnp.sum(wide[pl.ds(first, count)], axis=-1, keepdims=True)
    return jnp.sum(sums * eye[None], axis=1)


def dot_rows(left, right):
    return lax.dot_general(left, right, (((1,), (1,)), ((), ())), preferred_element_type=f32)


def backward_kernel(bits, names, *refs):
    r = types.SimpleNamespace(**dict(zip(names, refs)))
    tokens, width = r.stream.shape
    channels, rank, states = r.low.shape[1], r.w_dt.shape[0], r.logs.shape[0]
    quarter, chunks = tokens // 4, tokens // CHUNK
    ch_me, me = lax.axis_index("ch"), lax.axis_index("seq")
    seq_count = 1 << len(bits)
    low, across = flipped(ch_me, 1)
    high, along = flipped(ch_me, 2)
    mine, pair = flipped(me, bits[0])
    following, previous = lax.rem(me + 1, seq_count), lax.rem(me + seq_count - 1, seq_count)
    loads = {}

    def load(name, source, target):
        copy = pltpu.make_async_copy(source, target, r.load_sems.at[len(loads)])
        copy.start()
        loads[name] = copy

    def have(*wanted):
        for name in wanted:
            if name in loads and loads[name] is not None:
                loads[name].wait()
                loads[name] = None

    own, other = pl.ds(0, tokens), pl.ds(tokens, tokens)
    half = r.left_two.shape[0]
    hid = r.right_two.shape[1] // 2
    load("hidden", r.hidden_in.at[:, mine], r.left_hidden.at[:, :, own])
    load("cot", r.cot, r.right_down.at[own])
    load("cot_came", r.cot_came, r.right_down.at[other])
    load("two_right", r.gate_up_in, r.right_two.at[own])
    load("two", r.two_in.at[:, mine], r.left_two.at[:, :, own])
    load("mixer", r.mixer_in, r.mixer)
    load("w_out", r.w_out, r.weights)
    load("one", r.one_in.at[:, mine], r.left_one.at[:, :, own])
    load("one_came", r.one_came, r.left_one.at[:, :, other])
    load("gated", r.gated_in.at[:, mine], r.left_gated.at[:, :, own])
    load("scan_out", r.scan_in, r.scan)
    load("into", r.into_in, r.into)
    load("out_of", r.out_of_in, r.out_of)
    blocks = [slice(j, j + 128) for j in range(0, channels, 128)]
    load("hist0", r.hist_in.at[:, :, blocks[0]], r.hist.at[0])
    load("hist1", r.hist_in.at[:, :, blocks[1]], r.hist.at[1])

    greeted(
        [("ch", across), ("ch", along), ("seq", following), ("seq", previous)]
        + [("seq", flipped(me, bit)[1]) for bit in bits]
    )
    pair_copies, shared_copies = {}, {}

    def swap(name, source, target):
        slot = len(pair_copies)
        pair_copies[name] = sent(
            source, target, r.pair_sends, r.pair_receives, slot, "seq", pair
        )

    def came(name):
        return lambda: (pair_copies[name].wait(), pair_copies.__setitem__(name, Done))

    def swap_shared(name, source, target):
        slot = len(shared_copies)
        copy = sent(source, target, r.shared_sends, r.shared_receives, 2 * slot, "seq", pair)
        shared_copies[name] = (copy, target, 2 * slot + 1)

    def came_shared(name):
        def wait():
            copy, target, slot = shared_copies[name]
            copy.wait()
            sent(target, target, r.shared_sends, r.shared_receives, slot, "ch", across).wait()

        return wait

    n_bits = len(bits) - 1

    def unit(name, left, right, columns, slot, ready):
        refs = (
            [getattr(r, f"{name}_away").at[pl.ds(0, half >> (k + 1))] for k in range(n_bits)],
            [getattr(r, f"{name}_land{k}") for k in range(n_bits)],
            getattr(r, f"{name}_kept"),
        )
        return Unit(
            name, left, right, columns, refs, r.unit_sends, r.unit_receives, slot * n_bits,
            bits[1:], ready,
        )

    down = unit("down", r.left_hidden, r.right_down, (0, width), 0,
                [lambda: have("hidden", "cot", "cot_came"), came("hidden")])
    gate = unit("gate", r.left_two, r.right_two, (0, hid), 1,
                [lambda: have("two", "two_right"), came_shared("two"), came("gate")])
    up = unit("up", r.left_two, r.right_two, (hid, hid), 2, [came("up")])
    out = unit("out", r.left_gated, r.right_out, (0, width), 3,
               [lambda: have("gated"), came("gated"), came_shared("mixer")])
    gin = unit("gin", r.left_one, r.right_in, (channels, channels), 4,
               [lambda: have("one", "one_came"), came("gin")])
    cin = unit("cin", r.left_one, r.right_in, (0, channels), 5, [came("cin")])
    queue = [down, gate, up, down, gate, None, None, up, out, gin, out, gin, down, gate, up]
    if n_bits > 2:
        queue += [down, gate, up, out, gin] * (n_bits - 2)
    results = {"down": r.down_out, "gate": r.gate_out, "up": r.up_out, "out": r.out_out,
               "gin": r.gin_out, "cin": r.cin_out}
    written = []

    def step():
        if queue:
            item = queue.pop(0)
            if item is not None:
                advance(item)

    def advance(item):
        if item.stage > n_bits:
            return
        item.next()
        if item.stage == n_bits + 1:
            copy = pltpu.make_async_copy(
                item.kept.at[0], results[item.name], r.write_sems.at[len(written)]
            )
            copy.start()
            written.append(copy)

    swap("hidden", r.hidden_in.at[:, 1 - mine], r.left_hidden.at[:, :, other])
    some = pl.ds(low * (half // 2), half // 2)
    swap_shared("two", r.two_in.at[some, 1 - mine], r.left_two.at[some, :, other])
    swap("gate", r.gate_up_in.at[:, pl.ds(0, hid)], r.right_two.at[other, pl.ds(0, hid)])
    swap("up", r.gate_up_in.at[:, pl.ds(hid, hid)], r.right_two.at[other, pl.ds(hid, hid)])
    swap("gated", r.gated_in.at[:, 1 - mine], r.left_gated.at[:, :, other])

    sums = (r.first_land, r.second_land, r.second_move, r.sum_sends, r.sum_receives)

    def summed(value, base, fillers):
        first, second, moving, sends, receives = sums
        copy = sent(value.at[:, 1 - low], first, sends, receives, base, "ch", across)
        fillers[0]()
        copy.wait()
        moving[...] = (
            value[1 - high, low].astype(f32) + first[1 - high].astype(f32)
        ).astype(bf16)
        copy = sent(moving, second, sends, receives, base + 1, "ch", along)
        fillers[1]()
        copy.wait()
        r.total[high, low] = (
            value[high, low].astype(f32) + first[high].astype(f32) + second[...].astype(f32)
        ).astype(bf16)
        part = r.total.at[high, low]
        copy = sent(part, part, sends, receives, base + 2, "ch", along)
        fillers[2]()
        copy.wait()
        both = r.total.at[:, low]
        copy = sent(both, both, sends, receives, base + 3, "ch", across)
        fillers[3]()
        copy.wait()

    def idle():
        return None

    rates = -jnp.exp(r.logs[...]) * LOG2E

    def places_of(first, count):
        return me * tokens + first + lax.broadcasted_iota(jnp.int32, (count, 128), 0)

    def resteps():
        def body(index, total):
            first = pl.multiple_of(index * CHUNK, CHUNK)
            rows = pl.ds(first, CHUNK)
            size = softplus(r.step_pre[rows])
            r.drive[rows] = size * r.low[rows].astype(f32)
            places = places_of(first, CHUNK)
            resets = jnp.where((places == r.bounds[0]) | (places == r.bounds[1]), RESET, 0.0)
            size = size + widened(resets, channels)
            r.step[rows] = size
            return total + jnp.sum(size, axis=0, keepdims=True)

        r.step_sum[...] = jnp.broadcast_to(
            lax.fori_loop(0, chunks, body, jnp.zeros((1, channels), f32)), (8, channels)
        )

    load("part", r.two_part, r.part)
    have("part")
    summed(r.part, 0, [resteps, step, idle, idle])
    load("feed", r.feed_part, r.part)
    have("mixer", "cot")

    def quarter_rows(index):
        per = quarter // CHUNK
        part = lax.div(index, per)
        at = pl.ds(pl.multiple_of(lax.rem(index, per) * CHUNK, CHUNK), CHUNK)
        return lax.div(part, 2), lax.rem(part, 2), at

    def norm_two(index, total):
        first = pl.multiple_of(index * CHUNK, CHUNK)
        rows = pl.ds(first, CHUNK)
        a, b, at = quarter_rows(index)
        middle = r.stream[rows].astype(f32) + r.mixer[a, b, at].astype(f32)
        scale = lax.rsqrt(mean_square(middle) + 1e-06)
        back, gain = norm_back(middle, scale, r.gains[1:2], r.total[a, b, at].astype(f32))
        grad = r.right_down[rows].astype(f32) + back
        r.stream_grad[rows] = grad
        r.right_out[rows] = grad.astype(bf16)
        return total + jnp.sum(gain, axis=0, keepdims=True)

    gain_two = lax.fori_loop(0, chunks, norm_two, jnp.zeros((1, width), f32))
    r.flat_move[0] = jnp.zeros_like(r.flat_move[0])
    r.flat_move[0, 1:2] = gain_two
    first = pl.multiple_of(low * (tokens // 2), tokens // 2)
    swap_shared(
        "mixer",
        r.right_out.at[pl.ds(first, tokens // 2)],
        r.right_out.at[pl.ds(tokens + first, tokens // 2)],
    )
    have("w_out", "scan_out")

    skips = []
    for j in range(0, channels, 256):
        lanes = slice(j, j + 256)
        gated_grad = dot_rows(r.right_out[own], r.weights[pl.ds(j, 256)])
        gate_pre = r.proj[:, channels + j : channels + j + 256].astype(f32)
        part = sigmoid(gate_pre)
        slope = part * (1.0 + gate_pre * (1.0 - part))
        r.right_in[own, channels + j : channels + j + 256] = (
            gated_grad * r.scan[:, lanes] * slope
        ).astype(bf16)
        grad = gated_grad * gate_pre * part
        r.scan[:, lanes] = grad
        skips.append(jnp.sum(grad * r.low[:, lanes].astype(f32), axis=0, keepdims=True))
    skip_grad = jnp.concatenate(skips, 1)
    swap("gin", r.right_in.at[own, pl.ds(channels, channels)],
         r.right_in.at[other, pl.ds(channels, channels)])
    load("w_in0", r.w_in.at[pl.ds(0, channels)], r.weights)
    have("into", "out_of")
    for j in range(0, channels, LANES):
        lanes = slice(j, j + LANES)

        def ended(index, carried, lanes=lanes, block_rates=rates[:, j : j + LANES]):
            first = pl.multiple_of(tokens - UNROLL - index * UNROLL, UNROLL)
            steps, grads = r.step[pl.ds(first, UNROLL), lanes], r.scan[pl.ds(first, UNROLL), lanes]
            for k in reversed(range(UNROLL)):
                decay = jnp.exp2(steps[k : k + 1] * block_rates)
                carried = decay * (widened(r.out_of[first + k], LANES) * grads[k : k + 1] + carried)
            return carried

        r.starts[:, lanes] = lax.fori_loop(
            0, tokens // UNROLL, ended, jnp.zeros((states, LANES), f32)
        )

    all_state, all_steps = r.starts[...], r.step_sum[...]
    mine_state, mine_steps = jnp.zeros_like(all_state), jnp.zeros_like(all_steps)
    for k, bit in enumerate(bits):
        side, partner = flipped(me, bit)
        r.chain_move[k, :states] = all_state
        r.chain_move[k, states:] = all_steps
        copy = sent(r.chain_move.at[k], r.chain_land.at[k], r.chain_sends, r.chain_receives, k,
                    "seq", partner)
        if k == 0:
            step()
        copy.wait()
        other_state, other_steps = r.chain_land[k, :states], r.chain_land[k, states:]
        earlier = side == 0
        through = jnp.exp2(rates * mine_steps[:1])
        mine_state = jnp.where(earlier, mine_state + through * other_state, mine_state)
        mine_steps = jnp.where(earlier, mine_steps + other_steps, mine_steps)
        after = jnp.exp2(rates * all_steps[:1]) * other_state + all_state
        ahead_of = jnp.exp2(rates * other_steps[:1]) * all_state + other_state
        all_state = jnp.where(earlier, after, ahead_of)
        all_steps = all_steps + other_steps
    r.starts[...] = mine_state
    step()

    r.into_wide[...] = jnp.zeros_like(r.into_wide)
    r.out_wide[...] = jnp.zeros_like(r.out_wide)
    for number, lanes in enumerate(blocks):
        have(f"hist{number}")
        hist = r.hist.at[number % 2]
        block_rates = rates[:, lanes]

        def walked(index, carry, lanes=lanes, block_rates=block_rates, hist=hist):
            carried, state, total = carry
            first = pl.multiple_of(tokens - UNROLL - index * UNROLL, UNROLL)
            some = pl.ds(first, UNROLL)
            steps, drives, grads = r.step[some, lanes], r.drive[some, lanes], r.scan[some, lanes]
            decay_list, push_list = [None] * UNROLL, [None] * UNROLL
            for k in reversed(range(UNROLL)):
                place = first + k
                grad_row = grads[k : k + 1]
                decay = jnp.exp2(steps[k : k + 1] * block_rates)
                adjoint = r.out_of[place] * grad_row + carried
                carried = decay * adjoint
                r.out_wide[place] = r.out_wide[place] + state * grad_row
                r.into_wide[place] = r.into_wide[place] + adjoint * drives[k : k + 1]
                state = hist[place]
                share = carried * state
                total = total + share * steps[k : k + 1]
                decay_list[k] = jnp.sum(share * block_rates, axis=0, keepdims=True)
                push_list[k] = jnp.sum(r.into[place] * adjoint, axis=0, keepdims=True)
            r.decay_rows[some, :] = jnp.concatenate(decay_list, 0)
            r.push[some, lanes] = jnp.concatenate(push_list, 0)
            return (carried, state, total)

        _, _, total = lax.fori_loop(
            0,
            tokens // UNROLL,
            walked,
            (r.starts[:, lanes], r.last_state[:, lanes], jnp.zeros((states, 128), f32)),
        )
        r.rate_sum[:, lanes] = total * (rates[:, lanes] * LN2)

        def gathered(index, _, lanes=lanes):
            rows = pl.ds(pl.multiple_of(index * CHUNK, CHUNK), CHUNK)
            used, pushed = r.low[rows, lanes].astype(f32), r.push[rows, lanes]
            pre = r.step_pre[rows, lanes]
            grad = (LN2 * r.decay_rows[rows] + pushed * used) * sigmoid(pre)
            r.step_low_grad[rows, lanes] = grad.astype(bf16)
            r.push[rows, lanes] = pushed * softplus(pre) + r.chan[6:7, lanes] * r.scan[rows, lanes]
            return 0

        lax.fori_loop(0, chunks, gathered, 0)
        if number + 2 < len(blocks):
            load(f"hist{number + 2}", r.hist_in.at[:, :, blocks[number + 2]], r.hist.at[number % 2])
        step()

    def norm_grads(index, _):
        first = pl.multiple_of(index * CHUNK, CHUNK)
        rows = pl.ds(first, CHUNK)
        low_part = dot_rows(r.step_low_grad[rows], r.w_dt[...])
        r.raw_move[0, rows] = jnp.concatenate(
            [low_part, narrowed(r.into_wide, first, CHUNK), narrowed(r.out_wide, first, CHUNK)], 1
        )
        return 0

    lax.fori_loop(0, chunks, norm_grads, 0)
    copy = sent(r.raw_move.at[0], r.raw_land.at[0], r.raw_sends, r.raw_receives, 0, "ch", across)
    step()
    copy.wait()
    r.raw_move[1] = r.raw_move[0] + r.raw_land[0]
    copy = sent(r.raw_move.at[1], r.raw_land.at[1], r.raw_sends, r.raw_receives, 1, "ch", along)
    step()
    copy.wait()

    def raw_back(index, total):
        rows = pl.ds(pl.multiple_of(index * CHUNK, CHUNK), CHUNK)
        grads, raw = r.raw_move[1, rows] + r.raw_land[1, rows], r.raw[rows]
        gains = r.small_gains[...]
        values, sums_to = [], []
        for start, stop, floor in ((0, rank, None), (rank, rank + states, 0.1),
                                   (rank + states, rank + 2 * states, 0.1)):
            value = raw[:, start:stop]
            square = mean_square(value)
            if floor is None:
                scale, free = lax.rsqrt(square + 1e-06), True
            else:
                scale, free = lax.rsqrt(jnp.maximum(square, floor)), square > floor
            back, gain = norm_back(value, scale, gains[:, start:stop], grads[:, start:stop], free)
            values.append(back)
            sums_to.append(jnp.sum(gain, axis=0, keepdims=True))
        norm = raw[:, :rank] * lax.rsqrt(mean_square(raw[:, :rank]) + 1e-06) * gains[:, :rank]
        r.raw_low[rows] = jnp.concatenate(values, 1).astype(bf16)
        r.step_low[rows] = norm.astype(bf16)
        return total + jnp.concatenate(sums_to, 1)

    small = lax.fori_loop(0, chunks, raw_back, jnp.zeros((1, rank + 2 * states), f32))
    r.flat_move[0, 2:3, : rank + 2 * states] = small

    def conv_back(index, total):
        first = pl.multiple_of(index * CHUNK, CHUNK)
        rows = pl.ds(first, CHUNK)
        grad = r.push[rows] + dot_rows(r.raw_low[rows], r.w_x[...])
        grad = grad * silu_slope(r.pre[rows])
        r.grad_pre[rows] = grad
        return total + jnp.sum(grad, axis=0, keepdims=True)

    tap_bias = lax.fori_loop(0, chunks, conv_back, jnp.zeros((1, channels), f32))
    copy = sent(r.grad_pre.at[pl.ds(0, 8)], r.grad_pre.at[pl.ds(tokens, 8)], r.raw_sends,
                r.raw_receives, 2, "seq", previous)
    r.extended[0:16] = r.halo[...].astype(f32)

    def extend(index, _):
        first = pl.multiple_of(index * CHUNK, CHUNK)
        r.extended[pl.ds(first + 16, CHUNK)] = r.proj[pl.ds(first, CHUNK), :channels].astype(f32)
        return 0

    lax.fori_loop(0, chunks, extend, 0)

    def taps(index, totals):
        first = pl.multiple_of(index * CHUNK, CHUNK)
        places = places_of(first, CHUNK)
        window = r.extended[pl.ds(first, CHUNK + 16)]
        grad = r.grad_pre[pl.ds(first, CHUNK)]
        return tuple(
            totals[k]
            + jnp.sum(
                grad
                * widened(tap_mask(places, r.bounds, 3 - k), channels)
                * window[13 + k : 13 + k + CHUNK],
                axis=0,
                keepdims=True,
            )
            for k in range(4)
        )

    tap_grads = lax.fori_loop(
        0, chunks, taps, tuple(jnp.zeros((1, channels), f32) for _ in range(4))
    )
    copy.wait()

    def conv_in_back(index, _):
        first = pl.multiple_of(index * CHUNK, CHUNK)
        window = r.grad_pre[pl.ds(first, CHUNK + 8)]
        grad = jnp.zeros((CHUNK, channels), f32)
        for k in range(4):
            places = places_of(first + 3 - k, CHUNK)
            mask = jnp.where(
                places < seq_count * tokens, tap_mask(places, r.bounds, 3 - k), 0.0
            )
            grad = grad + r.chan[k : k + 1] * widened(mask, channels) * window[3 - k : 3 - k + CHUNK]
        r.right_in[pl.ds(first, CHUNK), :channels] = grad.astype(bf16)
        return 0

    lax.fori_loop(0, chunks, conv_in_back, 0)
    swap("cin", r.right_in.at[own, pl.ds(0, channels)], r.right_in.at[other, pl.ds(0, channels)])

    have("feed")
    summed(r.part, 4, [idle, step, step, idle])

    def results_of(index, totals):
        rows = pl.ds(pl.multiple_of(index * CHUNK, CHUNK), CHUNK)
        a, b, at = quarter_rows(index)
        mixed, feed = r.mixer[a, b, at].astype(f32), r.total[a, b, at].astype(f32)
        result = r.stream[rows].astype(f32) + mixed + feed
        r.out_rows[rows] = result.astype(bf16)
        return tuple(
            total + jnp.sum(v * v, axis=0, keepdims=True)
            for total, v in zip(totals, (result, mixed, feed))
        )

    squares = lax.fori_loop(
        0, chunks, results_of, tuple(jnp.zeros((1, width), f32) for _ in range(3))
    )
    for number, total in enumerate(squares):
        r.flat_move[0, 3 + number : 4 + number] = total

    have("w_in0")
    for number in range(width // channels):

        def one_part(index, _, first=number * channels):
            at = pl.multiple_of(index * 256, 256)
            product = dot_rows(r.right_in[own], r.weights[pl.ds(at, 256)]).astype(bf16)
            for k in range(4):
                r.part[k // 2, k % 2, :, pl.ds(first + at, 256)] = product[
                    k * quarter : (k + 1) * quarter
                ]
            return 0

        lax.fori_loop(0, channels // 256, one_part, 0)
        if (number + 1) * channels < width:
            load(f"w_in{number + 1}", r.w_in.at[pl.ds((number + 1) * channels, channels)], r.weights)
            have(f"w_in{number + 1}")
    queue[:] = [cin, *queue, out, gin, cin, cin]

    def small_columns():
        narrow = r.w_x.shape[1]
        pack = r.step
        pack[0:narrow] = lax.dot_general(
            r.raw_low[...], r.low[...], (((0,), (0,)), ((), ())), preferred_element_type=f32
        )
        pack[narrow : narrow + rank] = lax.dot_general(
            r.step_low[...], r.step_low_grad[...], (((0,), (0,)), ((), ())),
            preferred_element_type=f32,
        )
        at = narrow + rank
        pack[at : at + states] = r.rate_sum[...]
        at += states
        bias = jnp.sum(r.step_low_grad[...].astype(f32), axis=0, keepdims=True)
        pack[at : at + 8] = jnp.concatenate(
            [*tap_grads, tap_bias, bias, skip_grad, jnp.zeros((1, channels), f32)], 0
        )
        at += 8
        pack[at:] = jnp.zeros((pack.shape[0] - at, channels), f32)
        turned = pack[...].T
        r.small_work0[...] = turned.reshape(r.small_work0.shape)

    summed(r.part, 8, [step, small_columns, step, idle])

    def norm_one(index, total):
        rows = pl.ds(pl.multiple_of(index * CHUNK, CHUNK), CHUNK)
        a, b, at = quarter_rows(index)
        value = r.stream[rows].astype(f32)
        scale = lax.rsqrt(mean_square(value) + 1e-06)
        back, gain = norm_back(value, scale, r.gains[0:1], r.total[a, b, at].astype(f32))
        r.stream_grad[rows] = r.stream_grad[rows] + back
        return total + jnp.sum(gain, axis=0, keepdims=True)

    r.flat_move[0, 0:1] = lax.fori_loop(0, chunks, norm_one, jnp.zeros((1, width), f32))

    for k, bit in enumerate(bits):
        side, partner = flipped(me, bit)
        work = getattr(r, f"small_work{k}")
        away, land = getattr(r, f"small_away{k}"), getattr(r, f"small_land{k}")
        away[...] = work[:, 1 - side].astype(bf16)
        copy = sent(away, land, r.last_sends, r.last_receives, 2 * k, "seq", partner)
        flat = sent(r.flat_move.at[k], r.flat_land.at[k], r.last_sends, r.last_receives, 2 * k + 1,
                    "seq", partner)
        step()
        copy.wait()
        total = work[:, side] + land[...].astype(f32)
        flat.wait()
        if k + 1 < len(bits):
            target = getattr(r, f"small_work{k + 1}")
            target[...] = total.reshape(target.shape)
            r.flat_move[k + 1] = r.flat_move[k] + r.flat_land[k]
        else:
            r.small_out[...] = total.reshape(r.small_out.shape)
            r.flat_out[...] = r.flat_move[k] + r.flat_land[k]
    while queue:
        step()
    pending = [down, gate, up, out, gin, cin]
    while any(item.stage <= n_bits for item in pending):
        for item in pending:
            advance(item)
    for copy in written:
        copy.wait()


class Done:
    @staticmethod
    def wait():
        return None


def backward(ins, hbm_ins, count, ident):
    bits = bits_of(count)
    n_bits = len(bits) - 1
    tokens, width = ins["stream"].shape
    channels, rank, states = ins["low"].shape[1], ins["w_dt"].shape[0], ins["logs"].shape[0]
    hid = hbm_ins["gate_up_in"].shape[1] // 2
    narrow = ins["w_x"].shape[1]
    half, quarter = count // 2, tokens // 4
    rows_in, rows_out, rows_down = width // count, channels // count, hid // count
    rows = pltpu.VMEM((tokens, channels), f32)

    def low(*dims):
        return pltpu.VMEM(dims, bf16)

    def full(*dims):
        return pltpu.VMEM(dims, f32)

    outs = {
        "stream_grad": (shape_of(tokens, width), VMEM),
        "out_rows": (shape_of(tokens, width, dtype=bf16), VMEM),
        "small_out": (shape_of(rows_out, tokens), VMEM),
        "flat_out": (shape_of(8, width), VMEM),
        "down_out": (shape_of(rows_down, width), ANY),
        "gate_out": (shape_of(rows_in, hid), ANY),
        "up_out": (shape_of(rows_in, hid), ANY),
        "out_out": (shape_of(rows_out, width), ANY),
        "gin_out": (shape_of(rows_in, channels), ANY),
        "cin_out": (shape_of(rows_in, channels), ANY),
    }
    scratch = {
        "left_hidden": low(half, rows_down, 2 * tokens),
        "left_two": low(half, rows_in, 2 * tokens),
        "left_one": low(half, rows_in, 2 * tokens),
        "left_gated": low(half, rows_out, 2 * tokens),
        "right_down": low(2 * tokens, width),
        "right_two": low(2 * tokens, 2 * hid),
        "right_out": low(2 * tokens, width),
        "right_in": low(2 * tokens, 2 * channels),
        "mixer": low(2, 2, quarter, width),
        "weights": low(channels, width),
        "scan": rows, "step": rows, "drive": rows, "push": rows,
        "decay_rows": full(tokens, 128),
        "into": full(tokens, states, 128), "out_of": full(tokens, states, 128),
        "into_wide": full(tokens, states, 128), "out_wide": full(tokens, states, 128),
        "hist": full(2, tokens, states, 128),
        "step_sum": full(8, channels), "starts": full(states, channels),
        "rate_sum": full(states, channels),
        "step_low_grad": low(tokens, channels),
        "chain_move": full(len(bits), states + 8, channels),
        "chain_land": full(len(bits), states + 8, channels),
        "part": low(2, 2, quarter, width), "total": low(2, 2, quarter, width),
        "first_land": low(2, quarter, width), "second_land": low(quarter, width),
        "second_move": low(quarter, width),
        "raw_move": full(2, tokens, narrow), "raw_land": full(2, tokens, narrow),
        "raw_low": low(tokens, narrow), "step_low": low(tokens, rank),
        "grad_pre": full(tokens + 8, channels), "extended": full(tokens + 16, channels),
        "flat_move": full(len(bits), 8, width), "flat_land": full(len(bits), 8, width),
    }
    for k in range(len(bits)):
        size = count >> (k + 1)
        scratch[f"small_work{k}"] = full(size, 2, rows_out, tokens)
        scratch[f"small_away{k}"] = low(size, rows_out, tokens)
        scratch[f"small_land{k}"] = low(size, rows_out, tokens)
    units = {
        "down": (rows_down, width), "gate": (rows_in, hid), "up": (rows_in, hid),
        "out": (rows_out, width), "gin": (rows_in, channels), "cin": (rows_in, channels),
    }
    for name, (part, columns) in units.items():
        scratch[f"{name}_away"] = low(half // 2, part, columns)
        for k in range(n_bits):
            scratch[f"{name}_land{k}"] = low(half >> (k + 1), part, columns)
        scratch[f"{name}_kept"] = full(half // 2, part, columns)

    def sems(size):
        return pltpu.SemaphoreType.DMA((size,))

    scratch |= {
        "load_sems": sems(40), "write_sems": sems(6),
        "pair_sends": sems(8), "pair_receives": sems(8),
        "shared_sends": sems(4), "shared_receives": sems(4),
        "unit_sends": sems(6 * n_bits), "unit_receives": sems(6 * n_bits),
        "sum_sends": sems(12), "sum_receives": sems(12),
        "chain_sends": sems(len(bits)), "chain_receives": sems(len(bits)),
        "raw_sends": sems(3), "raw_receives": sems(3),
        "last_sends": sems(2 * len(bits)), "last_receives": sems(2 * len(bits)),
    }
    names = [*ins, *hbm_ins, *outs, *scratch]
    made = pl.pallas_call(
        functools.partial(backward_kernel, bits, names),
        out_shape=[shape for shape, _ in outs.values()],
        in_specs=[
            pl.BlockSpec(memory_space=pltpu.SMEM) if name == "bounds" else VMEM for name in ins
        ]
        + [ANY] * len(hbm_ins),
        out_specs=[spec for _, spec in outs.values()],
        scratch_shapes=list(scratch.values()),
        compiler_params=pltpu.CompilerParams(
            collective_id=ident, has_side_effects=True, vmem_limit_bytes=63 * 2**20
        ),
        name="block_backward",
    )(*ins.values(), *hbm_ins.values())
    return dict(zip(outs, made))


def rms_gain(values, gain_row):
    return values * lax.rsqrt(jnp.mean(values * values, axis=-1, keepdims=True) + 1e-06) * gain_row


def swiglu(gate_up):
    return jax.nn.silu(gate_up[:, 0]) * gate_up[:, 1]


def local(
    seq_count,
    stream,
    doc_bounds,
    norm_gains,
    w_in,
    chan_vectors,
    decay_logs,
    w_x,
    small_gains,
    w_dt,
    w_out,
    w_gate_up,
    w_down,
    cotangent,
):
    tokens, width = stream.shape
    rank, (states, channels) = w_dt.shape[0], decay_logs.shape

    def turned(values):
        return values.T.reshape(seq_count // 2, 2, values.shape[1] // seq_count, tokens)

    stream_in = stream.astype(f32)
    normed_low = rms_gain(stream_in, norm_gains[0]).astype(bf16)
    w_in_flat = w_in.reshape(width, 2 * channels)
    in_proj = jnp.dot(normed_low, w_in_flat, preferred_element_type=f32).astype(bf16)
    one_in = turned(normed_low)
    (
        halo, pre_conv, conv_low, raw_proj, step_pre, into, out_of, scan_out, gated_low,
        last_state, mixer_low, before, one_came, cot_came,
    ) = mixer_forward(
        doc_bounds, in_proj, chan_vectors, decay_logs, w_x, small_gains[None], w_dt, w_out,
        one_in, cotangent, seq_count, 1,
    )
    middle = stream_in + mixer_low.reshape(tokens, width).astype(f32)
    normed_two_low = rms_gain(middle, norm_gains[1]).astype(bf16)
    gate_up = jnp.einsum("td,dkf->tkf", normed_two_low, w_gate_up, preferred_element_type=f32)
    hidden_act, act_back = jax.vjp(swiglu, gate_up)
    hidden_low = hidden_act.astype(bf16)
    hidden_grad = jnp.einsum("td,fd->tf", cotangent, w_down, preferred_element_type=f32)
    (gate_up_grad,) = act_back(hidden_grad)
    gate_up_low = gate_up_grad.astype(bf16)
    normed_two_part = jnp.einsum("tkf,dkf->td", gate_up_low, w_gate_up, preferred_element_type=f32)
    feed_part = jnp.dot(hidden_low, w_down, preferred_element_type=f32)

    def quartered(values):
        return values.astype(bf16).reshape(2, 2, tokens // 4, width)

    made = backward(
        {
            "bounds": doc_bounds, "stream": stream, "gains": norm_gains, "proj": in_proj,
            "halo": halo, "pre": pre_conv, "low": conv_low, "raw": raw_proj,
            "step_pre": step_pre, "last_state": last_state, "chan": chan_vectors,
            "logs": decay_logs, "w_x": w_x, "w_dt": w_dt, "small_gains": small_gains[None],
        },
        {
            "two_part": quartered(normed_two_part), "feed_part": quartered(feed_part),
            "mixer_in": mixer_low, "cot": cotangent, "cot_came": cot_came,
            "gate_up_in": gate_up_low.reshape(tokens, -1), "two_in": turned(normed_two_low),
            "hidden_in": turned(hidden_low), "gated_in": turned(gated_low), "one_in": one_in,
            "one_came": one_came, "w_out": w_out, "w_in": w_in_flat, "scan_in": scan_out,
            "into_in": into, "out_of_in": out_of, "hist_in": before,
        },
        seq_count,
        2,
    )
    small, flat = made["small_out"], made["flat_out"]
    at = w_x.shape[1]
    x_part, small = small[:, :at], small[:, at:].T
    dt_part, decay_out = small[:rank], small[rank : rank + states]
    chan_part = small[rank + states : rank + states + 7]
    me = lax.axis_index("seq")
    gain_width = width // seq_count
    gains_part = lax.dynamic_slice_in_dim(flat[:2], me * gain_width, gain_width, 1)
    small_width = small_gains.shape[0] // seq_count
    small_part = lax.dynamic_slice_in_dim(flat[2], me * small_width, small_width, 0)
    rms_values = jnp.sqrt(jnp.sum(flat[3:6], axis=1) / (tokens * seq_count * width))
    return (
        made["out_rows"],
        made["stream_grad"],
        gains_part,
        jnp.stack([made["cin_out"], made["gin_out"]], 1),
        chan_part,
        decay_out,
        x_part,
        small_part,
        dt_part,
        made["out_out"],
        jnp.stack([made["gate_out"], made["up_out"]], 1),
        made["down_out"],
        rms_values,
    )


def solution(mesh):
    in_specs = (
        P("seq", None),
        P(),
        P(),
        P(None, None, "ch"),
        P(None, "ch"),
        P(None, "ch"),
        P("ch", None),
        P(),
        P(None, "ch"),
        P("ch", None),
        P(None, None, "ch"),
        P("ch", None),
        P("seq", None),
    )
    out_specs = (
        P("seq", None),
        P("seq", None),
        P(None, "seq"),
        P("seq", None, "ch"),
        P(None, ("ch", "seq")),
        P(None, ("ch", "seq")),
        P(("ch", "seq"), None),
        P("seq"),
        P(None, ("ch", "seq")),
        P(("ch", "seq"), None),
        P("seq", None, "ch"),
        P(("ch", "seq"), None),
        P(),
    )
    return jax.shard_map(
        functools.partial(local, mesh.shape["seq"]),
        mesh=mesh,
        in_specs=in_specs,
        out_specs=out_specs,
        check_vma=False,
    )
```

time: 455 us -> 328 us (0.72)
  the two profiles are of different devices: /device:TPU:0 before, /device:TPU:8 now
where the time goes in v1:
time: 328 us; the launch traced here: 327 us
  Pallas kernels  286 us (87%)
  local copies, waits for them, and re-layouts  22 us (7%)
  matrix products  13.8 us (4%)
  other arithmetic  4.71 us (1%)
    pallas_call x1, Pallas kernels, backward(): pl.pallas_call(functools.partial(backward_kernel, bits, names), out_shape...  226 us
    pallas_call x1, Pallas kernels, mixer_forward(): pl.pallas_call(functools.partial(forward_kernel, bits), out_shape=[shape_...  60 us
    unnamed x42, local copies, waits for them, and re-layouts  13.8 us

profile of v1, /device:TPU:8, one launch (start us, length us, event | category | flops | bytes accessed | tf_op | source)
XLA Modules:
  0.0 327.4 jit_solution(11166028870735140094)
XLA Ops:
  0.6 0.8 slice_reduce_fusion.1
  1.5 3.3 %copy.39 = bf16[192,8,2,768]{3,1,2,0:T(8,128)(2,1)S(1)} copy(bf16[192,8,2,768]{3,2,1,0:T(2,128)(2,1)} %bitcast.64) | data formatting | bytes 9437184
  5.1 2.4 convolution_convert_fusion.1.proj.refs_3_
  7.7 1.2 copy.26
  8.9 60.0 %mixer_forward.1 = (bf16[16,768]{1,0:T(8,128)(2,1)}, f32[256,768]{1,0:T(8,128)}, bf16[256,768]{1,0:T(8,128)(2,1)}, f32[256,128]{1,0:T(8,128)}, f32[256,768]{1,0:...) custom-call(s32[2]{0:T(128)} %refs_0_.1, ...), custom_call_target="tpu_custom_call" | custom-call | flops 6000000000 | bytes 6000000 | tf_op jit(solution)/shard_map/mixer_forward/pallas_call | solution.py:330
  68.9 1.5 multiply_reduce_fusion
  70.8 5.1 %fusion.2 = f32[256,2,1024]{2,0,1:T(8,128)S(1)} fusion(bf16[1536,2,1024]{2,1,0:T(2,128)(2,1)} %param.23, bf16[256,1536]{1,0:T(8,128)(2,1)S(1)} %multiply_convert_fusion), kind=kOutput, calls=%fused_computation.2 | convolution fusion | flops 1610612736 | bytes 9175040 | tf_op jit(solution)/shard_map/td,dkf->tkf/dot_general | solution.py:1146
  75.9 1.3 multiply_bitcast_fusion
  77.4 1.1 copy.38
  78.5 3.2 fusion.7
  81.7 1.9 convolution_convert_fusion
  83.5 1.0 copy.31
  84.5 1.2 copy.30
  85.7 0.9 copy.32
  86.7 226.1 %block_backward.1 = (f32[256,1536]{1,0:T(8,128)}, bf16[256,1536]{1,0:T(8,128)(2,1)}, f32[96,256]{1,0:T(8,128)}, f32[8,1536]{1,0:T(8,128)}, f32[128,1536]{1,0:T(8...) custom-call(s32[2]{0:T(128)} %refs_0_.1, ...), custom_call_target="tpu_custom_call" | custom-call | tf_op jit(solution)/shard_map/block_backward/pallas_call | solution.py:1085
  312.7 1.5 pad_maximum_fusion
  314.2 2.4 copy.37
  316.7 1.9 copy.33
  319.3 0.7 copy.35
  320.8 0.7 copy.36
  323.4 0.9 copy.52
  324.3 1.1 copy.53
  325.7 0.8 copy.54
  326.5 0.9 copy.55
  (50 shorter events, 4.8 us)
Async XLA Ops:
  1.5 3.4 %copy-start = (bf16[256,1536]{1,0:T(8,128)(2,1)S(1)}, bf16[256,1536]{1,0:T(8,128)(2,1)}, u32[]{:S(2)}) copy-start(bf16[256,1536]{1,0:T(8,128)(2,1)} %refs_1_.1) | copy-start | bytes 2359300
  4.8 2.6 copy-start.1
  68.8 1.6 copy-start.2
  70.4 8.1 %slice-start = ((s8[6291456]{0:T(1024)(128)(4,1)}), s8[4194304]{0:T(1024)(128)(4,1)S(1)}, s32[]{:S(2)}) async-start(s8[6291456]{0:T(1024)(128)(4,1)} %bitcast.83), calls=%async_computation | async-start | bytes 8388608
  70.8 5.2 %copy-start.6 = (bf16[256,1536]{1,0:T(8,128)(2,1)S(1)}, bf16[256,1536]{1,0:T(8,128)(2,1)}, u32[]{:S(2)}) copy-start(bf16[256,1536]{1,0:T(8,128)(2,1)} %refs_18_.1) | copy-start | bytes 2359300
  70.8 5.1 %copy-start.13 = (bf16[1024,1536]{1,0:T(8,128)(2,1)S(1)}, bf16[1024,1536]{1,0:T(8,128)(2,1)}, u32[]{:S(2)}) copy-start(bf16[1024,1536]{1,0:T(8,128)(2,1)} %param.24) | copy-start | bytes 9437188
  70.8 7.7 %slice-start.1 = ((s8[6291456]{0:T(1024)(128)(4,1)}), s8[2097152]{0:T(1024)(128)(4,1)S(1)}, s32[]{:S(2)}) async-start(s8[6291456]{0:T(1024)(128)(4,1)} %bitcast.83), calls=%async_computation.1 | async-start | bytes 4194304
  83.5 2.2 copy-start.10
  314.2 2.4 copy-start.8
  314.2 2.4 copy-start.9
  316.7 2.0 copy-start.11
  316.7 4.8 %copy-start.12 = (f32[8,1536]{1,0:T(8,128)S(1)}, f32[8,1536]{1,0:T(8,128)}, u32[]{:S(2)}) copy-start(f32[8,1536]{1,0:T(8,128)} %get-tuple-element.53) | copy-start | bytes 147460
  316.7 6.7 %copy-start.5 = (bf16[256,1536]{1,0:T(8,128)(2,1)S(1)}, bf16[256,1536]{1,0:T(8,128)(2,1)}, u32[]{:S(2)}) copy-start(bf16[256,1536]{1,0:T(8,128)(2,1)} %get-tuple-element.94) | copy-start | bytes 2359300
  318.6 5.6 %copy-start.3 = (f32[256,1536]{1,0:T(8,128)S(1)}, f32[256,1536]{1,0:T(8,128)}, u32[]{:S(2)}) copy-start(f32[256,1536]{1,0:T(8,128)} %get-tuple-element.95) | copy-start | bytes 4718596
  324.3 1.4 copy-start.7
  324.3 2.3 copy-start.4

commit v2 on v1

--- a/solution.py
+++ b/solution.py
@@ -157,7 +157,7 @@
         proj.at[pl.ds(tokens - 16, 16), pl.ds(0, channels)], halo, sends, receives, 0, "seq",
         following,
     )
-    mine, pair = flipped(me, bits[0])
+    mine, pair = flipped(me, bits[1])
     half = one_in.shape[0] // 2
     some = pl.ds(low * half, half)
     at = pl.ds(pl.multiple_of(low * (tokens // 2), tokens // 2), tokens // 2)
@@ -359,26 +359,34 @@
 
 
 class Unit:
-    def __init__(self, name, left, right, columns, refs, sends, receives, slot, bits, ready):
-        self.name, self.left, self.right, self.columns = name, left, right, columns
-        self.away, self.land, self.kept = refs
+    def __init__(self, left, right, columns, refs, sends, receives, slot, bits, result):
+        self.left, self.right, self.columns = left, right, columns
+        away, *self.land, self.kept = refs
+        self.away = [away.at[pl.ds(0, land.shape[0])] for land in self.land]
         self.sends, self.receives, self.slot, self.bits = sends, receives, slot, bits
-        self.ready = ready
+        self.result = result
         self.stage = 0
         self.copy = None
 
+    def made(self, *needed):
+        for item in needed:
+            item.wait()
+        mine, partner = flipped(lax.axis_index("seq"), self.bits[0])
+        self.make(1 - mine, self.away[0])
+        self.stage = 1
+        self.go = lambda: self.begin(partner, mine)
+        return self
+
+    def begin(self, partner, mine):
+        self.copy = self.start(0, partner)
+        self.make(mine, self.kept)
+
     def next(self):
         stage, me = self.stage, lax.axis_index("seq")
+        if stage > len(self.bits):
+            return
         self.stage += 1
         left_over = stage == len(self.bits)
-        if stage == 0:
-            for wait in self.ready:
-                wait()
-            mine, partner = flipped(me, self.bits[0])
-            self.make(1 - mine, self.away[0])
-            self.copy = self.start(0, partner)
-            self.make(mine, self.kept)
-            return
         self.copy.wait()
         count = self.land[stage - 1].shape[0]
         rows = self.kept.shape[1]
@@ -396,6 +404,7 @@
                 return 0
 
             lax.fori_loop(0, parts, finish, 0)
+            self.written = self.result(self.kept.at[0])
             return
         mine, partner = flipped(me, self.bits[stage])
 
@@ -431,7 +440,7 @@
             index = lax.div(step, tiles)
             column = pl.multiple_of(lax.rem(step, tiles) * tile, tile)
             product = jnp.dot(
-                self.left[2 * index + side],
+                self.left[index, side],
                 self.right[:, pl.ds(first + column, tile)],
                 preferred_element_type=f32,
             )
@@ -469,8 +478,29 @@
     return lax.dot_general(left, right, (((1,), (1,)), ((), ())), preferred_element_type=f32)
 
 
+class Once:
+    def __init__(self, *copies, then=None):
+        self.copies, self.then = copies, then
+
+    def wait(self):
+        for copy in self.copies:
+            copy.wait()
+        self.copies = ()
+        if self.then is not None:
+            after, self.then = self.then, None
+            after().wait()
+
+
+def named(names, refs):
+    refs, found = list(refs), {}
+    for name, count in names:
+        taken, refs = refs[: count or 1], refs[count or 1 :]
+        found[name] = taken if count else taken[0]
+    return types.SimpleNamespace(**found)
+
+
 def backward_kernel(bits, names, *refs):
-    r = types.SimpleNamespace(**dict(zip(names, refs)))
+    r = named(names, refs)
     tokens, width = r.stream.shape
     channels, rank, states = r.low.shape[1], r.w_dt.shape[0], r.logs.shape[0]
     quarter, chunks = tokens // 4, tokens // CHUNK
@@ -478,150 +508,113 @@
     seq_count = 1 << len(bits)
     low, across = flipped(ch_me, 1)
     high, along = flipped(ch_me, 2)
-    mine, pair = flipped(me, bits[0])
+    pair_bit, rest_bits = bits[1], [bits[0], *bits[2:]]
+    mine, pair = flipped(me, pair_bit)
     following, previous = lax.rem(me + 1, seq_count), lax.rem(me + seq_count - 1, seq_count)
-    loads = {}
-
-    def load(name, source, target):
-        copy = pltpu.make_async_copy(source, target, r.load_sems.at[len(loads)])
+    load_slots, pair_slots, shared_slots, write_slots = ([] for _ in range(4))
+
+    def slot_of(slots):
+        slots.append(0)
+        return len(slots) - 1
+
+    def load(source, target):
+        copy = pltpu.make_async_copy(source, target, r.load_sems.at[slot_of(load_slots)])
         copy.start()
-        loads[name] = copy
-
-    def have(*wanted):
-        for name in wanted:
-            if name in loads and loads[name] is not None:
-                loads[name].wait()
-                loads[name] = None
+        return Once(copy)
 
     own, other = pl.ds(0, tokens), pl.ds(tokens, tokens)
-    half = r.left_two.shape[0]
+    high_count = r.left_two.shape[0]
     hid = r.right_two.shape[1] // 2
-    load("hidden", r.hidden_in.at[:, mine], r.left_hidden.at[:, :, own])
-    load("cot", r.cot, r.right_down.at[own])
-    load("cot_came", r.cot_came, r.right_down.at[other])
-    load("two_right", r.gate_up_in, r.right_two.at[own])
-    load("two", r.two_in.at[:, mine], r.left_two.at[:, :, own])
-    load("mixer", r.mixer_in, r.mixer)
-    load("w_out", r.w_out, r.weights)
-    load("one", r.one_in.at[:, mine], r.left_one.at[:, :, own])
-    load("one_came", r.one_came, r.left_one.at[:, :, other])
-    load("gated", r.gated_in.at[:, mine], r.left_gated.at[:, :, own])
-    load("scan_out", r.scan_in, r.scan)
-    load("into", r.into_in, r.into)
-    load("out_of", r.out_of_in, r.out_of)
+    part_in = load(r.two_part, r.part)
+    hidden_own = load(r.hidden_in.at[:, mine], r.left_hidden.at[:, :, :, own])
+    cot_own = load(r.cot, r.right_down.at[own])
+    cot_other = load(r.cot_came, r.right_down.at[other])
+    gate_up_own = load(r.gate_up_in, r.right_two.at[own])
+    two_own = load(r.two_in.at[:, mine], r.left_two.at[:, :, :, own])
+    mixer_own = load(r.mixer_in, r.mixer)
+    weights = load(r.w_out, r.weights)
+    scan_own = load(r.scan_in, r.scan)
+    out_of_own = load(r.out_of_in, r.out_of)
+    into_own = load(r.into_in, r.into)
+    one_own = load(r.one_in.at[:, mine], r.left_one.at[:, :, :, own])
+    one_other = load(r.one_came, r.left_one.at[:, :, :, other])
+    gated_own = load(r.gated_in.at[:, mine], r.left_gated.at[:, :, :, own])
     blocks = [slice(j, j + 128) for j in range(0, channels, 128)]
-    load("hist0", r.hist_in.at[:, :, blocks[0]], r.hist.at[0])
-    load("hist1", r.hist_in.at[:, :, blocks[1]], r.hist.at[1])
+    hists = [load(r.hist_in.at[:, :, blocks[k]], r.hist.at[k]) for k in range(2)]
 
     greeted(
         [("ch", across), ("ch", along), ("seq", following), ("seq", previous)]
         + [("seq", flipped(me, bit)[1]) for bit in bits]
     )
-    pair_copies, shared_copies = {}, {}
-
-    def swap(name, source, target):
-        slot = len(pair_copies)
-        pair_copies[name] = sent(
-            source, target, r.pair_sends, r.pair_receives, slot, "seq", pair
-        )
-
-    def came(name):
-        return lambda: (pair_copies[name].wait(), pair_copies.__setitem__(name, Done))
-
-    def swap_shared(name, source, target):
-        slot = len(shared_copies)
-        copy = sent(source, target, r.shared_sends, r.shared_receives, 2 * slot, "seq", pair)
-        shared_copies[name] = (copy, target, 2 * slot + 1)
-
-    def came_shared(name):
-        def wait():
-            copy, target, slot = shared_copies[name]
-            copy.wait()
-            sent(target, target, r.shared_sends, r.shared_receives, slot, "ch", across).wait()
-
-        return wait
-
-    n_bits = len(bits) - 1
-
-    def unit(name, left, right, columns, slot, ready):
-        refs = (
-            [getattr(r, f"{name}_away").at[pl.ds(0, half >> (k + 1))] for k in range(n_bits)],
-            [getattr(r, f"{name}_land{k}") for k in range(n_bits)],
-            getattr(r, f"{name}_kept"),
-        )
+
+    def swap(source, target):
+        slot = slot_of(pair_slots)
+        return Once(sent(source, target, r.pair_sends, r.pair_receives, slot, "seq", pair))
+
+    def swap_shared(source, target):
+        slot = 2 * slot_of(shared_slots)
+        copy = sent(source, target, r.shared_sends, r.shared_receives, slot, "seq", pair)
+        return Once(
+            copy,
+            then=lambda: sent(
+                target, target, r.shared_sends, r.shared_receives, slot + 1, "ch", across
+            ),
+        )
+
+    n_bits = len(rest_bits)
+
+    def writer(target):
+        def write(source):
+            copy = pltpu.make_async_copy(source, target, r.write_sems.at[slot_of(write_slots)])
+            copy.start()
+            return copy
+
+        return write
+
+    def unit(left, right, columns, refs, slot, target):
         return Unit(
-            name, left, right, columns, refs, r.unit_sends, r.unit_receives, slot * n_bits,
-            bits[1:], ready,
-        )
-
-    down = unit("down", r.left_hidden, r.right_down, (0, width), 0,
-                [lambda: have("hidden", "cot", "cot_came"), came("hidden")])
-    gate = unit("gate", r.left_two, r.right_two, (0, hid), 1,
-                [lambda: have("two", "two_right"), came_shared("two"), came("gate")])
-    up = unit("up", r.left_two, r.right_two, (hid, hid), 2, [came("up")])
-    out = unit("out", r.left_gated, r.right_out, (0, width), 3,
-               [lambda: have("gated"), came("gated"), came_shared("mixer")])
-    gin = unit("gin", r.left_one, r.right_in, (channels, channels), 4,
-               [lambda: have("one", "one_came"), came("gin")])
-    cin = unit("cin", r.left_one, r.right_in, (0, channels), 5, [came("cin")])
-    queue = [down, gate, up, down, gate, None, None, up, out, gin, out, gin, down, gate, up]
-    if n_bits > 2:
-        queue += [down, gate, up, out, gin] * (n_bits - 2)
-    results = {"down": r.down_out, "gate": r.gate_out, "up": r.up_out, "out": r.out_out,
-               "gin": r.gin_out, "cin": r.cin_out}
-    written = []
-
-    def step():
-        if queue:
-            item = queue.pop(0)
-            if item is not None:
-                advance(item)
-
-    def advance(item):
-        if item.stage > n_bits:
-            return
-        item.next()
-        if item.stage == n_bits + 1:
-            copy = pltpu.make_async_copy(
-                item.kept.at[0], results[item.name], r.write_sems.at[len(written)]
-            )
-            copy.start()
-            written.append(copy)
-
-    swap("hidden", r.hidden_in.at[:, 1 - mine], r.left_hidden.at[:, :, other])
-    some = pl.ds(low * (half // 2), half // 2)
-    swap_shared("two", r.two_in.at[some, 1 - mine], r.left_two.at[some, :, other])
-    swap("gate", r.gate_up_in.at[:, pl.ds(0, hid)], r.right_two.at[other, pl.ds(0, hid)])
-    swap("up", r.gate_up_in.at[:, pl.ds(hid, hid)], r.right_two.at[other, pl.ds(hid, hid)])
-    swap("gated", r.gated_in.at[:, 1 - mine], r.left_gated.at[:, :, other])
+            left, right, columns, refs, r.unit_sends, r.unit_receives, slot * n_bits, rest_bits,
+            writer(target),
+        )
+
+    down = unit(r.left_hidden, r.right_down, (0, width), r.down, 0, r.down_out)
+    gate = unit(r.left_two, r.right_two, (0, hid), r.gate, 1, r.gate_out)
+    up = unit(r.left_two, r.right_two, (hid, hid), r.up, 2, r.up_out)
+    out = unit(r.left_gated, r.right_out, (0, width), r.out, 3, r.out_out)
+    gin = unit(r.left_one, r.right_in, (channels, channels), r.gin, 4, r.gin_out)
+    cin = unit(r.left_one, r.right_in, (0, channels), r.cin, 5, r.cin_out)
+
+    some = pl.ds(low * (high_count // 2), high_count // 2)
+    hidden_other = swap(r.hidden_in.at[:, 1 - mine], r.left_hidden.at[:, :, :, other])
+    two_other = swap_shared(r.two_in.at[some, 1 - mine], r.left_two.at[some, :, :, other])
+    gate_other = swap(r.gate_up_in.at[:, pl.ds(0, hid)], r.right_two.at[other, pl.ds(0, hid)])
+    up_other = swap(r.gate_up_in.at[:, pl.ds(hid, hid)], r.right_two.at[other, pl.ds(hid, hid)])
 
     sums = (r.first_land, r.second_land, r.second_move, r.sum_sends, r.sum_receives)
 
-    def summed(value, base, fillers):
+    def summed(value, base):
         first, second, moving, sends, receives = sums
         copy = sent(value.at[:, 1 - low], first, sends, receives, base, "ch", across)
-        fillers[0]()
+        yield
         copy.wait()
         moving[...] = (
             value[1 - high, low].astype(f32) + first[1 - high].astype(f32)
         ).astype(bf16)
         copy = sent(moving, second, sends, receives, base + 1, "ch", along)
-        fillers[1]()
+        yield
         copy.wait()
         r.total[high, low] = (
             value[high, low].astype(f32) + first[high].astype(f32) + second[...].astype(f32)
         ).astype(bf16)
         part = r.total.at[high, low]
         copy = sent(part, part, sends, receives, base + 2, "ch", along)
-        fillers[2]()
+        yield
         copy.wait()
         both = r.total.at[:, low]
         copy = sent(both, both, sends, receives, base + 3, "ch", across)
-        fillers[3]()
+        yield
         copy.wait()
-
-    def idle():
-        return None
+        yield
 
     rates = -jnp.exp(r.logs[...]) * LOG2E
 
@@ -644,11 +637,17 @@
             lax.fori_loop(0, chunks, body, jnp.zeros((1, channels), f32)), (8, channels)
         )
 
-    load("part", r.two_part, r.part)
-    have("part")
-    summed(r.part, 0, [resteps, step, idle, idle])
-    load("feed", r.feed_part, r.part)
-    have("mixer", "cot")
+    part_in.wait()
+    two_sum = summed(r.part, 0)
+    next(two_sum)
+    resteps()
+    next(two_sum)
+    down.made(hidden_own, cot_own, cot_other, hidden_other).go()
+    next(two_sum)
+    next(two_sum)
+    next(two_sum)
+    part_in = load(r.feed_part, r.part)
+    mixer_own.wait()
 
     def quarter_rows(index):
         per = quarter // CHUNK
@@ -671,14 +670,8 @@
     gain_two = lax.fori_loop(0, chunks, norm_two, jnp.zeros((1, width), f32))
     r.flat_move[0] = jnp.zeros_like(r.flat_move[0])
     r.flat_move[0, 1:2] = gain_two
-    first = pl.multiple_of(low * (tokens // 2), tokens // 2)
-    swap_shared(
-        "mixer",
-        r.right_out.at[pl.ds(first, tokens // 2)],
-        r.right_out.at[pl.ds(tokens + first, tokens // 2)],
-    )
-    have("w_out", "scan_out")
-
+    weights.wait()
+    scan_own.wait()
     skips = []
     for j in range(0, channels, 256):
         lanes = slice(j, j + 256)
@@ -693,10 +686,8 @@
         r.scan[:, lanes] = grad
         skips.append(jnp.sum(grad * r.low[:, lanes].astype(f32), axis=0, keepdims=True))
     skip_grad = jnp.concatenate(skips, 1)
-    swap("gin", r.right_in.at[own, pl.ds(channels, channels)],
-         r.right_in.at[other, pl.ds(channels, channels)])
-    load("w_in0", r.w_in.at[pl.ds(0, channels)], r.weights)
-    have("into", "out_of")
+    weights = load(r.w_in.at[pl.ds(0, channels)], r.weights)
+    out_of_own.wait()
     for j in range(0, channels, LANES):
         lanes = slice(j, j + LANES)
 
@@ -712,33 +703,84 @@
             0, tokens // UNROLL, ended, jnp.zeros((states, LANES), f32)
         )
 
-    all_state, all_steps = r.starts[...], r.step_sum[...]
-    mine_state, mine_steps = jnp.zeros_like(all_state), jnp.zeros_like(all_steps)
-    for k, bit in enumerate(bits):
-        side, partner = flipped(me, bit)
-        r.chain_move[k, :states] = all_state
-        r.chain_move[k, states:] = all_steps
-        copy = sent(r.chain_move.at[k], r.chain_land.at[k], r.chain_sends, r.chain_receives, k,
-                    "seq", partner)
-        if k == 0:
-            step()
-        copy.wait()
-        other_state, other_steps = r.chain_land[k, :states], r.chain_land[k, states:]
-        earlier = side == 0
-        through = jnp.exp2(rates * mine_steps[:1])
-        mine_state = jnp.where(earlier, mine_state + through * other_state, mine_state)
-        mine_steps = jnp.where(earlier, mine_steps + other_steps, mine_steps)
-        after = jnp.exp2(rates * all_steps[:1]) * other_state + all_state
-        ahead_of = jnp.exp2(rates * other_steps[:1]) * all_state + other_state
-        all_state = jnp.where(earlier, after, ahead_of)
-        all_steps = all_steps + other_steps
-    r.starts[...] = mine_state
-    step()
+    def handed():
+        all_state, all_steps = r.starts[...], r.step_sum[...]
+        mine_state, mine_steps = jnp.zeros_like(all_state), jnp.zeros_like(all_steps)
+        for k, bit in enumerate(bits):
+            side, partner = flipped(me, bit)
+            r.chain_move[k, :states] = all_state
+            r.chain_move[k, states:] = all_steps
+            copy = sent(r.chain_move.at[k], r.chain_land.at[k], r.chain_sends, r.chain_receives,
+                        k, "seq", partner)
+            yield
+            copy.wait()
+            other_state, other_steps = r.chain_land[k, :states], r.chain_land[k, states:]
+            earlier = side == 0
+            through = jnp.exp2(rates * mine_steps[:1])
+            mine_state = jnp.where(earlier, mine_state + through * other_state, mine_state)
+            mine_steps = jnp.where(earlier, mine_steps + other_steps, mine_steps)
+            after = jnp.exp2(rates * all_steps[:1]) * other_state + all_state
+            ahead_of = jnp.exp2(rates * other_steps[:1]) * all_state + other_state
+            all_state = jnp.where(earlier, after, ahead_of)
+            all_steps = all_steps + other_steps
+        r.starts[...] = mine_state
+        yield
+
+    chain = handed()
+    next(chain)
+    gate.made(two_own, gate_up_own, two_other, gate_other)
+    next(chain)
+    gate.go()
+    next(chain)
+    first = pl.multiple_of(low * (tokens // 2), tokens // 2)
+    mixer_other = swap_shared(
+        r.right_out.at[pl.ds(first, tokens // 2)],
+        r.right_out.at[pl.ds(tokens + first, tokens // 2)],
+    )
+    gated_other = swap(r.gated_in.at[:, 1 - mine], r.left_gated.at[:, :, :, other])
+    gin_other = swap(
+        r.right_in.at[own, pl.ds(channels, channels)],
+        r.right_in.at[other, pl.ds(channels, channels)],
+    )
+    up.made(up_other).go()
+    for _ in chain:
+        pass
+
+    part_in.wait()
+    feed_sum = summed(r.part, 4)
+    into_own.wait()
+
+    def results():
+        totals = lax.fori_loop(
+            0, chunks, results_of, tuple(jnp.zeros((1, width), f32) for _ in range(3))
+        )
+        for number, total in enumerate(totals):
+            r.flat_move[0, 3 + number : 4 + number] = total
+
+    between = [
+        lambda: (next(feed_sum), down.next()),
+        lambda: next(feed_sum),
+        lambda: (next(feed_sum), gate.next()),
+        lambda: (next(feed_sum), out.made(gated_own, mixer_other, gated_other).go()),
+        lambda: (next(feed_sum), results()),
+        lambda: gin.made(one_own, one_other, gin_other).go(),
+    ]
+
+    def results_of(index, totals):
+        rows = pl.ds(pl.multiple_of(index * CHUNK, CHUNK), CHUNK)
+        a, b, at = quarter_rows(index)
+        mixed, feed = r.mixer[a, b, at].astype(f32), r.total[a, b, at].astype(f32)
+        result = r.stream[rows].astype(f32) + mixed + feed
+        r.out_rows[rows] = result.astype(bf16)
+        return tuple(
+            total + jnp.sum(v * v, axis=0, keepdims=True)
+            for total, v in zip(totals, (result, mixed, feed))
+        )
 
     r.into_wide[...] = jnp.zeros_like(r.into_wide)
     r.out_wide[...] = jnp.zeros_like(r.out_wide)
     for number, lanes in enumerate(blocks):
-        have(f"hist{number}")
+        hists[number].wait()
         hist = r.hist.at[number % 2]
         block_rates = rates[:, lanes]
 
@@ -784,8 +826,11 @@
 
         lax.fori_loop(0, chunks, gathered, 0)
         if number + 2 < len(blocks):
-            load(f"hist{number + 2}", r.hist_in.at[:, :, blocks[number + 2]], r.hist.at[number % 2])
-        step()
+            hists.append(load(r.hist_in.at[:, :, blocks[number + 2]], r.hist.at[number % 2]))
+        if number < len(between):
+            between[number]()
+    for later in between[len(blocks) :]:
+        later()
 
     def norm_grads(index, _):
         first = pl.multiple_of(index * CHUNK, CHUNK)
@@ -798,11 +843,9 @@
 
     lax.fori_loop(0, chunks, norm_grads, 0)
     copy = sent(r.raw_move.at[0], r.raw_land.at[0], r.raw_sends, r.raw_receives, 0, "ch", across)
-    step()
     copy.wait()
     r.raw_move[1] = r.raw_move[0] + r.raw_land[0]
     copy = sent(r.raw_move.at[1], r.raw_land.at[1], r.raw_sends, r.raw_receives, 1, "ch", along)
-    step()
     copy.wait()
 
     def raw_back(index, total):
@@ -885,30 +928,12 @@
         return 0
 
     lax.fori_loop(0, chunks, conv_in_back, 0)
-    swap("cin", r.right_in.at[own, pl.ds(0, channels)], r.right_in.at[other, pl.ds(0, channels)])
-
-    have("feed")
-    summed(r.part, 4, [idle, step, step, idle])
-
-    def results_of(index, totals):
-        rows = pl.ds(pl.multiple_of(index * CHUNK, CHUNK), CHUNK)
-        a, b, at = quarter_rows(index)
-        mixed, feed = r.mixer[a, b, at].astype(f32), r.total[a, b, at].astype(f32)
-        result = r.stream[rows].astype(f32) + mixed + feed
-        r.out_rows[rows] = result.astype(bf16)
-        return tuple(
-            total + jnp.sum(v * v, axis=0, keepdims=True)
-            for total, v in zip(totals, (result, mixed, feed))
-        )
-
-    squares = lax.fori_loop(
-        0, chunks, results_of, tuple(jnp.zeros((1, width), f32) for _ in range(3))
-    )
-    for number, total in enumerate(squares):
-        r.flat_move[0, 3 + number : 4 + number] = total
-
-    have("w_in0")
+    cin_other = swap(
+        r.right_in.at[own, pl.ds(0, channels)], r.right_in.at[other, pl.ds(0, channels)]
+    )
+
     for number in range(width // channels):
+        weights.wait()
 
         def one_part(index, _, first=number * channels):
             at = pl.multiple_of(index * 256, 256)
@@ -921,9 +946,9 @@
 
         lax.fori_loop(0, channels // 256, one_part, 0)
         if (number + 1) * channels < width:
-            load(f"w_in{number + 1}", r.w_in.at[pl.ds((number + 1) * channels, channels)], r.weights)
-            have(f"w_in{number + 1}")
-    queue[:] = [cin, *queue, out, gin, cin, cin]
+            weights = load(r.w_in.at[pl.ds((number + 1) * channels, channels)], r.weights)
+    one_sum = summed(r.part, 8)
+    next(one_sum)
 
     def small_columns():
         narrow = r.w_x.shape[1]
@@ -945,9 +970,42 @@
         at += 8
         pack[at:] = jnp.zeros((pack.shape[0] - at, channels), f32)
         turned = pack[...].T
-        r.small_work0[...] = turned.reshape(r.small_work0.shape)
-
-    summed(r.part, 8, [step, small_columns, step, idle])
+        r.small_work[0][...] = turned.reshape(r.small_work[0].shape)
+
+    def small_summed():
+        for k, bit in enumerate(bits):
+            side, partner = flipped(me, bit)
+            work, away, land = r.small_work[k], r.small_away[k], r.small_land[k]
+            away[...] = work[:, 1 - side].astype(bf16)
+            copy = sent(away, land, r.last_sends, r.last_receives, 2 * k, "seq", partner)
+            yield
+            copy.wait()
+            total = work[:, side] + land[...].astype(f32)
+            target = r.small_work[k + 1] if k + 1 < len(bits) else r.small_out
+            target[...] = total.reshape(target.shape)
+        yield
+
+    def flat_summed():
+        for k, bit in enumerate(bits):
+            _, partner = flipped(me, bit)
+            copy = sent(r.flat_move.at[k], r.flat_land.at[k], r.last_sends, r.last_receives,
+                        2 * k + 1, "seq", partner)
+            yield
+            copy.wait()
+            target = r.flat_move.at[k + 1] if k + 1 < len(bits) else r.flat_out
+            target[...] = r.flat_move[k] + r.flat_land[k]
+        yield
+
+    small_columns()
+    next(one_sum)
+    small_sum = small_summed()
+    next(small_sum)
+    up.next()
+    next(one_sum)
+    out.next()
+    next(one_sum)
+    cin.made(cin_other).go()
+    next(one_sum)
 
     def norm_one(index, total):
         rows = pl.ds(pl.multiple_of(index * CHUNK, CHUNK), CHUNK)
@@ -960,39 +1018,25 @@
 
     r.flat_move[0, 0:1] = lax.fori_loop(0, chunks, norm_one, jnp.zeros((1, width), f32))
 
-    for k, bit in enumerate(bits):
-        side, partner = flipped(me, bit)
-        work = getattr(r, f"small_work{k}")
-        away, land = getattr(r, f"small_away{k}"), getattr(r, f"small_land{k}")
-        away[...] = work[:, 1 - side].astype(bf16)
-        copy = sent(away, land, r.last_sends, r.last_receives, 2 * k, "seq", partner)
-        flat = sent(r.flat_move.at[k], r.flat_land.at[k], r.last_sends, r.last_receives, 2 * k + 1,
-                    "seq", partner)
-        step()
-        copy.wait()
-        total = work[:, side] + land[...].astype(f32)
-        flat.wait()
-        if k + 1 < len(bits):
-            target = getattr(r, f"small_work{k + 1}")
-            target[...] = total.reshape(target.shape)
-            r.flat_move[k + 1] = r.flat_move[k] + r.flat_land[k]
-        else:
-            r.small_out[...] = total.reshape(r.small_out.shape)
-            r.flat_out[...] = r.flat_move[k] + r.flat_land[k]
-    while queue:
-        step()
-    pending = [down, gate, up, out, gin, cin]
-    while any(item.stage <= n_bits for item in pending):
+    flat_sum = flat_summed()
+    next(flat_sum)
+    next(small_sum)
+    gin.next()
+    down.next()
+    next(flat_sum)
+    gate.next()
+    next(small_sum)
+    up.next()
+    cin.next()
+    for waiting in (flat_sum, small_sum):
+        for _ in waiting:
+            pass
+    pending = [out, gin, cin, down, gate, up]
+    for _ in range(len(bits)):
         for item in pending:
-            advance(item)
-    for copy in written:
-        copy.wait()
-
-
-class Done:
-    @staticmethod
-    def wait():
-        return None
+            item.next()
+    for item in pending:
+        item.written.wait()
 
 
 def backward(ins, hbm_ins, count, ident):
@@ -1012,91 +1056,113 @@
     def full(*dims):
         return pltpu.VMEM(dims, f32)
 
-    outs = {
-        "stream_grad": (shape_of(tokens, width), VMEM),
-        "out_rows": (shape_of(tokens, width, dtype=bf16), VMEM),
-        "small_out": (shape_of(rows_out, tokens), VMEM),
-        "flat_out": (shape_of(8, width), VMEM),
-        "down_out": (shape_of(rows_down, width), ANY),
-        "gate_out": (shape_of(rows_in, hid), ANY),
-        "up_out": (shape_of(rows_in, hid), ANY),
-        "out_out": (shape_of(rows_out, width), ANY),
-        "gin_out": (shape_of(rows_in, channels), ANY),
-        "cin_out": (shape_of(rows_in, channels), ANY),
-    }
-    scratch = {
-        "left_hidden": low(half, rows_down, 2 * tokens),
-        "left_two": low(half, rows_in, 2 * tokens),
-        "left_one": low(half, rows_in, 2 * tokens),
-        "left_gated": low(half, rows_out, 2 * tokens),
-        "right_down": low(2 * tokens, width),
-        "right_two": low(2 * tokens, 2 * hid),
-        "right_out": low(2 * tokens, width),
-        "right_in": low(2 * tokens, 2 * channels),
-        "mixer": low(2, 2, quarter, width),
-        "weights": low(channels, width),
-        "scan": rows, "step": rows, "drive": rows, "push": rows,
-        "decay_rows": full(tokens, 128),
-        "into": full(tokens, states, 128), "out_of": full(tokens, states, 128),
-        "into_wide": full(tokens, states, 128), "out_wide": full(tokens, states, 128),
-        "hist": full(2, tokens, states, 128),
-        "step_sum": full(8, channels), "starts": full(states, channels),
-        "rate_sum": full(states, channels),
-        "step_low_grad": low(tokens, channels),
-        "chain_move": full(len(bits), states + 8, channels),
-        "chain_land": full(len(bits), states + 8, channels),
-        "part": low(2, 2, quarter, width), "total": low(2, 2, quarter, width),
-        "first_land": low(2, quarter, width), "second_land": low(quarter, width),
-        "second_move": low(quarter, width),
-        "raw_move": full(2, tokens, narrow), "raw_land": full(2, tokens, narrow),
-        "raw_low": low(tokens, narrow), "step_low": low(tokens, rank),
-        "grad_pre": full(tokens + 8, channels), "extended": full(tokens + 16, channels),
-        "flat_move": full(len(bits), 8, width), "flat_land": full(len(bits), 8, width),
-    }
-    for k in range(len(bits)):
-        size = count >> (k + 1)
-        scratch[f"small_work{k}"] = full(size, 2, rows_out, tokens)
-        scratch[f"small_away{k}"] = low(size, rows_out, tokens)
-        scratch[f"small_land{k}"] = low(size, rows_out, tokens)
-    units = {
-        "down": (rows_down, width), "gate": (rows_in, hid), "up": (rows_in, hid),
-        "out": (rows_out, width), "gin": (rows_in, channels), "cin": (rows_in, channels),
-    }
-    for name, (part, columns) in units.items():
-        scratch[f"{name}_away"] = low(half // 2, part, columns)
-        for k in range(n_bits):
-            scratch[f"{name}_land{k}"] = low(half >> (k + 1), part, columns)
-        scratch[f"{name}_kept"] = full(half // 2, part, columns)
+    outs = dict(
+        stream_grad=(shape_of(tokens, width), VMEM),
+        out_rows=(shape_of(tokens, width, dtype=bf16), VMEM),
+        small_out=(shape_of(rows_out, tokens), VMEM),
+        flat_out=(shape_of(8, width), VMEM),
+        down_out=(shape_of(rows_down, width), ANY),
+        gate_out=(shape_of(rows_in, hid), ANY),
+        up_out=(shape_of(rows_in, hid), ANY),
+        out_out=(shape_of(rows_out, width), ANY),
+        gin_out=(shape_of(rows_in, channels), ANY),
+        cin_out=(shape_of(rows_in, channels), ANY),
+    )
+    quads = count // 4
+
+    def unit(part, columns):
+        lands = [low(half >> (k + 1), part, columns) for k in range(n_bits)]
+        return [low(half // 2, part, columns), *lands, full(half // 2, part, columns)]
 
     def sems(size):
         return pltpu.SemaphoreType.DMA((size,))
 
-    scratch |= {
-        "load_sems": sems(40), "write_sems": sems(6),
-        "pair_sends": sems(8), "pair_receives": sems(8),
-        "shared_sends": sems(4), "shared_receives": sems(4),
-        "unit_sends": sems(6 * n_bits), "unit_receives": sems(6 * n_bits),
-        "sum_sends": sems(12), "sum_receives": sems(12),
-        "chain_sends": sems(len(bits)), "chain_receives": sems(len(bits)),
-        "raw_sends": sems(3), "raw_receives": sems(3),
-        "last_sends": sems(2 * len(bits)), "last_receives": sems(2 * len(bits)),
-    }
-    names = [*ins, *hbm_ins, *outs, *scratch]
+    halves = [count >> (k + 1) for k in range(len(bits))]
+    scratch = dict(
+        left_hidden=low(quads, 2, rows_down, 2 * tokens),
+        left_two=low(quads, 2, rows_in, 2 * tokens),
+        left_one=low(quads, 2, rows_in, 2 * tokens),
+        left_gated=low(quads, 2, rows_out, 2 * tokens),
+        right_down=low(2 * tokens, width),
+        right_two=low(2 * tokens, 2 * hid),
+        right_out=low(2 * tokens, width),
+        right_in=low(2 * tokens, 2 * channels),
+        mixer=low(2, 2, quarter, width),
+        weights=low(channels, width),
+        scan=rows,
+        step=rows,
+        drive=rows,
+        push=rows,
+        decay_rows=full(tokens, 128),
+        into=full(tokens, states, 128),
+        out_of=full(tokens, states, 128),
+        into_wide=full(tokens, states, 128),
+        out_wide=full(tokens, states, 128),
+        hist=full(2, tokens, states, 128),
+        step_sum=full(8, channels),
+        starts=full(states, channels),
+        rate_sum=full(states, channels),
+        step_low_grad=low(tokens, channels),
+        chain_move=full(len(bits), states + 8, channels),
+        chain_land=full(len(bits), states + 8, channels),
+        part=low(2, 2, quarter, width),
+        total=low(2, 2, quarter, width),
+        first_land=low(2, quarter, width),
+        second_land=low(quarter, width),
+        second_move=low(quarter, width),
+        raw_move=full(2, tokens, narrow),
+        raw_land=full(2, tokens, narrow),
+        raw_low=low(tokens, narrow),
+        step_low=low(tokens, rank),
+        grad_pre=full(tokens + 8, channels),
+        extended=full(tokens + 16, channels),
+        flat_move=full(len(bits), 8, width),
+        flat_land=full(len(bits), 8, width),
+        small_work=[full(size, 2, rows_out, tokens) for size in halves],
+        small_away=[low(size, rows_out, tokens) for size in halves],
+        small_land=[low(size, rows_out, tokens) for size in halves],
+        down=unit(rows_down, width),
+        gate=unit(rows_in, hid),
+        up=unit(rows_in, hid),
+        out=unit(rows_out, width),
+        gin=unit(rows_in, channels),
+        cin=unit(rows_in, channels),
+        load_sems=sems(32),
+        write_sems=sems(6),
+        pair_sends=sems(8),
+        pair_receives=sems(8),
+        shared_sends=sems(4),
+        shared_receives=sems(4),
+        unit_sends=sems(6 * n_bits),
+        unit_receives=sems(6 * n_bits),
+        sum_sends=sems(12),
+        sum_receives=sems(12),
+        chain_sends=sems(len(bits)),
+        chain_receives=sems(len(bits)),
+        raw_sends=sems(3),
+        raw_receives=sems(3),
+        last_sends=sems(2 * len(bits)),
+        last_receives=sems(2 * len(bits)),
+    )
+    names, shapes = [(name, 0) for name in [*ins, *hbm_ins, *outs]], []
+    for name, held in scratch.items():
+        listed = isinstance(held, list)
+        names.append((name, len(held) if listed else 0))
+        shapes += held if listed else [held]
+    places = [VMEM for _ in ins]
+    places[0] = pl.BlockSpec(memory_space=pltpu.SMEM)
     made = pl.pallas_call(
         functools.partial(backward_kernel, bits, names),
         out_shape=[shape for shape, _ in outs.values()],
-        in_specs=[
-            pl.BlockSpec(memory_space=pltpu.SMEM) if name == "bounds" else VMEM for name in ins
-        ]
-        + [ANY] * len(hbm_ins),
+        in_specs=places + [ANY] * len(hbm_ins),
         out_specs=[spec for _, spec in outs.values()],
-        scratch_shapes=list(scratch.values()),
+        scratch_shapes=shapes,
         compiler_params=pltpu.CompilerParams(
             collective_id=ident, has_side_effects=True, vmem_limit_bytes=63 * 2**20
         ),
         name="block_backward",
     )(*ins.values(), *hbm_ins.values())
-    return dict(zip(outs, made))
+    return types.SimpleNamespace(**dict(zip(outs, made)))
 
 
 def rms_gain(values, gain_row):
@@ -1127,7 +1193,7 @@
     rank, (states, channels) = w_dt.shape[0], decay_logs.shape
 
     def turned(values):
-        return values.T.reshape(seq_count // 2, 2, values.shape[1] // seq_count, tokens)
+        return values.T.reshape(seq_count // 4, 2, 2, values.shape[1] // seq_count, tokens)
 
     stream_in = stream.astype(f32)
     normed_low = rms_gain(stream_in, norm_gains[0]).astype(bf16)
@@ -1156,24 +1222,23 @@
         return values.astype(bf16).reshape(2, 2, tokens // 4, width)
 
     made = backward(
-        {
-            "bounds": doc_bounds, "stream": stream, "gains": norm_gains, "proj": in_proj,
-            "halo": halo, "pre": pre_conv, "low": conv_low, "raw": raw_proj,
-            "step_pre": step_pre, "last_state": last_state, "chan": chan_vectors,
-            "logs": decay_logs, "w_x": w_x, "w_dt": w_dt, "small_gains": small_gains[None],
-        },
-        {
-            "two_part": quartered(normed_two_part), "feed_part": quartered(feed_part),
-            "mixer_in": mixer_low, "cot": cotangent, "cot_came": cot_came,
-            "gate_up_in": gate_up_low.reshape(tokens, -1), "two_in": turned(normed_two_low),
-            "hidden_in": turned(hidden_low), "gated_in": turned(gated_low), "one_in": one_in,
-            "one_came": one_came, "w_out": w_out, "w_in": w_in_flat, "scan_in": scan_out,
-            "into_in": into, "out_of_in": out_of, "hist_in": before,
-        },
+        dict(
+            bounds=doc_bounds, stream=stream, gains=norm_gains, proj=in_proj, halo=halo,
+            pre=pre_conv, low=conv_low, raw=raw_proj, step_pre=step_pre, last_state=last_state,
+            chan=chan_vectors, logs=decay_logs, w_x=w_x, w_dt=w_dt, small_gains=small_gains[None],
+        ),
+        dict(
+            two_part=quartered(normed_two_part), feed_part=quartered(feed_part),
+            mixer_in=mixer_low, cot=cotangent, cot_came=cot_came,
+            gate_up_in=gate_up_low.reshape(tokens, -1), two_in=turned(normed_two_low),
+            hidden_in=turned(hidden_low), gated_in=turned(gated_low), one_in=one_in,
+            one_came=one_came, w_out=w_out, w_in=w_in_flat, scan_in=scan_out, into_in=into,
+            out_of_in=out_of, hist_in=before,
+        ),
         seq_count,
         2,
     )
-    small, flat = made["small_out"], made["flat_out"]
+    small, flat = made.small_out, made.flat_out
     at = w_x.shape[1]
     x_part, small = small[:, :at], small[:, at:].T
     dt_part, decay_out = small[:rank], small[rank : rank + states]
@@ -1185,18 +1250,18 @@
     small_part = lax.dynamic_slice_in_dim(flat[2], me * small_width, small_width, 0)
     rms_values = jnp.sqrt(jnp.sum(flat[3:6], axis=1) / (tokens * seq_count * width))
     return (
-        made["out_rows"],
-        made["stream_grad"],
+        made.out_rows,
+        made.stream_grad,
         gains_part,
-        jnp.stack([made["cin_out"], made["gin_out"]], 1),
+        jnp.stack([made.cin_out, made.gin_out], 1),
         chan_part,
         decay_out,
         x_part,
         small_part,
         dt_part,
-        made["out_out"],
-        jnp.stack([made["gate_out"], made["up_out"]], 1),
-        made["down_out"],
+        made.out_out,
+        jnp.stack([made.gate_out, made.up_out], 1),
+        made.down_out,
         rms_values,
     )
 

time: 328 us -> 276 us (0.84)
  the two profiles are of different devices: /device:TPU:8 before, /device:TPU:0 now
where the time goes in v2:
time: 276 us
  Pallas kernels  234 us (85%)
  local copies, waits for them, and re-layouts  22 us (8%)
  matrix products  13.8 us (5%)
  other arithmetic  4.71 us (2%)
    pallas_call x1, Pallas kernels, backward(): pl.pallas_call(functools.partial(backward_kernel, bits, names), out_shape...  172 us
    pallas_call x1, Pallas kernels, mixer_forward(): pl.pallas_call(functools.partial(forward_kernel, bits), out_shape=[shape_...  62.4 us
    unnamed x42, local copies, waits for them, and re-layouts  13.8 us

profile of v2, /device:TPU:0, one launch (start us, length us, event | category | flops | bytes accessed | tf_op | source)
XLA Modules:
  0.0 275.7 jit_solution(8522596956619272707)
XLA Ops:
  0.6 0.8 slice_reduce_fusion.1
  1.5 3.3 %copy.39 = bf16[192,8,2,768]{3,1,2,0:T(8,128)(2,1)S(1)} copy(bf16[192,8,2,768]{3,2,1,0:T(2,128)(2,1)} %bitcast.64) | data formatting | bytes 9437184
  5.1 2.4 convolution_convert_fusion.1.proj.refs_3_
  7.7 1.2 copy.26
  8.9 62.4 %mixer_forward.1 = (bf16[16,768]{1,0:T(8,128)(2,1)}, f32[256,768]{1,0:T(8,128)}, bf16[256,768]{1,0:T(8,128)(2,1)}, f32[256,128]{1,0:T(8,128)}, f32[256,768]{1,0:...) custom-call(s32[2]{0:T(128)} %refs_0_.1, ...), custom_call_target="tpu_custom_call" | custom-call | flops 6000000000 | bytes 6000000 | tf_op jit(solution)/shard_map/mixer_forward/pallas_call | solution.py:330
  71.3 1.5 multiply_reduce_fusion
  73.2 5.1 %fusion.2 = f32[256,2,1024]{2,0,1:T(8,128)S(1)} fusion(bf16[1536,2,1024]{2,1,0:T(2,128)(2,1)} %param.23, bf16[256,1536]{1,0:T(8,128)(2,1)S(1)} %multiply_convert_fusion), kind=kOutput, calls=%fused_computation.2 | convolution fusion | flops 1610612736 | bytes 9175040 | tf_op jit(solution)/shard_map/td,dkf->tkf/dot_general | solution.py:1212
  78.3 1.3 multiply_bitcast_fusion
  79.9 1.1 copy.38
  80.9 3.2 %fusion.7 = bf16[256,1536]{1,0:T(8,128)(2,1)} fusion(bf16[1536,2,1024]{2,1,0:T(2,128)(2,1)S(1)} %bitcast.84, f32[256,1,1024]{2,0,1:T(8,128)S(1)} %get-tuple-element.77, f32[256,1,1024]{2,0,1:T(8,128)S(1)} %get-tuple-element.76), kind=kOutput, calls=%fused_computation.5 | convolution fusion | flops 1612054528 | bytes 9175040 | tf_op jit(solution)/shard_map/tkf,dkf->td/dot_general | solution.py:1218
  84.1 1.9 convolution_convert_fusion
  86.0 1.0 copy.31
  87.0 1.2 copy.30
  88.1 0.9 copy.32
  89.1 172.0 %block_backward.1 = (f32[256,1536]{1,0:T(8,128)}, bf16[256,1536]{1,0:T(8,128)(2,1)}, f32[96,256]{1,0:T(8,128)}, f32[8,1536]{1,0:T(8,128)}, f32[128,1536]{1,0:T(8...) custom-call(s32[2]{0:T(128)} %refs_0_.1, ...), custom_call_target="tpu_custom_call" | custom-call | tf_op jit(solution)/shard_map/block_backward/pallas_call | solution.py:1154
  261.1 1.5 pad_maximum_fusion
  262.6 2.4 copy.37
  265.0 1.9 copy.33
  267.7 0.7 copy.35
  269.1 0.7 copy.36
  271.7 0.9 copy.52
  272.6 1.1 copy.53
  274.0 0.8 copy.54
  274.9 0.9 copy.55
  (50 shorter events, 4.8 us)
Async XLA Ops:
  1.5 3.4 %copy-start = (bf16[256,1536]{1,0:T(8,128)(2,1)S(1)}, bf16[256,1536]{1,0:T(8,128)(2,1)}, u32[]{:S(2)}) copy-start(bf16[256,1536]{1,0:T(8,128)(2,1)} %refs_1_.1) | copy-start | bytes 2359300
  4.8 2.6 copy-start.1
  71.3 1.6 copy-start.2
  72.8 8.1 %slice-start = ((s8[6291456]{0:T(1024)(128)(4,1)}), s8[4194304]{0:T(1024)(128)(4,1)S(1)}, s32[]{:S(2)}) async-start(s8[6291456]{0:T(1024)(128)(4,1)} %bitcast.83), calls=%async_computation | async-start | bytes 8388608
  73.2 5.1 %copy-start.6 = (bf16[256,1536]{1,0:T(8,128)(2,1)S(1)}, bf16[256,1536]{1,0:T(8,128)(2,1)}, u32[]{:S(2)}) copy-start(bf16[256,1536]{1,0:T(8,128)(2,1)} %refs_18_.1) | copy-start | bytes 2359300
  73.2 5.1 %copy-start.13 = (bf16[1024,1536]{1,0:T(8,128)(2,1)S(1)}, bf16[1024,1536]{1,0:T(8,128)(2,1)}, u32[]{:S(2)}) copy-start(bf16[1024,1536]{1,0:T(8,128)(2,1)} %param.24) | copy-start | bytes 9437188
  73.2 7.7 %slice-start.1 = ((s8[6291456]{0:T(1024)(128)(4,1)}), s8[2097152]{0:T(1024)(128)(4,1)S(1)}, s32[]{:S(2)}) async-start(s8[6291456]{0:T(1024)(128)(4,1)} %bitcast.83), calls=%async_computation.1 | async-start | bytes 4194304
  86.0 2.2 copy-start.10
  262.5 2.4 copy-start.8
  262.6 2.4 copy-start.9
  265.0 2.0 copy-start.11
  265.0 4.8 %copy-start.12 = (f32[8,1536]{1,0:T(8,128)S(1)}, f32[8,1536]{1,0:T(8,128)}, u32[]{:S(2)}) copy-start(f32[8,1536]{1,0:T(8,128)} %get-tuple-element.53) | copy-start | bytes 147460
  265.0 6.7 %copy-start.5 = (bf16[256,1536]{1,0:T(8,128)(2,1)S(1)}, bf16[256,1536]{1,0:T(8,128)(2,1)}, u32[]{:S(2)}) copy-start(bf16[256,1536]{1,0:T(8,128)(2,1)} %get-tuple-element.94) | copy-start | bytes 2359300
  267.0 5.6 %copy-start.3 = (f32[256,1536]{1,0:T(8,128)S(1)}, f32[256,1536]{1,0:T(8,128)}, u32[]{:S(2)}) copy-start(f32[256,1536]{1,0:T(8,128)} %get-tuple-element.95) | copy-start | bytes 4718596
  272.6 1.4 copy-start.7
  272.6 2.3 copy-start.4

commit v3 on v2

--- a/solution.py
+++ b/solution.py
@@ -140,6 +140,7 @@
     mixer, hist_out, one_came, cot_came,
     extended, raw_move, raw_land, step, drive, starts, moving, landed, part, first_land,
     second_move, second_land, hist, sends, receives, hist_sem, shared_sends, shared_receives,
+    sum_sends, sum_receives,
 ):
     tokens, channels = low_out.shape
     rank, states = w_dt.shape[0], logs.shape[0]
@@ -170,8 +171,6 @@
         for k, (source, target) in enumerate(shared)
     ]
     rates = -jnp.exp(logs[...]) * LOG2E
-    halo_copy.wait()
-    extended[0:16] = halo[...].astype(f32)
 
     def spread(index, _):
         first = pl.multiple_of(index * CHUNK, CHUNK)
@@ -192,7 +191,10 @@
         low_out[pl.ds(first, CHUNK)] = (summed * sigmoid(summed)).astype(bf16)
         return 0
 
-    lax.fori_loop(0, chunks, convolved, 0)
+    lax.fori_loop(1, chunks, convolved, 0)
+    halo_copy.wait()
+    extended[0:16] = halo[...].astype(f32)
+    convolved(0, 0)
     raw_move[0] = jnp.dot(low_out[...], w_x[...], preferred_element_type=f32)
     sent(raw_move.at[0], raw_land.at[0], sends, receives, 1, "ch", across).wait()
     raw_move[1] = raw_move[0] + raw_land[0]
@@ -283,38 +285,26 @@
         )
 
     def mixed(index, _):
-        first = pl.multiple_of(index * 512, 512)
+        first = pl.multiple_of(index * 256, 256)
         product = jnp.dot(
-            gated_out[...], w_out[:, pl.ds(first, 512)], preferred_element_type=f32
+            gated_out[...], w_out[:, pl.ds(first, 256)], preferred_element_type=f32
         ).astype(bf16)
         for k in range(4):
-            part[k // 2, k % 2, :, pl.ds(first, 512)] = product[k * quarter : (k + 1) * quarter]
+            part[k // 2, k % 2, :, pl.ds(first, 256)] = product[k * quarter : (k + 1) * quarter]
         return 0
 
-    lax.fori_loop(0, width // 512, mixed, 0)
-    four_summed(
-        part, mixer, first_land, second_land, second_move, sends, receives, 3, low, across, high,
-        along,
-    )
+    held = types.SimpleNamespace(
+        first_land=first_land, second_land=second_land, second_move=second_move, total=mixer,
+        sum_sends=sum_sends, sum_receives=sum_receives,
+    )
+    sums = [four_summed(held, (low, across, high, along), part, 0, k) for k in range(2)]
+    for k, item in enumerate(sums):
+        lax.fori_loop(k * width // 512, (k + 1) * width // 512, mixed, 0)
+        next(item)
+    for _ in in_turn(*sums):
+        pass
     for copy in hist_copies + shared_copies:
         copy.wait()
-
-
-def four_summed(
-    value, total, first, second, moving, sends, receives, base, low, across, high, along
-):
-    sent(value.at[:, 1 - low], first, sends, receives, base, "ch", across).wait()
-    moving[...] = (
-        value[1 - high, low].astype(f32) + first[1 - high].astype(f32)
-    ).astype(bf16)
-    copy = sent(moving, second, sends, receives, base + 1, "ch", along)
-    kept = value[high, low].astype(f32) + first[high].astype(f32)
-    copy.wait()
-    total[high, low] = (kept + second[...].astype(f32)).astype(bf16)
-    own = total.at[high, low]
-    sent(own, own, sends, receives, base + 2, "ch", along).wait()
-    both = total.at[:, low]
-    sent(both, both, sends, receives, base + 3, "ch", across).wait()
 
 
 def mixer_forward(bounds, proj, chan, logs, w_x, gains, w_dt, w_out, one_in, cot, count, ident):
@@ -348,6 +338,7 @@
             pltpu.SemaphoreType.DMA((7 + len(bits),)), pltpu.SemaphoreType.DMA((7 + len(bits),)),
             pltpu.SemaphoreType.DMA((channels // LANES,)),
             pltpu.SemaphoreType.DMA((4,)), pltpu.SemaphoreType.DMA((4,)),
+            pltpu.SemaphoreType.DMA((8,)), pltpu.SemaphoreType.DMA((8,)),
         ],
         compiler_params=pltpu.CompilerParams(
             collective_id=ident, has_side_effects=True, vmem_limit_bytes=56 * 2**20
@@ -381,7 +372,18 @@
         self.copy = self.start(0, partner)
         self.make(mine, self.kept)
 
-    def next(self):
+    def begun(self):
+        _, partner = flipped(lax.axis_index("seq"), self.bits[0])
+        self.stage = 1
+        self.copy = self.start(0, partner)
+
+    def resume(self):
+        self.stage = 2
+        if len(self.bits) > 1:
+            _, partner = flipped(lax.axis_index("seq"), self.bits[1])
+            self.copy = self.start(1, partner)
+
+    def next(self, send_on=True):
         stage, me = self.stage, lax.axis_index("seq")
         if stage > len(self.bits):
             return
@@ -415,7 +417,8 @@
             return 0
 
         lax.fori_loop(0, (count // 2) * parts, send, 0)
-        self.copy = self.start(stage, partner)
+        if send_on:
+            self.copy = self.start(stage, partner)
 
         def keep(step, _):
             index = lax.div(step, parts)
@@ -433,21 +436,25 @@
 
     def make(self, side, target):
         first, width = self.columns
-        tile = 512 if width % 512 == 0 else 256
+        tile = width if width <= 512 else 512 if width % 512 == 0 else 384
         tiles = width // tile
+        count, rows = target.shape[:2]
+        together = count if rows % 16 == 0 else 1
 
         def block(step, _):
             index = lax.div(step, tiles)
             column = pl.multiple_of(lax.rem(step, tiles) * tile, tile)
+            left = self.left[:, side] if together > 1 else self.left[pl.ds(index, 1), side]
             product = jnp.dot(
-                self.left[index, side],
+                left.reshape(together * rows, left.shape[2]),
                 self.right[:, pl.ds(first + column, tile)],
                 preferred_element_type=f32,
-            )
-            target[index, :, pl.ds(column, tile)] = product.astype(target.dtype)
+            ).astype(target.dtype)
+            at = pl.ds(0, count) if together > 1 else pl.ds(index, 1)
+            target[at, :, pl.ds(column, tile)] = product.reshape(together, rows, tile)
             return 0
 
-        lax.fori_loop(0, target.shape[0] * tiles, block, 0)
+        lax.fori_loop(0, count // together * tiles, block, 0)
 
 
 def norm_back(values, scale, gains, grad, free=True):
@@ -497,6 +504,272 @@
         taken, refs = refs[: count or 1], refs[count or 1 :]
         found[name] = taken if count else taken[0]
     return types.SimpleNamespace(**found)
+
+
+def four_summed(r, place, value, base, part):
+    low, across, high, along = place
+    half = value.shape[3] // 2
+    cols = pl.ds(part * half, half)
+    first, second, moving = (
+        r.first_land.at[:, :, cols], r.second_land.at[:, cols], r.second_move.at[:, cols]
+    )
+    total, value = r.total.at[:, :, :, cols], value.at[:, :, :, cols]
+    sends, receives, base = r.sum_sends, r.sum_receives, base + 4 * part
+    copy = sent(value.at[:, 1 - low], first, sends, receives, base, "ch", across)
+    yield
+    copy.wait()
+    moving[...] = (
+        value[1 - high, low].astype(f32) + first[1 - high].astype(f32)
+    ).astype(bf16)
+    copy = sent(moving, second, sends, receives, base + 1, "ch", along)
+    yield
+    copy.wait()
+    total[high, low] = (
+        value[high, low].astype(f32) + first[high].astype(f32) + second[...].astype(f32)
+    ).astype(bf16)
+    own = total.at[high, low]
+    copy = sent(own, own, sends, receives, base + 2, "ch", along)
+    yield
+    copy.wait()
+    both = total.at[:, low]
+    copy = sent(both, both, sends, receives, base + 3, "ch", across)
+    yield
+    copy.wait()
+    yield
+
+
+def in_turn(*steps):
+    for _ in range(4):
+        yield
+        for item in steps:
+            next(item)
+    yield
+
+
+def feed_forward_kernel(bits, names, *refs):
+    r = named(names, refs)
+    tokens, width = r.stream.shape
+    quarter, chunks, seq_count = tokens // 4, tokens // CHUNK, 1 << len(bits)
+    ch_me, me = lax.axis_index("ch"), lax.axis_index("seq")
+    low, across = flipped(ch_me, 1)
+    high, along = flipped(ch_me, 2)
+    pair_bit, rest_bits = bits[1], [bits[0], *bits[2:]]
+    mine, pair = flipped(me, pair_bit)
+    hid = r.w_down_in.shape[0]
+    tile = 256
+    tiles = range(0, hid, tile)
+    own, other = pl.ds(0, tokens), pl.ds(tokens, tokens)
+    slots = []
+
+    def load(source, target):
+        copy = pltpu.make_async_copy(source, target, r.load_sems.at[len(slots)])
+        copy.start()
+        slots.append(0)
+        return Once(copy)
+
+    cot_own = load(r.cot, r.right_down.at[own])
+    loads = []
+    for at in tiles:
+        loads.append(
+            [
+                load(r.w_gate_up_in.at[:, pl.ds(at, tile)], r.w_gate_up.at[:, pl.ds(at, tile)]),
+                load(
+                    r.w_gate_up_in.at[:, pl.ds(hid + at, tile)],
+                    r.w_gate_up.at[:, pl.ds(hid + at, tile)],
+                ),
+                load(r.w_down_in.at[pl.ds(at, tile)], r.w_down.at[pl.ds(at, tile)]),
+            ]
+        )
+    cot_other = load(r.cot_came, r.right_down.at[other])
+    greeted(
+        [("ch", across), ("ch", along), ("seq", pair), ("seq", flipped(me, rest_bits[0])[1])]
+    )
+
+    def norm_two(index, _):
+        rows = pl.ds(pl.multiple_of(index * CHUNK, CHUNK), CHUNK)
+        per = quarter // CHUNK
+        part = lax.div(index, per)
+        at = pl.ds(pl.multiple_of(lax.rem(index, per) * CHUNK, CHUNK), CHUNK)
+        mixed = r.mixer[lax.div(part, 2), lax.rem(part, 2), at].astype(f32)
+        middle = r.stream[rows].astype(f32) + mixed
+        scale = lax.rsqrt(mean_square(middle) + 1e-06)
+        r.normed[rows] = (middle * scale * r.gains[1:2]).astype(bf16)
+        return 0
+
+    lax.fori_loop(0, chunks, norm_two, 0)
+
+    def turn(values, first, turned):
+        rows = turned.shape[3]
+        across_rows = values.T
+        for k in range(values.shape[1] // rows):
+            owner = first // rows + k
+            turned[owner // 4, (owner // 2) % 2, owner % 2] = across_rows[
+                k * rows : (k + 1) * rows
+            ]
+
+    group = 384
+    for at in range(0, width, group):
+        turn(r.normed[:, at : at + group], at, r.two_turned)
+    half = r.two_turned.shape[0] // 2
+    some = pl.ds(low * half, half)
+    target = r.left_two.at[some, :, :, other]
+    two_copy = sent(
+        r.two_turned.at[some, 1 - mine], target, r.pair_sends, r.pair_receives, 0, "seq", pair
+    )
+    r.left_two[:, :, :, own] = r.two_turned[:, mine]
+    cot_own.wait()
+    hidden_copies, quads_sent = [], 0
+    for number, at in enumerate(tiles):
+        for item in loads[number]:
+            item.wait()
+        gate = jnp.dot(
+            r.normed[...], r.w_gate_up[:, pl.ds(at, tile)], preferred_element_type=f32
+        )
+        up = jnp.dot(
+            r.normed[...], r.w_gate_up[:, pl.ds(hid + at, tile)], preferred_element_type=f32
+        )
+        part = sigmoid(gate)
+        act = gate * part
+        hidden = (act * up).astype(bf16)
+        r.hidden[:, pl.ds(at, tile)] = hidden
+        turn(hidden, at, r.hidden_turned)
+        grad = dot_rows(r.right_down[own], r.w_down[pl.ds(at, tile)])
+        r.right_two[own, pl.ds(at, tile)] = (
+            grad * up * (part * (1.0 + gate * (1.0 - part)))
+        ).astype(bf16)
+        r.right_two[own, pl.ds(hid + at, tile)] = (grad * act).astype(bf16)
+        quads = (at + tile) // r.hidden_turned.shape[3] // 4
+        if quads > quads_sent:
+            some = pl.ds(quads_sent, quads - quads_sent)
+            hidden_copies.append(
+                sent(
+                    r.hidden_turned.at[some, 1 - mine], r.left_hidden.at[some, :, :, other],
+                    r.pair_sends, r.pair_receives, 3 + len(hidden_copies), "seq", pair,
+                )
+            )
+            quads_sent = quads
+    gate_copy = sent(
+        r.right_two.at[own, pl.ds(0, hid)], r.right_two.at[other, pl.ds(0, hid)], r.pair_sends,
+        r.pair_receives, 1, "seq", pair,
+    )
+    r.left_hidden[:, :, :, own] = r.hidden_turned[:, mine]
+
+    def store(values, target, at):
+        for k in range(4):
+            target[k // 2, k % 2, :, pl.ds(at, tile)] = values[k * quarter : (k + 1) * quarter]
+
+    def two_part(index, _):
+        at = pl.multiple_of(index * tile, tile)
+        store(dot_rows(r.right_two[own], r.w_gate_up[pl.ds(at, tile)]).astype(bf16), r.part, at)
+        return 0
+
+    sums = [four_summed(r, (low, across, high, along), r.part, 0, k) for k in range(2)]
+    for k, item in enumerate(sums):
+        lax.fori_loop(k * width // (2 * tile), (k + 1) * width // (2 * tile), two_part, 0)
+        next(item)
+    total = in_turn(*sums)
+    next(total)
+
+    def feed_part(index, _):
+        at = pl.multiple_of(index * tile, tile)
+        product = jnp.dot(
+            r.hidden[...], r.w_down[:, pl.ds(at, tile)], preferred_element_type=f32
+        )
+        store(product.astype(bf16), r.feed_part, at)
+        return 0
+
+    n_bits = len(rest_bits)
+    part = width // 2
+    down, down_late = (
+        Unit(r.left_hidden, r.right_down, (k * part, part), r.down, r.unit_sends,
+             r.unit_receives, 0, rest_bits, None)
+        for k in range(2)
+    )
+    next(total)
+    cot_other.wait()
+    down.made(*hidden_copies).go()
+    next(total)
+    lax.fori_loop(0, width // tile, feed_part, 0)
+    next(total)
+    side, _ = flipped(me, rest_bits[0])
+    down_late.make(1 - side, r.late_away)
+    down_late.make(side, r.late_kept)
+    two_copy.wait()
+    two_copy = sent(target, target, r.pair_sends, r.pair_receives, 2, "ch", across)
+    next(total)
+    two_copy.wait()
+    gate_copy.wait()
+    if n_bits > 1:
+        down.next(send_on=False)
+    r.down_away[...] = down.away[1][...]
+    kept = r.down_kept.shape[0]
+    r.down_kept[...] = down.kept[0:kept]
+
+
+def feed_forward(ins, hbm_ins, count, ident):
+    bits = bits_of(count)
+    n_bits = len(bits) - 1
+    tokens, width = ins["stream"].shape
+    hid = hbm_ins["w_down_in"].shape[0]
+    half, quarter = count // 2, tokens // 4
+    rows_in, rows_down = width // count, hid // count
+
+    def low(*dims):
+        return pltpu.VMEM(dims, bf16)
+
+    def sems(size):
+        return pltpu.SemaphoreType.DMA((size,))
+
+    lands = [low(half >> (k + 1), rows_down, width // 2) for k in range(n_bits)]
+    outs = dict(
+        total=shape_of(2, 2, quarter, width, dtype=bf16),
+        feed_part=shape_of(2, 2, quarter, width, dtype=bf16),
+        left_two=shape_of(count // 4, 2, rows_in, 2 * tokens, dtype=bf16),
+        right_two=shape_of(2 * tokens, 2 * hid, dtype=bf16),
+        down_away=shape_of(half >> 2, rows_down, width // 2, dtype=bf16),
+        down_kept=shape_of(half >> 2, rows_down, width // 2),
+        late_away=shape_of(half >> 1, rows_down, width // 2, dtype=bf16),
+        late_kept=shape_of(half >> 1, rows_down, width // 2),
+    )
+    scratch = dict(
+        w_gate_up=low(width, 2 * hid),
+        w_down=low(hid, width),
+        normed=low(tokens, width),
+        hidden=low(tokens, hid),
+        two_turned=low(count // 4, 2, 2, rows_in, tokens),
+        hidden_turned=low(count // 4, 2, 2, rows_down, tokens),
+        left_hidden=low(count // 4, 2, rows_down, 2 * tokens),
+        right_down=low(2 * tokens, width),
+        part=low(2, 2, quarter, width),
+        first_land=low(2, quarter, width),
+        second_land=low(quarter, width),
+        second_move=low(quarter, width),
+        down=[low(half // 2, rows_down, width // 2), *lands, pltpu.VMEM((half // 2, rows_down, width // 2), f32)],
+        load_sems=sems(2 + 3 * (hid // 256)),
+        pair_sends=sems(7),
+        pair_receives=sems(7),
+        sum_sends=sems(8),
+        sum_receives=sems(8),
+        unit_sends=sems(n_bits),
+        unit_receives=sems(n_bits),
+    )
+    names, shapes = [(name, 0) for name in [*ins, *hbm_ins, *outs]], []
+    for name, held in scratch.items():
+        listed = isinstance(held, list)
+        names.append((name, len(held) if listed else 0))
+        shapes += held if listed else [held]
+    made = pl.pallas_call(
+        functools.partial(feed_forward_kernel, bits, names),
+        out_shape=list(outs.values()),
+        in_specs=[VMEM] * len(ins) + [ANY] * len(hbm_ins),
+        out_specs=[VMEM] * len(outs),
+        scratch_shapes=shapes,
+        compiler_params=pltpu.CompilerParams(
+            collective_id=ident, has_side_effects=True, vmem_limit_bytes=56 * 2**20
+        ),
+        name="feed_forward",
+    )(*ins.values(), *hbm_ins.values())
+    return types.SimpleNamespace(**dict(zip(outs, made)))
 
 
 def backward_kernel(bits, names, *refs):
@@ -523,19 +796,23 @@
         return Once(copy)
 
     own, other = pl.ds(0, tokens), pl.ds(tokens, tokens)
-    high_count = r.left_two.shape[0]
-    hid = r.right_two.shape[1] // 2
-    part_in = load(r.two_part, r.part)
-    hidden_own = load(r.hidden_in.at[:, mine], r.left_hidden.at[:, :, :, own])
-    cot_own = load(r.cot, r.right_down.at[own])
-    cot_other = load(r.cot_came, r.right_down.at[other])
-    gate_up_own = load(r.gate_up_in, r.right_two.at[own])
-    two_own = load(r.two_in.at[:, mine], r.left_two.at[:, :, :, own])
     mixer_own = load(r.mixer_in, r.mixer)
+    cot_own = load(r.cot, r.cot_rows)
     weights = load(r.w_out, r.weights)
     scan_own = load(r.scan_in, r.scan)
     out_of_own = load(r.out_of_in, r.out_of)
     into_own = load(r.into_in, r.into)
+    hid = r.right_two_in.shape[1] // 2
+    down_away = load(r.down_away_in, r.down[0].at[pl.ds(0, r.down_away_in.shape[0])])
+    late_away = load(r.late_away_in, r.late[0])
+    two_own = load(r.left_two_in, r.left_two)
+    gate_up_own = load(r.right_two_in.at[own], r.right_two.at[own])
+    gate_other = load(
+        r.right_two_in.at[other, pl.ds(0, hid)], r.right_two.at[other, pl.ds(0, hid)]
+    )
+    down_kept = load(r.down_kept_in, r.down[-1].at[pl.ds(0, r.down_kept_in.shape[0])])
+    late_kept = load(r.late_kept_in, r.late[-1])
+    part_in = load(r.feed_part, r.part)
     one_own = load(r.one_in.at[:, mine], r.left_one.at[:, :, :, own])
     one_other = load(r.one_came, r.left_one.at[:, :, :, other])
     gated_own = load(r.gated_in.at[:, mine], r.left_gated.at[:, :, :, own])
@@ -577,44 +854,41 @@
             writer(target),
         )
 
-    down = unit(r.left_hidden, r.right_down, (0, width), r.down, 0, r.down_out)
-    gate = unit(r.left_two, r.right_two, (0, hid), r.gate, 1, r.gate_out)
-    up = unit(r.left_two, r.right_two, (hid, hid), r.up, 2, r.up_out)
-    out = unit(r.left_gated, r.right_out, (0, width), r.out, 3, r.out_out)
-    gin = unit(r.left_one, r.right_in, (channels, channels), r.gin, 4, r.gin_out)
-    cin = unit(r.left_one, r.right_in, (0, channels), r.cin, 5, r.cin_out)
-
-    some = pl.ds(low * (high_count // 2), high_count // 2)
-    hidden_other = swap(r.hidden_in.at[:, 1 - mine], r.left_hidden.at[:, :, :, other])
-    two_other = swap_shared(r.two_in.at[some, 1 - mine], r.left_two.at[some, :, :, other])
-    gate_other = swap(r.gate_up_in.at[:, pl.ds(0, hid)], r.right_two.at[other, pl.ds(0, hid)])
-    up_other = swap(r.gate_up_in.at[:, pl.ds(hid, hid)], r.right_two.at[other, pl.ds(hid, hid)])
-
-    sums = (r.first_land, r.second_land, r.second_move, r.sum_sends, r.sum_receives)
-
-    def summed(value, base):
-        first, second, moving, sends, receives = sums
-        copy = sent(value.at[:, 1 - low], first, sends, receives, base, "ch", across)
-        yield
-        copy.wait()
-        moving[...] = (
-            value[1 - high, low].astype(f32) + first[1 - high].astype(f32)
-        ).astype(bf16)
-        copy = sent(moving, second, sends, receives, base + 1, "ch", along)
-        yield
-        copy.wait()
-        r.total[high, low] = (
-            value[high, low].astype(f32) + first[high].astype(f32) + second[...].astype(f32)
-        ).astype(bf16)
-        part = r.total.at[high, low]
-        copy = sent(part, part, sends, receives, base + 2, "ch", along)
-        yield
-        copy.wait()
-        both = r.total.at[:, low]
-        copy = sent(both, both, sends, receives, base + 3, "ch", across)
-        yield
-        copy.wait()
-        yield
+    part = width // 2
+    down, late = (
+        unit(None, None, None, refs, k, r.down_out.at[:, pl.ds(k * part, part)])
+        for k, refs in enumerate((r.down, r.late))
+    )
+    part = hid // 2
+    quarters = [
+        unit(
+            r.left_two, r.right_two, (k * part, part), refs, 2 + k,
+            (r.gate_out, r.up_out)[k // 2].at[:, pl.ds(k % 2 * part, part)],
+        )
+        for k, refs in enumerate((r.gate0, r.gate1, r.up0, r.up1))
+    ]
+    gate0, gate1, up0, up1 = quarters
+    out = unit(r.left_gated, r.right_out, (0, width), r.out, 6, r.out_out)
+    gin = unit(r.left_one, r.right_in, (channels, channels), r.gin, 7, r.gin_out)
+    part = channels // 2
+    cins = [
+        unit(
+            r.left_one, r.right_in, (k * part, part), refs, 8 + k,
+            r.cin_out.at[:, pl.ds(k * part, part)],
+        )
+        for k, refs in enumerate((r.cin0, r.cin1))
+    ]
+
+    up_other = swap(
+        r.right_two_in.at[own, pl.ds(hid, hid)], r.right_two.at[other, pl.ds(hid, hid)]
+    )
+    down_away.wait()
+    down.resume()
+    late_away.wait()
+    late.begun()
+
+    summed = functools.partial(four_summed, r, (low, across, high, along))
+
 
     rates = -jnp.exp(r.logs[...]) * LOG2E
 
@@ -637,17 +911,9 @@
             lax.fori_loop(0, chunks, body, jnp.zeros((1, channels), f32)), (8, channels)
         )
 
-    part_in.wait()
-    two_sum = summed(r.part, 0)
-    next(two_sum)
     resteps()
-    next(two_sum)
-    down.made(hidden_own, cot_own, cot_other, hidden_other).go()
-    next(two_sum)
-    next(two_sum)
-    next(two_sum)
-    part_in = load(r.feed_part, r.part)
     mixer_own.wait()
+    cot_own.wait()
 
     def quarter_rows(index):
         per = quarter // CHUNK
@@ -661,8 +927,8 @@
         a, b, at = quarter_rows(index)
         middle = r.stream[rows].astype(f32) + r.mixer[a, b, at].astype(f32)
         scale = lax.rsqrt(mean_square(middle) + 1e-06)
-        back, gain = norm_back(middle, scale, r.gains[1:2], r.total[a, b, at].astype(f32))
-        grad = r.right_down[rows].astype(f32) + back
+        back, gain = norm_back(middle, scale, r.gains[1:2], r.two_total[a, b, at].astype(f32))
+        grad = r.cot_rows[rows].astype(f32) + back
         r.stream_grad[rows] = grad
         r.right_out[rows] = grad.astype(bf16)
         return total + jnp.sum(gain, axis=0, keepdims=True)
@@ -728,10 +994,17 @@
 
     chain = handed()
     next(chain)
-    gate.made(two_own, gate_up_own, two_other, gate_other)
+    gate0.made(two_own, gate_up_own, gate_other)
     next(chain)
-    gate.go()
+    gate0.go()
+    gate1.made()
     next(chain)
+    late_kept.wait()
+    late.next()
+    gate1.go()
+    up0.made(up_other)
+    for _ in chain:
+        pass
     first = pl.multiple_of(low * (tokens // 2), tokens // 2)
     mixer_other = swap_shared(
         r.right_out.at[pl.ds(first, tokens // 2)],
@@ -742,12 +1015,11 @@
         r.right_in.at[own, pl.ds(channels, channels)],
         r.right_in.at[other, pl.ds(channels, channels)],
     )
-    up.made(up_other).go()
-    for _ in chain:
-        pass
+    up0.go()
+    up1.made().go()
 
     part_in.wait()
-    feed_sum = summed(r.part, 4)
+    feed_sums = [summed(r.part, 0, k) for k in range(2)]
     into_own.wait()
 
     def results():
@@ -757,13 +1029,19 @@
         for number, total in enumerate(totals):
             r.flat_move[0, 3 + number : 4 + number] = total
 
+    def feed_start():
+        for item in feed_sums:
+            next(item)
+        return in_turn(*feed_sums)
+
+    feed = []
     between = [
-        lambda: (next(feed_sum), down.next()),
-        lambda: next(feed_sum),
-        lambda: (next(feed_sum), gate.next()),
-        lambda: (next(feed_sum), out.made(gated_own, mixer_other, gated_other).go()),
-        lambda: (next(feed_sum), results()),
-        lambda: gin.made(one_own, one_other, gin_other).go(),
+        lambda: (feed.append(feed_start()), next(feed[0]), gate0.next()),
+        lambda: next(feed[0]),
+        lambda: (next(feed[0]), gate1.next()),
+        lambda: next(feed[0]),
+        lambda: (next(feed[0]), up0.next()),
+        lambda: (results(), out.made(gated_own, mixer_other, gated_other).go()),
     ]
 
     def results_of(index, totals):
@@ -843,9 +1121,11 @@
 
     lax.fori_loop(0, chunks, norm_grads, 0)
     copy = sent(r.raw_move.at[0], r.raw_land.at[0], r.raw_sends, r.raw_receives, 0, "ch", across)
+    gin.made(one_own, one_other, gin_other)
     copy.wait()
     r.raw_move[1] = r.raw_move[0] + r.raw_land[0]
     copy = sent(r.raw_move.at[1], r.raw_land.at[1], r.raw_sends, r.raw_receives, 1, "ch", along)
+    up1.next()
     copy.wait()
 
     def raw_back(index, total):
@@ -883,6 +1163,7 @@
     tap_bias = lax.fori_loop(0, chunks, conv_back, jnp.zeros((1, channels), f32))
     copy = sent(r.grad_pre.at[pl.ds(0, 8)], r.grad_pre.at[pl.ds(tokens, 8)], r.raw_sends,
                 r.raw_receives, 2, "seq", previous)
+    gin.go()
     r.extended[0:16] = r.halo[...].astype(f32)
 
     def extend(index, _):
@@ -928,10 +1209,53 @@
         return 0
 
     lax.fori_loop(0, chunks, conv_in_back, 0)
-    cin_other = swap(
-        r.right_in.at[own, pl.ds(0, channels)], r.right_in.at[other, pl.ds(0, channels)]
-    )
-
+    cin_others = [
+        swap(
+            r.right_in.at[own, pl.ds(*item.columns)], r.right_in.at[other, pl.ds(*item.columns)]
+        )
+        for item in cins
+    ]
+
+    def small_columns():
+        narrow = r.w_x.shape[1]
+        pack = r.step
+        pack[0:narrow] = lax.dot_general(
+            r.raw_low[...], r.low[...], (((0,), (0,)), ((), ())), preferred_element_type=f32
+        )
+        pack[narrow : narrow + rank] = lax.dot_general(
+            r.step_low[...], r.step_low_grad[...], (((0,), (0,)), ((), ())),
+            preferred_element_type=f32,
+        )
+        at = narrow + rank
+        pack[at : at + states] = r.rate_sum[...]
+        at += states
+        bias = jnp.sum(r.step_low_grad[...].astype(f32), axis=0, keepdims=True)
+        pack[at : at + 8] = jnp.concatenate(
+            [*tap_grads, tap_bias, bias, skip_grad, jnp.zeros((1, channels), f32)], 0
+        )
+        at += 8
+        pack[at:] = jnp.zeros((pack.shape[0] - at, channels), f32)
+        turned = pack[...].T
+        r.small_work[0][...] = turned.reshape(r.small_work[0].shape)
+
+    def small_summed():
+        for k, bit in enumerate(bits):
+            side, partner = flipped(me, bit)
+            work, away, land = r.small_work[k], r.small_away[k], r.small_land[k]
+            away[...] = work[:, 1 - side].astype(bf16)
+            copy = sent(away, land, r.last_sends, r.last_receives, k, "seq", partner)
+            yield
+            copy.wait()
+            total = work[:, side] + land[...].astype(f32)
+            target = r.small_work[k + 1] if k + 1 < len(bits) else r.small_out
+            target[...] = total.reshape(target.shape)
+        yield
+
+    small_columns()
+    small_sum = small_summed()
+    next(small_sum)
+
+    one_sums = [summed(r.part, 8, k) for k in range(2)]
     for number in range(width // channels):
         weights.wait()
 
@@ -945,93 +1269,70 @@
             return 0
 
         lax.fori_loop(0, channels // 256, one_part, 0)
+        next(one_sums[number])
         if (number + 1) * channels < width:
             weights = load(r.w_in.at[pl.ds((number + 1) * channels, channels)], r.weights)
-    one_sum = summed(r.part, 8)
+    one_sum = in_turn(*one_sums)
     next(one_sum)
 
-    def small_columns():
-        narrow = r.w_x.shape[1]
-        pack = r.step
-        pack[0:narrow] = lax.dot_general(
-            r.raw_low[...], r.low[...], (((0,), (0,)), ((), ())), preferred_element_type=f32
-        )
-        pack[narrow : narrow + rank] = lax.dot_general(
-            r.step_low[...], r.step_low_grad[...], (((0,), (0,)), ((), ())),
-            preferred_element_type=f32,
-        )
-        at = narrow + rank
-        pack[at : at + states] = r.rate_sum[...]
-        at += states
-        bias = jnp.sum(r.step_low_grad[...].astype(f32), axis=0, keepdims=True)
-        pack[at : at + 8] = jnp.concatenate(
-            [*tap_grads, tap_bias, bias, skip_grad, jnp.zeros((1, channels), f32)], 0
-        )
-        at += 8
-        pack[at:] = jnp.zeros((pack.shape[0] - at, channels), f32)
-        turned = pack[...].T
-        r.small_work[0][...] = turned.reshape(r.small_work[0].shape)
-
-    def small_summed():
-        for k, bit in enumerate(bits):
-            side, partner = flipped(me, bit)
-            work, away, land = r.small_work[k], r.small_away[k], r.small_land[k]
-            away[...] = work[:, 1 - side].astype(bf16)
-            copy = sent(away, land, r.last_sends, r.last_receives, 2 * k, "seq", partner)
-            yield
-            copy.wait()
-            total = work[:, side] + land[...].astype(f32)
-            target = r.small_work[k + 1] if k + 1 < len(bits) else r.small_out
-            target[...] = total.reshape(target.shape)
-        yield
-
-    def flat_summed():
-        for k, bit in enumerate(bits):
-            _, partner = flipped(me, bit)
-            copy = sent(r.flat_move.at[k], r.flat_land.at[k], r.last_sends, r.last_receives,
-                        2 * k + 1, "seq", partner)
-            yield
-            copy.wait()
-            target = r.flat_move.at[k + 1] if k + 1 < len(bits) else r.flat_out
-            target[...] = r.flat_move[k] + r.flat_land[k]
-        yield
-
-    small_columns()
-    next(one_sum)
-    small_sum = small_summed()
-    next(small_sum)
-    up.next()
-    next(one_sum)
-    out.next()
-    next(one_sum)
-    cin.made(cin_other).go()
-    next(one_sum)
-
-    def norm_one(index, total):
+    def gain_part(index, total):
         rows = pl.ds(pl.multiple_of(index * CHUNK, CHUNK), CHUNK)
         a, b, at = quarter_rows(index)
         value = r.stream[rows].astype(f32)
         scale = lax.rsqrt(mean_square(value) + 1e-06)
-        back, gain = norm_back(value, scale, r.gains[0:1], r.total[a, b, at].astype(f32))
-        r.stream_grad[rows] = r.stream_grad[rows] + back
-        return total + jnp.sum(gain, axis=0, keepdims=True)
-
-    r.flat_move[0, 0:1] = lax.fori_loop(0, chunks, norm_one, jnp.zeros((1, width), f32))
+        return total + jnp.sum(r.part[a, b, at].astype(f32) * value * scale, axis=0, keepdims=True)
+
+    r.flat_move[0] = r.flat_move[0] * 0.25
+    r.flat_move[0, 0:1] = lax.fori_loop(0, chunks, gain_part, jnp.zeros((1, width), f32))
+    ways = [("ch", across), ("ch", along)] + [("seq", flipped(me, bit)[1]) for bit in bits]
+
+    def flat_summed():
+        for k, (axis, partner) in enumerate(ways):
+            copy = sent(r.flat_move.at[k], r.flat_land.at[k], r.flat_sends, r.flat_receives, k,
+                        axis, partner)
+            yield
+            copy.wait()
+            target = r.flat_move.at[k + 1] if k + 1 < len(ways) else r.flat_out
+            target[...] = r.flat_move[k] + r.flat_land[k]
+        yield
 
     flat_sum = flat_summed()
+    next(flat_sum)
+
+    out.next()
+    next(one_sum)
+    next(flat_sum)
+    cins[0].made(cin_others[0]).go()
+    next(one_sum)
+    next(flat_sum)
+    cins[1].made(cin_others[1]).go()
+    next(one_sum)
     next(flat_sum)
     next(small_sum)
     gin.next()
-    down.next()
+    next(one_sum)
+
+    def norm_one(index, _):
+        rows = pl.ds(pl.multiple_of(index * CHUNK, CHUNK), CHUNK)
+        a, b, at = quarter_rows(index)
+        value = r.stream[rows].astype(f32)
+        scale = lax.rsqrt(mean_square(value) + 1e-06)
+        back, _ = norm_back(value, scale, r.gains[0:1], r.total[a, b, at].astype(f32))
+        r.stream_grad[rows] = r.stream_grad[rows] + back
+        return 0
+
+    lax.fori_loop(0, chunks, norm_one, 0)
+    down_kept.wait()
+    for item in (down, late, *quarters):
+        item.next()
+    cins[0].next()
     next(flat_sum)
-    gate.next()
     next(small_sum)
-    up.next()
-    cin.next()
+    cins[1].next()
     for waiting in (flat_sum, small_sum):
         for _ in waiting:
             pass
-    pending = [out, gin, cin, down, gate, up]
+    pending = [out, gin, *cins, down, late, *quarters]
     for _ in range(len(bits)):
         for item in pending:
             item.next()
@@ -1044,7 +1345,7 @@
     n_bits = len(bits) - 1
     tokens, width = ins["stream"].shape
     channels, rank, states = ins["low"].shape[1], ins["w_dt"].shape[0], ins["logs"].shape[0]
-    hid = hbm_ins["gate_up_in"].shape[1] // 2
+    hid = hbm_ins["right_two_in"].shape[1] // 2
     narrow = ins["w_x"].shape[1]
     half, quarter = count // 2, tokens // 4
     rows_in, rows_out, rows_down = width // count, channels // count, hid // count
@@ -1079,11 +1380,10 @@
 
     halves = [count >> (k + 1) for k in range(len(bits))]
     scratch = dict(
-        left_hidden=low(quads, 2, rows_down, 2 * tokens),
         left_two=low(quads, 2, rows_in, 2 * tokens),
         left_one=low(quads, 2, rows_in, 2 * tokens),
         left_gated=low(quads, 2, rows_out, 2 * tokens),
-        right_down=low(2 * tokens, width),
+        cot_rows=low(tokens, width),
         right_two=low(2 * tokens, 2 * hid),
         right_out=low(2 * tokens, width),
         right_in=low(2 * tokens, 2 * channels),
@@ -1116,33 +1416,39 @@
         step_low=low(tokens, rank),
         grad_pre=full(tokens + 8, channels),
         extended=full(tokens + 16, channels),
-        flat_move=full(len(bits), 8, width),
-        flat_land=full(len(bits), 8, width),
+        flat_move=full(2 + len(bits), 8, width),
+        flat_land=full(2 + len(bits), 8, width),
         small_work=[full(size, 2, rows_out, tokens) for size in halves],
         small_away=[low(size, rows_out, tokens) for size in halves],
         small_land=[low(size, rows_out, tokens) for size in halves],
-        down=unit(rows_down, width),
-        gate=unit(rows_in, hid),
-        up=unit(rows_in, hid),
+        down=unit(rows_down, width // 2),
+        late=unit(rows_down, width // 2),
+        gate0=unit(rows_in, hid // 2),
+        gate1=unit(rows_in, hid // 2),
+        up0=unit(rows_in, hid // 2),
+        up1=unit(rows_in, hid // 2),
         out=unit(rows_out, width),
         gin=unit(rows_in, channels),
-        cin=unit(rows_in, channels),
+        cin0=unit(rows_in, channels // 2),
+        cin1=unit(rows_in, channels // 2),
         load_sems=sems(32),
-        write_sems=sems(6),
+        write_sems=sems(10),
         pair_sends=sems(8),
         pair_receives=sems(8),
         shared_sends=sems(4),
         shared_receives=sems(4),
-        unit_sends=sems(6 * n_bits),
-        unit_receives=sems(6 * n_bits),
-        sum_sends=sems(12),
-        sum_receives=sems(12),
+        unit_sends=sems(10 * n_bits),
+        unit_receives=sems(10 * n_bits),
+        sum_sends=sems(16),
+        sum_receives=sems(16),
         chain_sends=sems(len(bits)),
         chain_receives=sems(len(bits)),
         raw_sends=sems(3),
         raw_receives=sems(3),
-        last_sends=sems(2 * len(bits)),
-        last_receives=sems(2 * len(bits)),
+        last_sends=sems(len(bits)),
+        last_receives=sems(len(bits)),
+        flat_sends=sems(2 + len(bits)),
+        flat_receives=sems(2 + len(bits)),
     )
     names, shapes = [(name, 0) for name in [*ins, *hbm_ins, *outs]], []
     for name, held in scratch.items():
@@ -1169,10 +1475,6 @@
     return values * lax.rsqrt(jnp.mean(values * values, axis=-1, keepdims=True) + 1e-06) * gain_row
 
 
-def swiglu(gate_up):
-    return jax.nn.silu(gate_up[:, 0]) * gate_up[:, 1]
-
-
 def local(
     seq_count,
     stream,
@@ -1207,31 +1509,27 @@
         doc_bounds, in_proj, chan_vectors, decay_logs, w_x, small_gains[None], w_dt, w_out,
         one_in, cotangent, seq_count, 1,
     )
-    middle = stream_in + mixer_low.reshape(tokens, width).astype(f32)
-    normed_two_low = rms_gain(middle, norm_gains[1]).astype(bf16)
-    gate_up = jnp.einsum("td,dkf->tkf", normed_two_low, w_gate_up, preferred_element_type=f32)
-    hidden_act, act_back = jax.vjp(swiglu, gate_up)
-    hidden_low = hidden_act.astype(bf16)
-    hidden_grad = jnp.einsum("td,fd->tf", cotangent, w_down, preferred_element_type=f32)
-    (gate_up_grad,) = act_back(hidden_grad)
-    gate_up_low = gate_up_grad.astype(bf16)
-    normed_two_part = jnp.einsum("tkf,dkf->td", gate_up_low, w_gate_up, preferred_element_type=f32)
-    feed_part = jnp.dot(hidden_low, w_down, preferred_element_type=f32)
-
-    def quartered(values):
-        return values.astype(bf16).reshape(2, 2, tokens // 4, width)
-
+    mid = feed_forward(
+        dict(stream=stream, mixer=mixer_low, gains=norm_gains),
+        dict(
+            cot=cotangent, cot_came=cot_came, w_gate_up_in=w_gate_up.reshape(width, -1),
+            w_down_in=w_down,
+        ),
+        seq_count,
+        3,
+    )
     made = backward(
         dict(
-            bounds=doc_bounds, stream=stream, gains=norm_gains, proj=in_proj, halo=halo,
+            bounds=doc_bounds, stream=stream, gains=norm_gains, two_total=mid.total,
+            proj=in_proj, halo=halo,
             pre=pre_conv, low=conv_low, raw=raw_proj, step_pre=step_pre, last_state=last_state,
             chan=chan_vectors, logs=decay_logs, w_x=w_x, w_dt=w_dt, small_gains=small_gains[None],
         ),
         dict(
-            two_part=quartered(normed_two_part), feed_part=quartered(feed_part),
-            mixer_in=mixer_low, cot=cotangent, cot_came=cot_came,
-            gate_up_in=gate_up_low.reshape(tokens, -1), two_in=turned(normed_two_low),
-            hidden_in=turned(hidden_low), gated_in=turned(gated_low), one_in=one_in,
+            feed_part=mid.feed_part, left_two_in=mid.left_two, right_two_in=mid.right_two,
+            down_away_in=mid.down_away, down_kept_in=mid.down_kept,
+            late_away_in=mid.late_away, late_kept_in=mid.late_kept, mixer_in=mixer_low,
+            cot=cotangent, gated_in=turned(gated_low), one_in=one_in,
             one_came=one_came, w_out=w_out, w_in=w_in_flat, scan_in=scan_out, into_in=into,
             out_of_in=out_of, hist_in=before,
         ),

time: 276 us -> 255 us (0.924)
  matrix products: 13.8 us -> 2.35 us
  Pallas kernels: 234 us -> 226 us
    pallas_call x1, Pallas kernels: 172 us -> 137 us  [backward(): pl.pallas_call(functools.partial(backward_kernel, bits, names), out_shape...]
    pallas_call x0 -> x1, Pallas kernels: none -> 30.1 us  [feed_forward(): pl.pallas_call(functools.partial(feed_forward_kernel, bits, names), out_s...]
    dot_general x4 -> x0, matrix products: 11.5 us -> none  [the longest x1 5.1 us: local(): jnp.einsum('td,dkf->tkf', normed_two_low, w_gate_up, preferred_element_ty...]
    unnamed x42 -> x39, local copies, waits for them, and re-layouts: 13.8 us -> 19 us
    pallas_call x1, Pallas kernels: 62.4 us -> 58.6 us  [mixer_forward(): pl.pallas_call(functools.partial(forward_kernel, bits), out_shape=[shape_...]
where the time goes in v3:
time: 255 us
  Pallas kernels  226 us (89%)
  local copies, waits for them, and re-layouts  23.1 us (9%)
  other arithmetic  2.69 us (1%)
    pallas_call x1, Pallas kernels, backward(): pl.pallas_call(functools.partial(backward_kernel, bits, names), out_shape...  137 us
    pallas_call x1, Pallas kernels, mixer_forward(): pl.pallas_call(functools.partial(forward_kernel, bits), out_shape=[shape_...  58.6 us
    pallas_call x1, Pallas kernels, feed_forward(): pl.pallas_call(functools.partial(feed_forward_kernel, bits, names), out_s...  30.1 us
    unnamed x39, local copies, waits for them, and re-layouts  19 us

profile of v3, /device:TPU:0, one launch (start us, length us, event | category | flops | bytes accessed | tf_op | source)
XLA Modules:
  0.0 254.9 jit_solution(4288097478483356273)
XLA Ops:
  0.7 3.3 %copy.33 = bf16[192,8,2,768]{3,1,2,0:T(8,128)(2,1)S(1)} copy(bf16[192,8,2,768]{3,2,1,0:T(2,128)(2,1)} %bitcast.26) | data formatting | bytes 9437184
  4.3 2.4 convolution_convert_fusion.proj.refs_4_
  6.7 0.2 fusion.3
  6.9 1.2 copy.26
  8.1 58.6 %mixer_forward.1 = (bf16[16,768]{1,0:T(8,128)(2,1)}, f32[256,768]{1,0:T(8,128)}, bf16[256,768]{1,0:T(8,128)(2,1)}, f32[256,128]{1,0:T(8,128)}, f32[256,768]{1,0:...) custom-call(s32[2]{0:T(128)} %refs_0_.3, ...), custom_call_target="tpu_custom_call" | custom-call | flops 6000000000 | bytes 6000000 | tf_op jit(solution)/shard_map/mixer_forward/pallas_call | solution.py:320
  66.8 5.2 %copy.34 = bf16[192,8,2,1024]{3,1,2,0:T(8,128)(2,1)} copy(bf16[192,8,2,1024]{3,2,1,0:T(2,128)(2,1)S(1)} %bitcast.25) | data formatting | bytes 12582912
  72.0 30.1 %feed_forward.1 = (bf16[2,2,64,1536]{3,2,1,0:T(8,128)(2,1)}, bf16[2,2,64,1536]{3,2,1,0:T(8,128)(2,1)}, bf16[2,2,192,512]{3,2,1,0:T(8,128)(2,1)}, bf16[512,2048]{...) custom-call(bf16[256,1536]{1,0:T(8,128)(2,1)} %refs_1_.1, ...), custom_call_target="tpu_custom_call" | custom-call | tf_op jit(solution)/shard_map/feed_forward/pallas_call | solution.py:761
  102.1 0.9 copy.27
  103.0 137.2 %block_backward.1 = (f32[256,1536]{1,0:T(8,128)}, bf16[256,1536]{1,0:T(8,128)(2,1)}, f32[96,256]{1,0:T(8,128)}, f32[8,1536]{1,0:T(8,128)}, f32[128,1536]{1,0:T(8...) custom-call(s32[2]{0:T(128)} %refs_0_.3, ...), custom_call_target="tpu_custom_call" | custom-call | tf_op jit(solution)/shard_map/block_backward/pallas_call | solution.py:1460
  240.3 1.5 pad_maximum_fusion
  241.8 2.4 copy.32
  244.2 1.9 copy.28
  246.2 0.6 fusion.5
  246.9 0.7 copy.30
  247.6 0.7 copy.29
  248.3 0.7 copy.31
  249.0 0.7 constant_dynamic-slice_fusion
  249.7 0.6 dynamic-slice_bitcast_fusion
  250.4 0.5 multiply_sqrt_fusion
  250.9 0.9 copy.39
  251.8 1.1 copy.40
  252.9 0.3 copy-done.5
  253.2 0.8 copy.41
  254.0 0.9 copy.42
  (37 shorter events, 0.7 us)
Async XLA Ops:
  0.6 3.4 %copy-start.10 = (f32[2,1536]{1,0:T(2,128)S(1)}, f32[2,1536]{1,0:T(2,128)}, u32[]{:S(2)}) copy-start(f32[2,1536]{1,0:T(2,128)} %refs_2_.3) | copy-start | bytes 36868
  0.7 3.4 %copy-start.1 = (bf16[256,1536]{1,0:T(8,128)(2,1)S(1)}, bf16[256,1536]{1,0:T(8,128)(2,1)}, u32[]{:S(2)}) copy-start(bf16[256,1536]{1,0:T(8,128)(2,1)} %refs_1_.1) | copy-start | bytes 2359300
  4.0 2.7 %copy-start = (bf16[192,8,2,768]{3,1,2,0:T(8,128)(2,1)}, bf16[192,8,2,768]{3,1,2,0:T(8,128)(2,1)S(1)}, u32[]{:S(2)}) copy-start(bf16[192,8,2,768]{3,1,2,0:T(8,128)(2,1)S(1)} %copy.33) | copy-start | bytes 14155780
  8.1 58.6 %slice-start = ((s8[6291456]{0:T(1024)(128)(4,1)}), s8[4194304]{0:T(1024)(128)(4,1)S(1)}, s32[]{:S(2)}) async-start(s8[6291456]{0:T(1024)(128)(4,1)} %bitcast.23), calls=%async_computation | async-start | bytes 8388608
  8.1 58.7 %slice-start.1 = ((s8[6291456]{0:T(1024)(128)(4,1)}), s8[2097152]{0:T(1024)(128)(4,1)S(1)}, s32[]{:S(2)}) async-start(s8[6291456]{0:T(1024)(128)(4,1)} %bitcast.23), calls=%async_computation.1 | async-start | bytes 4194304
  72.0 30.2 %copy-start.8 = (bf16[256,768]{1,0:T(8,128)(2,1)S(1)}, bf16[256,768]{1,0:T(8,128)(2,1)}, u32[]{:S(2)}) copy-start(bf16[256,768]{1,0:T(8,128)(2,1)} %get-tuple-element.61) | copy-start | bytes 1179652
  241.7 2.4 copy-start.6
  241.7 2.4 copy-start.7
  244.2 2.0 copy-start.9
  244.2 4.8 %copy-start.11 = (f32[8,1536]{1,0:T(8,128)S(1)}, f32[8,1536]{1,0:T(8,128)}, u32[]{:S(2)}) copy-start(f32[8,1536]{1,0:T(8,128)} %get-tuple-element.69) | copy-start | bytes 147460
  244.2 6.7 %copy-start.4 = (bf16[256,1536]{1,0:T(8,128)(2,1)S(1)}, bf16[256,1536]{1,0:T(8,128)(2,1)}, u32[]{:S(2)}) copy-start(bf16[256,1536]{1,0:T(8,128)(2,1)} %get-tuple-element.105) | copy-start | bytes 2359300
  246.2 5.6 %copy-start.2 = (f32[256,1536]{1,0:T(8,128)S(1)}, f32[256,1536]{1,0:T(8,128)}, u32[]{:S(2)}) copy-start(f32[256,1536]{1,0:T(8,128)} %get-tuple-element.106) | copy-start | bytes 4718596
  251.8 1.4 copy-start.5
  251.8 2.3 copy-start.3

commit v4 on v3

--- a/solution.py
+++ b/solution.py
@@ -112,35 +112,53 @@
     pl.semaphore_wait(barrier, len(axis_partners))
 
 
-def chained(forward, bits, state, steps, rates, moving, landed, sends, receives, base):
-    me = lax.axis_index("seq")
-    states = state.shape[0]
-    all_state, all_steps = state, steps
-    mine_state, mine_steps = jnp.zeros_like(all_state), jnp.zeros_like(all_steps)
-    for k, bit in enumerate(bits):
-        mine, partner = flipped(me, bit)
-        moving[k, :states] = all_state
-        moving[k, states:] = all_steps
-        sent(moving.at[k], landed.at[k], sends, receives, base + k, "seq", partner).wait()
-        other_state, other_steps = landed[k, :states], landed[k, states:]
-        earlier = (mine == 1) if forward else (mine == 0)
-        through = jnp.exp2(rates * mine_steps[:1])
-        mine_state = jnp.where(earlier, mine_state + through * other_state, mine_state)
-        mine_steps = jnp.where(earlier, mine_steps + other_steps, mine_steps)
-        after = jnp.exp2(rates * all_steps[:1]) * other_state + all_state
-        ahead_of = jnp.exp2(rates * other_steps[:1]) * all_state + other_state
-        all_state = jnp.where(earlier, after, ahead_of)
-        all_steps = all_steps + other_steps
-    return mine_state
+def handed_on(forward, state, steps, rates, r):
+    me, count = lax.axis_index("seq"), r.state_land.shape[0] + 1
+    r.state_move[...] = state.astype(bf16)
+    r.steps_move[...] = steps
+    copies = []
+    for k in range(1, count):
+        to = lax.rem(me + k, count)
+        for source, land, sends, receives in (
+            (r.state_move, r.state_land, r.state_sends, r.state_receives),
+            (r.steps_move, r.steps_land, r.steps_sends, r.steps_receives),
+        ):
+            copies.append(sent(source, land.at[k - 1], sends, receives, k - 1, "seq", to))
+    yield
+    for copy in copies:
+        copy.wait()
+    total = jnp.zeros_like(state)
+    passed = jnp.zeros_like(steps)
+    for k in range(1, count):
+        slot = k - 1 if forward else count - k - 1
+        valid = (me >= k) if forward else (me + k < count)
+        term = jnp.exp2(rates * passed) * r.state_land[slot].astype(f32)
+        total = total + jnp.where(valid, term, 0.0)
+        passed = passed + jnp.where(valid, r.steps_land[slot], 0.0)
+    yield total
+
+
+def handing(count, states, channels):
+    sems = pltpu.SemaphoreType.DMA((count - 1,))
+    return dict(
+        state_move=pltpu.VMEM((states, channels), bf16),
+        steps_move=pltpu.VMEM((1, channels), f32),
+        state_land=pltpu.VMEM((count - 1, states, channels), bf16),
+        steps_land=pltpu.VMEM((count - 1, 1, channels), f32),
+        state_sends=sems,
+        state_receives=sems,
+        steps_sends=sems,
+        steps_receives=sems,
+    )
 
 
 def forward_kernel(
     bits, bounds, proj, chan, logs, w_x, gains, w_dt, w_out, one_in, cot,
     halo, pre_out, low_out, raw_out, step_pre_out, into, out_of, scan_out, gated_out, last_state,
     mixer, hist_out, one_came, cot_came,
-    extended, raw_move, raw_land, step, drive, starts, moving, landed, part, first_land,
+    extended, raw_move, raw_land, step, drive, starts, part, first_land,
     second_move, second_land, hist, sends, receives, hist_sem, shared_sends, shared_receives,
-    sum_sends, sum_receives,
+    sum_sends, sum_receives, *handed,
 ):
     tokens, channels = low_out.shape
     rank, states = w_dt.shape[0], logs.shape[0]
@@ -149,10 +167,10 @@
     seq_count = 1 << len(bits)
     low, across = flipped(ch_me, 1)
     high, along = flipped(ch_me, 2)
-    following, previous = lax.rem(me + 1, seq_count), lax.rem(me + seq_count - 1, seq_count)
+    following = lax.rem(me + 1, seq_count)
     greeted(
-        [("ch", across), ("ch", along), ("seq", following), ("seq", previous)]
-        + [("seq", flipped(me, bit)[1]) for bit in bits]
+        [("ch", across), ("ch", along)]
+        + [("seq", lax.rem(me + k, seq_count)) for k in range(1, seq_count)]
     )
     halo_copy = sent(
         proj.at[pl.ds(tokens - 16, 16), pl.ds(0, channels)], halo, sends, receives, 0, "seq",
@@ -236,10 +254,10 @@
         starts[:, lanes] = lax.fori_loop(
             0, tokens // UNROLL, ended, jnp.zeros((states, LANES), f32)
         )
-    starts[...] = chained(
-        True, bits, starts[...], jnp.broadcast_to(total, (8, channels)), rates, moving, landed,
-        sends, receives, 7,
-    )
+    hand = types.SimpleNamespace(**dict(zip(handing(2, 8, 128), handed)))
+    handed_in = handed_on(True, starts[...], total, rates, hand)
+    next(handed_in)
+    starts[...] = next(handed_in)
     hist_copies = []
     for number, lanes in enumerate(blocks):
         block_rates = rates[:, lanes]
@@ -315,7 +333,6 @@
     rows = shape_of(tokens, channels)
     low_rows = shape_of(tokens, channels, dtype=bf16)
     wide = shape_of(tokens, states, 128)
-    slots = pltpu.VMEM((len(bits), states + 8, channels), f32)
     raws = pltpu.VMEM((2, tokens, narrow), f32)
     out = pl.pallas_call(
         functools.partial(forward_kernel, bits),
@@ -331,14 +348,15 @@
         scratch_shapes=[
             pltpu.VMEM((tokens + 16, channels), f32), raws, raws,
             pltpu.VMEM((tokens, channels), f32), pltpu.VMEM((tokens, channels), f32),
-            pltpu.VMEM((states, channels), f32), slots, slots,
+            pltpu.VMEM((states, channels), f32),
             pltpu.VMEM((2, 2, quarter, width), bf16), pltpu.VMEM((2, quarter, width), bf16),
             pltpu.VMEM((quarter, width), bf16), pltpu.VMEM((quarter, width), bf16),
             pltpu.VMEM((tokens, states, channels), f32),
-            pltpu.SemaphoreType.DMA((7 + len(bits),)), pltpu.SemaphoreType.DMA((7 + len(bits),)),
+            pltpu.SemaphoreType.DMA((3,)), pltpu.SemaphoreType.DMA((3,)),
             pltpu.SemaphoreType.DMA((channels // LANES,)),
             pltpu.SemaphoreType.DMA((4,)), pltpu.SemaphoreType.DMA((4,)),
             pltpu.SemaphoreType.DMA((8,)), pltpu.SemaphoreType.DMA((8,)),
+            *handing(count, states, channels).values(),
         ],
         compiler_params=pltpu.CompilerParams(
             collective_id=ident, has_side_effects=True, vmem_limit_bytes=56 * 2**20
@@ -783,7 +801,7 @@
     high, along = flipped(ch_me, 2)
     pair_bit, rest_bits = bits[1], [bits[0], *bits[2:]]
     mine, pair = flipped(me, pair_bit)
-    following, previous = lax.rem(me + 1, seq_count), lax.rem(me + seq_count - 1, seq_count)
+    previous = lax.rem(me + seq_count - 1, seq_count)
     load_slots, pair_slots, shared_slots, write_slots = ([] for _ in range(4))
 
     def slot_of(slots):
@@ -820,8 +838,8 @@
     hists = [load(r.hist_in.at[:, :, blocks[k]], r.hist.at[k]) for k in range(2)]
 
     greeted(
-        [("ch", across), ("ch", along), ("seq", following), ("seq", previous)]
-        + [("seq", flipped(me, bit)[1]) for bit in bits]
+        [("ch", across), ("ch", along)]
+        + [("seq", lax.rem(me + k, seq_count)) for k in range(1, seq_count)]
     )
 
     def swap(source, target):
@@ -969,42 +987,16 @@
             0, tokens // UNROLL, ended, jnp.zeros((states, LANES), f32)
         )
 
-    def handed():
-        all_state, all_steps = r.starts[...], r.step_sum[...]
-        mine_state, mine_steps = jnp.zeros_like(all_state), jnp.zeros_like(all_steps)
-        for k, bit in enumerate(bits):
-            side, partner = flipped(me, bit)
-            r.chain_move[k, :states] = all_state
-            r.chain_move[k, states:] = all_steps
-            copy = sent(r.chain_move.at[k], r.chain_land.at[k], r.chain_sends, r.chain_receives,
-                        k, "seq", partner)
-            yield
-            copy.wait()
-            other_state, other_steps = r.chain_land[k, :states], r.chain_land[k, states:]
-            earlier = side == 0
-            through = jnp.exp2(rates * mine_steps[:1])
-            mine_state = jnp.where(earlier, mine_state + through * other_state, mine_state)
-            mine_steps = jnp.where(earlier, mine_steps + other_steps, mine_steps)
-            after = jnp.exp2(rates * all_steps[:1]) * other_state + all_state
-            ahead_of = jnp.exp2(rates * other_steps[:1]) * all_state + other_state
-            all_state = jnp.where(earlier, after, ahead_of)
-            all_steps = all_steps + other_steps
-        r.starts[...] = mine_state
-        yield
-
-    chain = handed()
+    chain = handed_on(False, r.starts[...], r.step_sum[0:1], rates, r)
     next(chain)
     gate0.made(two_own, gate_up_own, gate_other)
-    next(chain)
+    gate1.made()
+    r.starts[...] = next(chain)
     gate0.go()
-    gate1.made()
-    next(chain)
     late_kept.wait()
     late.next()
     gate1.go()
     up0.made(up_other)
-    for _ in chain:
-        pass
     first = pl.multiple_of(low * (tokens // 2), tokens // 2)
     mixer_other = swap_shared(
         r.right_out.at[pl.ds(first, tokens // 2)],
@@ -1251,10 +1243,6 @@
             target[...] = total.reshape(target.shape)
         yield
 
-    small_columns()
-    small_sum = small_summed()
-    next(small_sum)
-
     one_sums = [summed(r.part, 8, k) for k in range(2)]
     for number in range(width // channels):
         weights.wait()
@@ -1299,17 +1287,19 @@
     flat_sum = flat_summed()
     next(flat_sum)
 
-    out.next()
-    next(one_sum)
-    next(flat_sum)
     cins[0].made(cin_others[0]).go()
     next(one_sum)
     next(flat_sum)
+    out.next()
     cins[1].made(cin_others[1]).go()
     next(one_sum)
     next(flat_sum)
+    small_columns()
+    small_sum = small_summed()
     next(small_sum)
+    next(one_sum)
     gin.next()
+    next(flat_sum)
     next(one_sum)
 
     def norm_one(index, _):
@@ -1322,13 +1312,14 @@
         return 0
 
     lax.fori_loop(0, chunks, norm_one, 0)
+    cins[0].next()
+    next(small_sum)
+    next(flat_sum)
+    cins[1].next()
     down_kept.wait()
     for item in (down, late, *quarters):
         item.next()
-    cins[0].next()
-    next(flat_sum)
     next(small_sum)
-    cins[1].next()
     for waiting in (flat_sum, small_sum):
         for _ in waiting:
             pass
@@ -1403,8 +1394,7 @@
         starts=full(states, channels),
         rate_sum=full(states, channels),
         step_low_grad=low(tokens, channels),
-        chain_move=full(len(bits), states + 8, channels),
-        chain_land=full(len(bits), states + 8, channels),
+        **handing(count, states, channels),
         part=low(2, 2, quarter, width),
         total=low(2, 2, quarter, width),
         first_land=low(2, quarter, width),
@@ -1441,8 +1431,6 @@
         unit_receives=sems(10 * n_bits),
         sum_sends=sems(16),
         sum_receives=sems(16),
-        chain_sends=sems(len(bits)),
-        chain_receives=sems(len(bits)),
         raw_sends=sems(3),
         raw_receives=sems(3),
         last_sends=sems(len(bits)),

time: 255 us -> 246 us (0.965)
  Pallas kernels: 226 us -> 217 us
    pallas_call x1, Pallas kernels: 137 us -> 132 us  [backward(): pl.pallas_call(functools.partial(backward_kernel, bits, names), out_shape...]
    pallas_call x1, Pallas kernels: 58.6 us -> 53.9 us  [mixer_forward(): pl.pallas_call(functools.partial(forward_kernel, bits), out_shape=[shape_...]
where the time goes in v4:
time: 246 us
  Pallas kernels  217 us (88%)
  local copies, waits for them, and re-layouts  23.1 us (9%)
  other arithmetic  2.69 us (1%)
    pallas_call x1, Pallas kernels, backward(): pl.pallas_call(functools.partial(backward_kernel, bits, names), out_shape...  132 us
    pallas_call x1, Pallas kernels, mixer_forward(): pl.pallas_call(functools.partial(forward_kernel, bits), out_shape=[shape_...  53.9 us
    pallas_call x1, Pallas kernels, feed_forward(): pl.pallas_call(functools.partial(feed_forward_kernel, bits, names), out_s...  31.3 us
    unnamed x39, local copies, waits for them, and re-layouts  19 us

profile of v4, /device:TPU:0, one launch (start us, length us, event | category | flops | bytes accessed | tf_op | source)
XLA Modules:
  0.0 246.2 jit_solution(3788212059879322416)
XLA Ops:
  0.7 3.3 %copy.33 = bf16[192,8,2,768]{3,1,2,0:T(8,128)(2,1)S(1)} copy(bf16[192,8,2,768]{3,2,1,0:T(2,128)(2,1)} %bitcast.26) | data formatting | bytes 9437184
  4.3 2.4 convolution_convert_fusion.proj.refs_4_
  6.7 0.2 fusion.3
  6.9 1.2 copy.26
  8.1 53.9 %mixer_forward.1 = (bf16[16,768]{1,0:T(8,128)(2,1)}, f32[256,768]{1,0:T(8,128)}, bf16[256,768]{1,0:T(8,128)(2,1)}, f32[256,128]{1,0:T(8,128)}, f32[256,768]{1,0:...) custom-call(s32[2]{0:T(128)} %refs_0_.3, ...), custom_call_target="tpu_custom_call" | custom-call | flops 6000000000 | bytes 6000000 | tf_op jit(solution)/shard_map/mixer_forward/pallas_call | solution.py:337
  62.0 5.2 %copy.34 = bf16[192,8,2,1024]{3,1,2,0:T(8,128)(2,1)} copy(bf16[192,8,2,1024]{3,2,1,0:T(2,128)(2,1)S(1)} %bitcast.25) | data formatting | bytes 12582912
  67.2 31.3 %feed_forward.1 = (bf16[2,2,64,1536]{3,2,1,0:T(8,128)(2,1)}, bf16[2,2,64,1536]{3,2,1,0:T(8,128)(2,1)}, bf16[2,2,192,512]{3,2,1,0:T(8,128)(2,1)}, bf16[512,2048]{...) custom-call(bf16[256,1536]{1,0:T(8,128)(2,1)} %refs_1_.1, ...), custom_call_target="tpu_custom_call" | custom-call | tf_op jit(solution)/shard_map/feed_forward/pallas_call | solution.py:779
  98.6 0.9 copy.27
  99.5 132.0 %block_backward.1 = (f32[256,1536]{1,0:T(8,128)}, bf16[256,1536]{1,0:T(8,128)(2,1)}, f32[96,256]{1,0:T(8,128)}, f32[8,1536]{1,0:T(8,128)}, f32[128,1536]{1,0:T(8...) custom-call(s32[2]{0:T(128)} %refs_0_.3, ...), custom_call_target="tpu_custom_call" | custom-call | tf_op jit(solution)/shard_map/block_backward/pallas_call | solution.py:1448
  231.6 1.5 pad_maximum_fusion
  233.1 2.4 copy.32
  235.5 1.9 copy.28
  237.5 0.6 fusion.5
  238.2 0.7 copy.30
  238.9 0.7 copy.29
  239.6 0.7 copy.31
  240.3 0.7 constant_dynamic-slice_fusion
  241.0 0.6 dynamic-slice_bitcast_fusion
  241.7 0.5 multiply_sqrt_fusion
  242.2 0.9 copy.39
  243.1 1.1 copy.40
  244.2 0.3 copy-done.5
  244.5 0.8 copy.41
  245.4 0.9 copy.42
  (37 shorter events, 0.7 us)
Async XLA Ops:
  0.6 3.4 %copy-start.10 = (f32[2,1536]{1,0:T(2,128)S(1)}, f32[2,1536]{1,0:T(2,128)}, u32[]{:S(2)}) copy-start(f32[2,1536]{1,0:T(2,128)} %refs_2_.3) | copy-start | bytes 36868
  0.7 3.4 %copy-start.1 = (bf16[256,1536]{1,0:T(8,128)(2,1)S(1)}, bf16[256,1536]{1,0:T(8,128)(2,1)}, u32[]{:S(2)}) copy-start(bf16[256,1536]{1,0:T(8,128)(2,1)} %refs_1_.1) | copy-start | bytes 2359300
  4.0 2.7 %copy-start = (bf16[192,8,2,768]{3,1,2,0:T(8,128)(2,1)}, bf16[192,8,2,768]{3,1,2,0:T(8,128)(2,1)S(1)}, u32[]{:S(2)}) copy-start(bf16[192,8,2,768]{3,1,2,0:T(8,128)(2,1)S(1)} %copy.33) | copy-start | bytes 14155780
  8.1 53.9 %slice-start = ((s8[6291456]{0:T(1024)(128)(4,1)}), s8[4194304]{0:T(1024)(128)(4,1)S(1)}, s32[]{:S(2)}) async-start(s8[6291456]{0:T(1024)(128)(4,1)} %bitcast.23), calls=%async_computation | async-start | bytes 8388608
  8.1 53.9 %slice-start.1 = ((s8[6291456]{0:T(1024)(128)(4,1)}), s8[2097152]{0:T(1024)(128)(4,1)S(1)}, s32[]{:S(2)}) async-start(s8[6291456]{0:T(1024)(128)(4,1)} %bitcast.23), calls=%async_computation.1 | async-start | bytes 4194304
  67.2 31.4 %copy-start.8 = (bf16[256,768]{1,0:T(8,128)(2,1)S(1)}, bf16[256,768]{1,0:T(8,128)(2,1)}, u32[]{:S(2)}) copy-start(bf16[256,768]{1,0:T(8,128)(2,1)} %get-tuple-element.61) | copy-start | bytes 1179652
  233.0 2.4 copy-start.6
  233.1 2.4 copy-start.7
  235.5 2.0 copy-start.9
  235.5 4.8 %copy-start.11 = (f32[8,1536]{1,0:T(8,128)S(1)}, f32[8,1536]{1,0:T(8,128)}, u32[]{:S(2)}) copy-start(f32[8,1536]{1,0:T(8,128)} %get-tuple-element.69) | copy-start | bytes 147460
  235.5 6.7 %copy-start.4 = (bf16[256,1536]{1,0:T(8,128)(2,1)S(1)}, bf16[256,1536]{1,0:T(8,128)(2,1)}, u32[]{:S(2)}) copy-start(bf16[256,1536]{1,0:T(8,128)(2,1)} %get-tuple-element.105) | copy-start | bytes 2359300
  237.5 5.6 %copy-start.2 = (f32[256,1536]{1,0:T(8,128)S(1)}, f32[256,1536]{1,0:T(8,128)}, u32[]{:S(2)}) copy-start(f32[256,1536]{1,0:T(8,128)} %get-tuple-element.106) | copy-start | bytes 4718596
  243.1 1.4 copy-start.5
  243.1 2.3 copy-start.3

commit v5 on v4

--- a/solution.py
+++ b/solution.py
@@ -152,17 +152,32 @@
     )
 
 
+def turn(values, first, turned):
+    rows = turned.shape[3]
+    across_rows = values.T
+    for k in range(values.shape[1] // rows):
+        owner = first // rows + k
+        turned[owner // 4, (owner // 2) % 2, owner % 2] = across_rows[k * rows : (k + 1) * rows]
+
+
 def forward_kernel(
-    bits, bounds, proj, chan, logs, w_x, gains, w_dt, w_out, one_in, cot,
-    halo, pre_out, low_out, raw_out, step_pre_out, into, out_of, scan_out, gated_out, last_state,
+    bits, bounds, stream, norm_gains, chan, logs, w_x, gains, w_dt, w_out, w_in, cot,
+    proj, one_in, halo, pre_out, low_out, raw_out, step_pre_out, into, out_of, scan_out, gated_out, last_state,
     mixer, hist_out, one_came, cot_came,
     extended, raw_move, raw_land, step, drive, starts, part, first_land,
     second_move, second_land, hist, sends, receives, hist_sem, shared_sends, shared_receives,
-    sum_sends, sum_receives, *handed,
+    sum_sends, sum_receives, weights, normed, weight_sem, *handed,
 ):
     tokens, channels = low_out.shape
     rank, states = w_dt.shape[0], logs.shape[0]
     chunks = tokens // CHUNK
+    width = stream.shape[1]
+    loads = []
+    for k in range(width // 512):
+        cols = pl.ds(k * 512, 512)
+        copy = pltpu.make_async_copy(w_in.at[:, cols], weights.at[:, cols], weight_sem.at[k])
+        copy.start()
+        loads.append(copy)
     ch_me, me = lax.axis_index("ch"), lax.axis_index("seq")
     seq_count = 1 << len(bits)
     low, across = flipped(ch_me, 1)
@@ -172,10 +187,31 @@
         [("ch", across), ("ch", along)]
         + [("seq", lax.rem(me + k, seq_count)) for k in range(1, seq_count)]
     )
+    def norm_one(index, _):
+        rows = pl.ds(pl.multiple_of(index * CHUNK, CHUNK), CHUNK)
+        value = stream[rows].astype(f32)
+        scale = lax.rsqrt(mean_square(value) + 1e-06)
+        normed[rows] = (value * scale * norm_gains[0:1]).astype(bf16)
+        return 0
+
+    lax.fori_loop(0, chunks, norm_one, 0)
+
+    def project(index, _):
+        cols = pl.ds(pl.multiple_of(index * 256, 256), 256)
+        proj[:, cols] = jnp.dot(
+            normed[...], weights[:, cols], preferred_element_type=f32
+        ).astype(bf16)
+        return 0
+
+    for copy in loads:
+        copy.wait()
+    lax.fori_loop(0, channels // 256, project, 0)
     halo_copy = sent(
         proj.at[pl.ds(tokens - 16, 16), pl.ds(0, channels)], halo, sends, receives, 0, "seq",
         following,
     )
+    for at in range(0, width, 384):
+        turn(normed[:, at : at + 384], at, one_in)
     mine, pair = flipped(me, bits[1])
     half = one_in.shape[0] // 2
     some = pl.ds(low * half, half)
@@ -188,6 +224,7 @@
         sent(source, target, shared_sends, shared_receives, k, "seq", pair)
         for k, (source, target) in enumerate(shared)
     ]
+    lax.fori_loop(channels // 256, 2 * channels // 256, project, 0)
     rates = -jnp.exp(logs[...]) * LOG2E
 
     def spread(index, _):
@@ -295,7 +332,6 @@
 
     lax.fori_loop(0, chunks, gate, 0)
     quarter = tokens // 4
-    width = w_out.shape[1]
     for k, (_, target) in enumerate(shared):
         shared_copies[k].wait()
         shared_copies[k] = sent(
@@ -325,9 +361,11 @@
         copy.wait()
 
 
-def mixer_forward(bounds, proj, chan, logs, w_x, gains, w_dt, w_out, one_in, cot, count, ident):
+def mixer_forward(
+    bounds, stream, norm_gains, chan, logs, w_x, gains, w_dt, w_out, w_in, cot, count, ident
+):
     bits = bits_of(count)
-    tokens, channels = proj.shape[0], proj.shape[1] // 2
+    tokens, channels = stream.shape[0], w_out.shape[0]
     states, rank, width = logs.shape[0], w_dt.shape[0], w_out.shape[1]
     quarter, narrow = tokens // 4, w_x.shape[1]
     rows = shape_of(tokens, channels)
@@ -337,14 +375,16 @@
     out = pl.pallas_call(
         functools.partial(forward_kernel, bits),
         out_shape=[
+            shape_of(tokens, 2 * channels, dtype=bf16),
+            shape_of(count // 4, 2, 2, width // count, tokens, dtype=bf16),
             shape_of(16, channels, dtype=bf16), rows, low_rows, shape_of(tokens, narrow), rows,
             wide, wide, rows, low_rows, shape_of(states, channels),
             shape_of(2, 2, quarter, width, dtype=bf16), shape_of(tokens, states, channels),
-            shape_of(one_in.shape[0], *one_in.shape[2:], dtype=bf16),
+            shape_of(count // 4, 2, width // count, tokens, dtype=bf16),
             shape_of(tokens, width, dtype=bf16),
         ],
-        in_specs=[pl.BlockSpec(memory_space=pltpu.SMEM)] + [VMEM] * 7 + [ANY] * 2,
-        out_specs=[VMEM] * 11 + [ANY] * 3,
+        in_specs=[pl.BlockSpec(memory_space=pltpu.SMEM)] + [VMEM] * 8 + [ANY] * 2,
+        out_specs=[VMEM] * 13 + [ANY] * 3,
         scratch_shapes=[
             pltpu.VMEM((tokens + 16, channels), f32), raws, raws,
             pltpu.VMEM((tokens, channels), f32), pltpu.VMEM((tokens, channels), f32),
@@ -356,6 +396,8 @@
             pltpu.SemaphoreType.DMA((channels // LANES,)),
             pltpu.SemaphoreType.DMA((4,)), pltpu.SemaphoreType.DMA((4,)),
             pltpu.SemaphoreType.DMA((8,)), pltpu.SemaphoreType.DMA((8,)),
+            pltpu.VMEM(w_in.shape, bf16), pltpu.VMEM((tokens, width), bf16),
+            pltpu.SemaphoreType.DMA((width // 512,)),
             *handing(count, states, channels).values(),
         ],
         compiler_params=pltpu.CompilerParams(
@@ -363,7 +405,7 @@
         ),
         cost_estimate=cost(6),
         name="mixer_forward",
-    )(bounds, proj, chan, logs, w_x, gains, w_dt, w_out, one_in, cot)
+    )(bounds, stream, norm_gains, chan, logs, w_x, gains, w_dt, w_out, w_in, cot)
     return out
 
 
@@ -615,15 +657,6 @@
         return 0
 
     lax.fori_loop(0, chunks, norm_two, 0)
-
-    def turn(values, first, turned):
-        rows = turned.shape[3]
-        across_rows = values.T
-        for k in range(values.shape[1] // rows):
-            owner = first // rows + k
-            turned[owner // 4, (owner // 2) % 2, owner % 2] = across_rows[
-                k * rows : (k + 1) * rows
-            ]
 
     group = 384
     for at in range(0, width, group):
@@ -1459,8 +1492,99 @@
     return types.SimpleNamespace(**dict(zip(outs, made)))
 
 
-def rms_gain(values, gain_row):
-    return values * lax.rsqrt(jnp.mean(values * values, axis=-1, keepdims=True) + 1e-06) * gain_row
+def finish_kernel(cells, names, *refs):
+    r = named(names, refs)
+    me = lax.axis_index("seq")
+    moves = [
+        (r.out_rows, r.out), (r.stream_grad, r.stream), (r.out_out, r.w_out),
+        (r.down_out, r.w_down), (r.gate_out, r.w_gate_up.at[:, 0]),
+        (r.up_out, r.w_gate_up.at[:, 1]), (r.cin_out, r.w_in.at[:, 0]),
+        (r.gin_out, r.w_in.at[:, 1]),
+    ]
+    little = [(r.small_out, r.small_here), (r.flat_out, r.flat_here)]
+    loads = [
+        pltpu.make_async_copy(source, here, r.sems.at[k])
+        for k, (source, here) in enumerate(
+            [*little, *((source, here) for (source, _), here in zip(moves, r.here))]
+        )
+    ]
+    for copy in loads:
+        copy.start()
+    copies = []
+    for k, (_, target) in enumerate(moves):
+        loads[k + 2].wait()
+        copy = pltpu.make_async_copy(r.here[k], target, r.out_sems.at[k])
+        copy.start()
+        copies.append(copy)
+    for copy in loads[:2]:
+        copy.wait()
+    narrow, rank, states = r.x.shape[1], r.dt.shape[0], r.decay.shape[0]
+    small = r.small_here[...]
+    r.x[...] = small[:, :narrow]
+    turned = small[:, narrow:].T
+    r.dt[...] = turned[:rank]
+    r.decay[...] = turned[rank : rank + states]
+    r.chan[...] = turned[rank + states : rank + states + 7]
+    flat = r.flat_here[...]
+    width = flat.shape[1]
+    count = width // r.gains.shape[1]
+    gains, tail = jnp.zeros(r.gains.shape, f32), jnp.zeros(r.small.shape, f32)
+    for k in range(count):
+        gain_at, tail_at = k * r.gains.shape[1], k * r.small.shape[1]
+        mine = me == k
+        gains = gains + jnp.where(mine, flat[0:2, gain_at : gain_at + r.gains.shape[1]], 0.0)
+        tail = tail + jnp.where(mine, flat[2:3, tail_at : tail_at + r.small.shape[1]], 0.0)
+    r.gains[...] = gains
+    r.small[...] = tail
+    r.rms[...] = jnp.sqrt(jnp.sum(flat[3:6], axis=1, keepdims=True) / cells)
+    for copy in copies:
+        copy.wait()
+
+
+def finish(made, cells, narrow, rank, states, count):
+    rows_out = made.small_out.shape[0]
+    width = made.flat_out.shape[1]
+    rows_in, hid = made.gate_out.shape
+    channels = made.cin_out.shape[1]
+    outs = dict(
+        out=shape_of(*made.out_rows.shape, dtype=bf16),
+        stream=shape_of(*made.stream_grad.shape),
+        gains=shape_of(2, width // count),
+        w_in=shape_of(rows_in, 2, channels),
+        chan=shape_of(7, rows_out),
+        decay=shape_of(states, rows_out),
+        x=shape_of(rows_out, narrow),
+        small=shape_of(1, narrow // count),
+        dt=shape_of(rank, rows_out),
+        w_out=shape_of(*made.out_out.shape),
+        w_gate_up=shape_of(rows_in, 2, hid),
+        w_down=shape_of(*made.down_out.shape),
+        rms=shape_of(3, 1),
+    )
+    ins = vars(made)
+    held = [
+        made.out_rows, made.stream_grad, made.out_out, made.down_out, made.gate_out, made.up_out,
+        made.cin_out, made.gin_out, made.small_out, made.flat_out,
+    ]
+    places = [pltpu.VMEM(item.shape, item.dtype) for item in held]
+    names = [(name, 0) for name in [*ins, *outs]]
+    rest = dict(here=8, small_here=0, flat_here=0, sems=0, out_sems=0)
+    names += list(rest.items())
+    big = {id(outs[name]) for name in ("out", "stream", "w_in", "w_out", "w_gate_up", "w_down")}
+    done = pl.pallas_call(
+        functools.partial(finish_kernel, cells, names),
+        out_shape=list(outs.values()),
+        in_specs=[ANY for _ in ins],
+        out_specs=[ANY if id(item) in big else VMEM for item in outs.values()],
+        scratch_shapes=[*places, pltpu.SemaphoreType.DMA((10,)), pltpu.SemaphoreType.DMA((8,))],
+        compiler_params=pltpu.CompilerParams(vmem_limit_bytes=62 * 2**20),
+        name="finish",
+    )(*ins.values())
+    out, stream, gains, w_in, chan, decay, x, small, dt, w_out, w_gate_up, w_down, rms = done
+    return (
+        out, stream, gains, w_in, chan, decay, x, small.reshape(-1), dt, w_out, w_gate_up, w_down,
+        rms.reshape(-1),
+    )
 
 
 def local(
@@ -1485,17 +1609,13 @@
     def turned(values):
         return values.T.reshape(seq_count // 4, 2, 2, values.shape[1] // seq_count, tokens)
 
-    stream_in = stream.astype(f32)
-    normed_low = rms_gain(stream_in, norm_gains[0]).astype(bf16)
     w_in_flat = w_in.reshape(width, 2 * channels)
-    in_proj = jnp.dot(normed_low, w_in_flat, preferred_element_type=f32).astype(bf16)
-    one_in = turned(normed_low)
     (
-        halo, pre_conv, conv_low, raw_proj, step_pre, into, out_of, scan_out, gated_low,
+        in_proj, one_in, halo, pre_conv, conv_low, raw_proj, step_pre, into, out_of, scan_out, gated_low,
         last_state, mixer_low, before, one_came, cot_came,
     ) = mixer_forward(
-        doc_bounds, in_proj, chan_vectors, decay_logs, w_x, small_gains[None], w_dt, w_out,
-        one_in, cotangent, seq_count, 1,
+        doc_bounds, stream, norm_gains, chan_vectors, decay_logs, w_x, small_gains[None], w_dt,
+        w_out, w_in_flat, cotangent, seq_count, 1,
     )
     mid = feed_forward(
         dict(stream=stream, mixer=mixer_low, gains=norm_gains),
@@ -1524,31 +1644,8 @@
         seq_count,
         2,
     )
-    small, flat = made.small_out, made.flat_out
-    at = w_x.shape[1]
-    x_part, small = small[:, :at], small[:, at:].T
-    dt_part, decay_out = small[:rank], small[rank : rank + states]
-    chan_part = small[rank + states : rank + states + 7]
-    me = lax.axis_index("seq")
-    gain_width = width // seq_count
-    gains_part = lax.dynamic_slice_in_dim(flat[:2], me * gain_width, gain_width, 1)
-    small_width = small_gains.shape[0] // seq_count
-    small_part = lax.dynamic_slice_in_dim(flat[2], me * small_width, small_width, 0)
-    rms_values = jnp.sqrt(jnp.sum(flat[3:6], axis=1) / (tokens * seq_count * width))
-    return (
-        made.out_rows,
-        made.stream_grad,
-        gains_part,
-        jnp.stack([made.cin_out, made.gin_out], 1),
-        chan_part,
-        decay_out,
-        x_part,
-        small_part,
-        dt_part,
-        made.out_out,
-        jnp.stack([made.gate_out, made.up_out], 1),
-        made.down_out,
-        rms_values,
+    return finish(
+        made, tokens * seq_count * width, w_x.shape[1], rank, states, seq_count
     )
 
 

time: 246 us -> 240 us (0.976)
  local copies, waits for them, and re-layouts: 23.1 us -> 11.7 us
  Pallas kernels: 217 us -> 226 us
    unnamed x39 -> x6, local copies, waits for them, and re-layouts: 19 us -> 10.8 us
    pallas_call x0 -> x1, Pallas kernels: none -> 6.18 us  [finish(): pl.pallas_call(functools.partial(finish_kernel, cells, names), out_shape=...]
    pallas_call x1, Pallas kernels: 53.9 us -> 56.4 us  [mixer_forward(): pl.pallas_call(functools.partial(forward_kernel, bits), out_shape=[shape_...]
where the time goes in v5:
time: 240 us
  Pallas kernels  226 us (94%)
  local copies, waits for them, and re-layouts  11.7 us (5%)
    pallas_call x1, Pallas kernels, backward(): pl.pallas_call(functools.partial(backward_kernel, bits, names), out_shape...  132 us
    pallas_call x1, Pallas kernels, mixer_forward(): pl.pallas_call(functools.partial(forward_kernel, bits), out_shape=[shape_...  56.4 us
    pallas_call x1, Pallas kernels, feed_forward(): pl.pallas_call(functools.partial(feed_forward_kernel, bits, names), out_s...  31.3 us
    unnamed x6, local copies, waits for them, and re-layouts  10.8 us
    pallas_call x1, Pallas kernels, finish(): pl.pallas_call(functools.partial(finish_kernel, cells, names), out_shape=...  6.18 us

profile of v5, /device:TPU:0, one launch (start us, length us, event | category | flops | bytes accessed | tf_op | source)
XLA Modules:
  0.0 239.7 jit_solution(5056054369052791481)
XLA Ops:
  0.6 0.0 copy-start
  0.7 5.6 %copy.28 = bf16[192,8,2,768]{3,1,2,0:T(8,128)(2,1)} copy(bf16[192,8,2,768]{3,2,1,0:T(2,128)(2,1)} %bitcast.12) | data formatting | bytes 9437184
  6.2 0.0 copy-done
  6.2 5.2 %copy.29 = bf16[192,8,2,1024]{3,1,2,0:T(8,128)(2,1)} copy(bf16[192,8,2,1024]{3,2,1,0:T(2,128)(2,1)S(1)} %bitcast.11) | data formatting | bytes 12582912
  11.4 56.4 %mixer_forward.1 = (bf16[256,1536]{1,0:T(8,128)(2,1)}, bf16[2,2,2,192,256]{4,3,2,1,0:T(8,128)(2,1)}, bf16[16,768]{1,0:T(8,128)(2,1)}, f32[256,768]{1,0:T(8,128)}...) custom-call(s32[2]{0:T(128)} %refs_0_.3, ...), custom_call_target="tpu_custom_call" | custom-call | flops 6000000000 | bytes 6000000 | tf_op jit(solution)/shard_map/mixer_forward/pallas_call | solution.py:375
  67.8 0.0 copy-start.1
  67.8 31.3 %feed_forward.1 = (bf16[2,2,64,1536]{3,2,1,0:T(8,128)(2,1)}, bf16[2,2,64,1536]{3,2,1,0:T(8,128)(2,1)}, bf16[2,2,192,512]{3,2,1,0:T(8,128)(2,1)}, bf16[512,2048]{...) custom-call(bf16[256,1536]{1,0:T(8,128)(2,1)} %refs_1_.1, ...), custom_call_target="tpu_custom_call" | custom-call | tf_op jit(solution)/shard_map/feed_forward/pallas_call | solution.py:812
  99.2 0.0 copy-done.1
  99.2 0.9 copy.27
  100.1 132.1 %block_backward.1 = (f32[256,1536]{1,0:T(8,128)}, bf16[256,1536]{1,0:T(8,128)(2,1)}, f32[96,256]{1,0:T(8,128)}, f32[8,1536]{1,0:T(8,128)}, f32[128,1536]{1,0:T(8...) custom-call(s32[2]{0:T(128)} %refs_0_.3, ...), custom_call_target="tpu_custom_call" | custom-call | tf_op jit(solution)/shard_map/block_backward/pallas_call | solution.py:1481
  232.3 6.2 %finish.1 = (bf16[256,1536]{1,0:T(8,128)(2,1)}, f32[256,1536]{1,0:T(8,128)}, f32[2,192]{1,0:T(2,128)}, f32[192,2,768]{2,1,0:T(2,128)}, f32[7,96]{1,0:T(8,128)}, ...) custom-call(f32[256,1536]{1,0:T(8,128)} %get-tuple-element.84.refs_0, ...), custom_call_target="tpu_custom_call" | custom-call | tf_op jit(solution)/shard_map/finish/pallas_call | solution.py:1574
  238.4 1.3 reduce
Async XLA Ops:
  0.6 5.6 %copy-start = (bf16[1536,2,1024]{2,1,0:T(2,128)(2,1)S(1)}, bf16[1536,2,1024]{2,1,0:T(2,128)(2,1)}, u32[]{:S(2)}) copy-start(bf16[1536,2,1024]{2,1,0:T(2,128)(2,1)} %param.23) | copy-start | bytes 18874372
  67.8 31.4 %copy-start.1 = (bf16[256,768]{1,0:T(8,128)(2,1)S(1)}, bf16[256,768]{1,0:T(8,128)(2,1)}, u32[]{:S(2)}) copy-start(bf16[256,768]{1,0:T(8,128)(2,1)} %get-tuple-element.77) | copy-start | bytes 1179652

commit v6 on v5

--- a/solution.py
+++ b/solution.py
@@ -161,12 +161,12 @@
 
 
 def forward_kernel(
-    bits, bounds, stream, norm_gains, chan, logs, w_x, gains, w_dt, w_out, w_in, cot,
+    bits, bounds, stream, norm_gains, chan, logs, w_x, gains, w_dt, w_out, w_in, cot, w_pairs,
     proj, one_in, halo, pre_out, low_out, raw_out, step_pre_out, into, out_of, scan_out, gated_out, last_state,
-    mixer, hist_out, one_came, cot_came,
+    mixer, hist_out, one_came, cot_came, w_flat,
     extended, raw_move, raw_land, step, drive, starts, part, first_land,
     second_move, second_land, hist, sends, receives, hist_sem, shared_sends, shared_receives,
-    sum_sends, sum_receives, weights, normed, weight_sem, *handed,
+    sum_sends, sum_receives, weights, normed, weight_sem, pairs, flat, pair_sems, *handed,
 ):
     tokens, channels = low_out.shape
     rank, states = w_dt.shape[0], logs.shape[0]
@@ -178,6 +178,31 @@
         copy = pltpu.make_async_copy(w_in.at[:, cols], weights.at[:, cols], weight_sem.at[k])
         copy.start()
         loads.append(copy)
+    pair_copies = [pltpu.make_async_copy(w_pairs, pairs, pair_sems.at[0])]
+    pair_copies[0].start()
+    ahead = [0]
+
+    def relay(count):
+        first = ahead[0]
+        ahead[0] = last = min(first + count, width // CHUNK)
+        if first == 0:
+            pair_copies.pop().wait()
+        hid = pairs.shape[2]
+
+        def laid(index, _):
+            rows = pl.ds(pl.multiple_of(index * CHUNK, CHUNK), CHUNK)
+            flat[rows, 0:hid] = pairs[rows, 0, :]
+            flat[rows, hid:] = pairs[rows, 1, :]
+            return 0
+
+        lax.fori_loop(first, last, laid, 0)
+        rows = pl.ds(first * CHUNK, (last - first) * CHUNK)
+        copy = pltpu.make_async_copy(
+            flat.at[rows], w_flat.at[rows], pair_sems.at[1 + len(pair_copies)]
+        )
+        copy.start()
+        pair_copies.append(copy)
+
     ch_me, me = lax.axis_index("ch"), lax.axis_index("seq")
     seq_count = 1 << len(bits)
     low, across = flipped(ch_me, 1)
@@ -251,9 +276,13 @@
     extended[0:16] = halo[...].astype(f32)
     convolved(0, 0)
     raw_move[0] = jnp.dot(low_out[...], w_x[...], preferred_element_type=f32)
-    sent(raw_move.at[0], raw_land.at[0], sends, receives, 1, "ch", across).wait()
+    copy = sent(raw_move.at[0], raw_land.at[0], sends, receives, 1, "ch", across)
+    relay(4)
+    copy.wait()
     raw_move[1] = raw_move[0] + raw_land[0]
-    sent(raw_move.at[1], raw_land.at[1], sends, receives, 2, "ch", along).wait()
+    copy = sent(raw_move.at[1], raw_land.at[1], sends, receives, 2, "ch", along)
+    relay(9)
+    copy.wait()
 
     def stepped(index, total):
         first = pl.multiple_of(index * CHUNK, CHUNK)
@@ -294,6 +323,7 @@
     hand = types.SimpleNamespace(**dict(zip(handing(2, 8, 128), handed)))
     handed_in = handed_on(True, starts[...], total, rates, hand)
     next(handed_in)
+    relay(14)
     starts[...] = next(handed_in)
     hist_copies = []
     for number, lanes in enumerate(blocks):
@@ -355,14 +385,19 @@
     for k, item in enumerate(sums):
         lax.fori_loop(k * width // 512, (k + 1) * width // 512, mixed, 0)
         next(item)
-    for _ in in_turn(*sums):
-        pass
-    for copy in hist_copies + shared_copies:
+    turns = in_turn(*sums)
+    for count in (3, 8, 8, width):
+        next(turns)
+        if ahead[0] < width // CHUNK:
+            relay(count)
+    next(turns)
+    for copy in hist_copies + shared_copies + pair_copies:
         copy.wait()
 
 
 def mixer_forward(
-    bounds, stream, norm_gains, chan, logs, w_x, gains, w_dt, w_out, w_in, cot, count, ident
+    bounds, stream, norm_gains, chan, logs, w_x, gains, w_dt, w_out, w_in, cot, w_pairs, count,
+    ident,
 ):
     bits = bits_of(count)
     tokens, channels = stream.shape[0], w_out.shape[0]
@@ -382,9 +417,10 @@
             shape_of(2, 2, quarter, width, dtype=bf16), shape_of(tokens, states, channels),
             shape_of(count // 4, 2, width // count, tokens, dtype=bf16),
             shape_of(tokens, width, dtype=bf16),
+            shape_of(width, 2 * w_pairs.shape[2], dtype=bf16),
         ],
-        in_specs=[pl.BlockSpec(memory_space=pltpu.SMEM)] + [VMEM] * 8 + [ANY] * 2,
-        out_specs=[VMEM] * 13 + [ANY] * 3,
+        in_specs=[pl.BlockSpec(memory_space=pltpu.SMEM)] + [VMEM] * 8 + [ANY] * 3,
+        out_specs=[VMEM] * 13 + [ANY] * 4,
         scratch_shapes=[
             pltpu.VMEM((tokens + 16, channels), f32), raws, raws,
             pltpu.VMEM((tokens, channels), f32), pltpu.VMEM((tokens, channels), f32),
@@ -398,6 +434,8 @@
             pltpu.SemaphoreType.DMA((8,)), pltpu.SemaphoreType.DMA((8,)),
             pltpu.VMEM(w_in.shape, bf16), pltpu.VMEM((tokens, width), bf16),
             pltpu.SemaphoreType.DMA((width // 512,)),
+            pltpu.VMEM(w_pairs.shape, bf16), pltpu.VMEM((width, 2 * w_pairs.shape[2]), bf16),
+            pltpu.SemaphoreType.DMA((9,)),
             *handing(count, states, channels).values(),
         ],
         compiler_params=pltpu.CompilerParams(
@@ -405,7 +443,7 @@
         ),
         cost_estimate=cost(6),
         name="mixer_forward",
-    )(bounds, stream, norm_gains, chan, logs, w_x, gains, w_dt, w_out, w_in, cot)
+    )(bounds, stream, norm_gains, chan, logs, w_x, gains, w_dt, w_out, w_in, cot, w_pairs)
     return out
 
 
@@ -1536,7 +1574,8 @@
         tail = tail + jnp.where(mine, flat[2:3, tail_at : tail_at + r.small.shape[1]], 0.0)
     r.gains[...] = gains
     r.small[...] = tail
-    r.rms[...] = jnp.sqrt(jnp.sum(flat[3:6], axis=1, keepdims=True) / cells)
+    totals = [jnp.sum(flat[3 + k : 4 + k], axis=1, keepdims=True) for k in range(3)]
+    r.rms[...] = jnp.sqrt(jnp.concatenate(totals, 1) / cells)
     for copy in copies:
         copy.wait()
 
@@ -1559,7 +1598,7 @@
         w_out=shape_of(*made.out_out.shape),
         w_gate_up=shape_of(rows_in, 2, hid),
         w_down=shape_of(*made.down_out.shape),
-        rms=shape_of(3, 1),
+        rms=shape_of(1, 3),
     )
     ins = vars(made)
     held = [
@@ -1612,15 +1651,15 @@
     w_in_flat = w_in.reshape(width, 2 * channels)
     (
         in_proj, one_in, halo, pre_conv, conv_low, raw_proj, step_pre, into, out_of, scan_out, gated_low,
-        last_state, mixer_low, before, one_came, cot_came,
+        last_state, mixer_low, before, one_came, cot_came, w_gate_up_flat,
     ) = mixer_forward(
         doc_bounds, stream, norm_gains, chan_vectors, decay_logs, w_x, small_gains[None], w_dt,
-        w_out, w_in_flat, cotangent, seq_count, 1,
+        w_out, w_in_flat, cotangent, w_gate_up, seq_count, 1,
     )
     mid = feed_forward(
         dict(stream=stream, mixer=mixer_low, gains=norm_gains),
         dict(
-            cot=cotangent, cot_came=cot_came, w_gate_up_in=w_gate_up.reshape(width, -1),
+            cot=cotangent, cot_came=cot_came, w_gate_up_in=w_gate_up_flat,
             w_down_in=w_down,
         ),
         seq_count,

time: 240 us -> 234 us (0.975)
  local copies, waits for them, and re-layouts: 11.7 us -> 6.36 us
    unnamed x6 -> x3, local copies, waits for them, and re-layouts: 10.8 us -> 5.44 us
where the time goes in v6:
time: 234 us; the launch traced here: 233 us
  Pallas kernels  226 us (97%)
  local copies, waits for them, and re-layouts  6.36 us (3%)
    pallas_call x1, Pallas kernels, backward(): pl.pallas_call(functools.partial(backward_kernel, bits, names), out_shape...  132 us
    pallas_call x1, Pallas kernels, mixer_forward(): pl.pallas_call(functools.partial(forward_kernel, bits), out_shape=[shape_...  57.2 us
    pallas_call x1, Pallas kernels, feed_forward(): pl.pallas_call(functools.partial(feed_forward_kernel, bits, names), out_s...  31.2 us
    pallas_call x1, Pallas kernels, finish(): pl.pallas_call(functools.partial(finish_kernel, cells, names), out_shape=...  6.18 us
    unnamed x3, local copies, waits for them, and re-layouts  5.44 us

profile of v6, /device:TPU:0, one launch (start us, length us, event | category | flops | bytes accessed | tf_op | source)
XLA Modules:
  0.0 233.4 jit_solution(14798983314935942085)
XLA Ops:
  0.6 5.4 %copy.27 = bf16[192,8,2,768]{3,1,2,0:T(8,128)(2,1)} copy(bf16[192,8,2,768]{3,2,1,0:T(2,128)(2,1)} %bitcast.9) | data formatting | bytes 9437184
  6.1 57.2 %mixer_forward.1 = (bf16[256,1536]{1,0:T(8,128)(2,1)}, bf16[2,2,2,192,256]{4,3,2,1,0:T(8,128)(2,1)}, bf16[16,768]{1,0:T(8,128)(2,1)}, f32[256,768]{1,0:T(8,128)}...) custom-call(s32[2]{0:T(128)} %refs_0_.3, ...), custom_call_target="tpu_custom_call" | custom-call | flops 6000000000 | bytes 6000000 | tf_op jit(solution)/shard_map/mixer_forward/pallas_call | solution.py:410
  63.3 0.0 copy-start
  63.3 31.2 %feed_forward.1 = (bf16[2,2,64,1536]{3,2,1,0:T(8,128)(2,1)}, bf16[2,2,64,1536]{3,2,1,0:T(8,128)(2,1)}, bf16[2,2,192,512]{3,2,1,0:T(8,128)(2,1)}, bf16[512,2048]{...) custom-call(bf16[256,1536]{1,0:T(8,128)(2,1)} %refs_1_.1, ...), custom_call_target="tpu_custom_call" | custom-call | tf_op jit(solution)/shard_map/feed_forward/pallas_call | solution.py:850
  94.4 0.0 copy-done
  94.5 0.9 copy.26
  95.4 131.7 %block_backward.1 = (f32[256,1536]{1,0:T(8,128)}, bf16[256,1536]{1,0:T(8,128)(2,1)}, f32[96,256]{1,0:T(8,128)}, f32[8,1536]{1,0:T(8,128)}, f32[128,1536]{1,0:T(8...) custom-call(s32[2]{0:T(128)} %refs_0_.3, ...), custom_call_target="tpu_custom_call" | custom-call | tf_op jit(solution)/shard_map/block_backward/pallas_call | solution.py:1519
  227.1 6.2 %finish.1 = (bf16[256,1536]{1,0:T(8,128)(2,1)}, f32[256,1536]{1,0:T(8,128)}, f32[2,192]{1,0:T(2,128)}, f32[192,2,768]{2,1,0:T(2,128)}, f32[7,96]{1,0:T(8,128)}, ...) custom-call(f32[256,1536]{1,0:T(8,128)} %get-tuple-element.86.refs_0, ...), custom_call_target="tpu_custom_call" | custom-call | tf_op jit(solution)/shard_map/finish/pallas_call | solution.py:1613
Async XLA Ops:
  63.3 31.2 %copy-start = (bf16[256,768]{1,0:T(8,128)(2,1)S(1)}, bf16[256,768]{1,0:T(8,128)(2,1)}, u32[]{:S(2)}) copy-start(bf16[256,768]{1,0:T(8,128)(2,1)} %get-tuple-element.79) | copy-start | bytes 1179652

commit v7 on v6

--- a/solution.py
+++ b/solution.py
@@ -163,7 +163,7 @@
 def forward_kernel(
     bits, bounds, stream, norm_gains, chan, logs, w_x, gains, w_dt, w_out, w_in, cot, w_pairs,
     proj, one_in, halo, pre_out, low_out, raw_out, step_pre_out, into, out_of, scan_out, gated_out, last_state,
-    mixer, hist_out, one_came, cot_came, w_flat,
+    mixer, turned_gate, hist_out, one_came, cot_came, w_flat,
     extended, raw_move, raw_land, step, drive, starts, part, first_land,
     second_move, second_land, hist, sends, receives, hist_sem, shared_sends, shared_receives,
     sum_sends, sum_receives, weights, normed, weight_sem, pairs, flat, pair_sems, *handed,
@@ -386,6 +386,8 @@
         lax.fori_loop(k * width // 512, (k + 1) * width // 512, mixed, 0)
         next(item)
     turns = in_turn(*sums)
+    for at in range(0, channels, 384):
+        turn(gated_out[:, at : at + 384], at, turned_gate)
     for count in (3, 8, 8, width):
         next(turns)
         if ahead[0] < width // CHUNK:
@@ -414,13 +416,15 @@
             shape_of(count // 4, 2, 2, width // count, tokens, dtype=bf16),
             shape_of(16, channels, dtype=bf16), rows, low_rows, shape_of(tokens, narrow), rows,
             wide, wide, rows, low_rows, shape_of(states, channels),
-            shape_of(2, 2, quarter, width, dtype=bf16), shape_of(tokens, states, channels),
+            shape_of(2, 2, quarter, width, dtype=bf16),
+            shape_of(count // 4, 2, 2, channels // count, tokens, dtype=bf16),
+            shape_of(tokens, states, channels),
             shape_of(count // 4, 2, width // count, tokens, dtype=bf16),
             shape_of(tokens, width, dtype=bf16),
             shape_of(width, 2 * w_pairs.shape[2], dtype=bf16),
         ],
         in_specs=[pl.BlockSpec(memory_space=pltpu.SMEM)] + [VMEM] * 8 + [ANY] * 3,
-        out_specs=[VMEM] * 13 + [ANY] * 4,
+        out_specs=[VMEM] * 14 + [ANY] * 4,
         scratch_shapes=[
             pltpu.VMEM((tokens + 16, channels), f32), raws, raws,
             pltpu.VMEM((tokens, channels), f32), pltpu.VMEM((tokens, channels), f32),
@@ -957,7 +961,14 @@
         for k, refs in enumerate((r.gate0, r.gate1, r.up0, r.up1))
     ]
     gate0, gate1, up0, up1 = quarters
-    out = unit(r.left_gated, r.right_out, (0, width), r.out, 6, r.out_out)
+    part = width // 2
+    outs = [
+        unit(
+            r.left_gated, r.right_out, (k * part, part), refs, 6 + 4 * k,
+            r.out_out.at[:, pl.ds(k * part, part)],
+        )
+        for k, refs in enumerate((r.out0, r.out1))
+    ]
     gin = unit(r.left_one, r.right_in, (channels, channels), r.gin, 7, r.gin_out)
     part = channels // 2
     cins = [
@@ -1104,7 +1115,9 @@
         lambda: (next(feed[0]), gate1.next()),
         lambda: next(feed[0]),
         lambda: (next(feed[0]), up0.next()),
-        lambda: (results(), out.made(gated_own, mixer_other, gated_other).go()),
+        lambda: (
+            results(), outs[0].made(gated_own, mixer_other, gated_other).go(), outs[1].made(),
+        ),
     ]
 
     def results_of(index, totals):
@@ -1226,6 +1239,7 @@
     tap_bias = lax.fori_loop(0, chunks, conv_back, jnp.zeros((1, channels), f32))
     copy = sent(r.grad_pre.at[pl.ds(0, 8)], r.grad_pre.at[pl.ds(tokens, 8)], r.raw_sends,
                 r.raw_receives, 2, "seq", previous)
+    outs[1].go()
     gin.go()
     r.extended[0:16] = r.halo[...].astype(f32)
 
@@ -1358,19 +1372,25 @@
     flat_sum = flat_summed()
     next(flat_sum)
 
+    outs[0].next()
     cins[0].made(cin_others[0]).go()
     next(one_sum)
     next(flat_sum)
-    out.next()
+    outs[1].next()
     cins[1].made(cin_others[1]).go()
     next(one_sum)
     next(flat_sum)
     small_columns()
     small_sum = small_summed()
     next(small_sum)
+    down_kept.wait()
+    down.next()
+    late.next()
     next(one_sum)
     gin.next()
+    gate0.next()
     next(flat_sum)
+    gate1.next()
     next(one_sum)
 
     def norm_one(index, _):
@@ -1387,14 +1407,13 @@
     next(small_sum)
     next(flat_sum)
     cins[1].next()
-    down_kept.wait()
-    for item in (down, late, *quarters):
+    for item in (up0, up1):
         item.next()
     next(small_sum)
     for waiting in (flat_sum, small_sum):
         for _ in waiting:
             pass
-    pending = [out, gin, *cins, down, late, *quarters]
+    pending = [*outs, gin, *cins, down, late, *quarters]
     for _ in range(len(bits)):
         for item in pending:
             item.next()
@@ -1488,18 +1507,19 @@
         gate1=unit(rows_in, hid // 2),
         up0=unit(rows_in, hid // 2),
         up1=unit(rows_in, hid // 2),
-        out=unit(rows_out, width),
+        out0=unit(rows_out, width // 2),
+        out1=unit(rows_out, width // 2),
         gin=unit(rows_in, channels),
         cin0=unit(rows_in, channels // 2),
         cin1=unit(rows_in, channels // 2),
         load_sems=sems(32),
-        write_sems=sems(10),
+        write_sems=sems(11),
         pair_sends=sems(8),
         pair_receives=sems(8),
         shared_sends=sems(4),
         shared_receives=sems(4),
-        unit_sends=sems(10 * n_bits),
-        unit_receives=sems(10 * n_bits),
+        unit_sends=sems(11 * n_bits),
+        unit_receives=sems(11 * n_bits),
         sum_sends=sems(16),
         sum_receives=sems(16),
         raw_sends=sems(3),
@@ -1645,13 +1665,10 @@
     tokens, width = stream.shape
     rank, (states, channels) = w_dt.shape[0], decay_logs.shape
 
-    def turned(values):
-        return values.T.reshape(seq_count // 4, 2, 2, values.shape[1] // seq_count, tokens)
-
     w_in_flat = w_in.reshape(width, 2 * channels)
     (
         in_proj, one_in, halo, pre_conv, conv_low, raw_proj, step_pre, into, out_of, scan_out, gated_low,
-        last_state, mixer_low, before, one_came, cot_came, w_gate_up_flat,
+        last_state, mixer_low, gated_in, before, one_came, cot_came, w_gate_up_flat,
     ) = mixer_forward(
         doc_bounds, stream, norm_gains, chan_vectors, decay_logs, w_x, small_gains[None], w_dt,
         w_out, w_in_flat, cotangent, w_gate_up, seq_count, 1,
@@ -1676,7 +1693,7 @@
             feed_part=mid.feed_part, left_two_in=mid.left_two, right_two_in=mid.right_two,
             down_away_in=mid.down_away, down_kept_in=mid.down_kept,
             late_away_in=mid.late_away, late_kept_in=mid.late_kept, mixer_in=mixer_low,
-            cot=cotangent, gated_in=turned(gated_low), one_in=one_in,
+            cot=cotangent, gated_in=gated_in, one_in=one_in,
             one_came=one_came, w_out=w_out, w_in=w_in_flat, scan_in=scan_out, into_in=into,
             out_of_in=out_of, hist_in=before,
         ),

time: 234 us -> 231 us (0.987)
    unnamed x3 -> x1, local copies, waits for them, and re-layouts: 5.44 us -> 5.43 us
where the time goes in v7:
time: 231 us
  Pallas kernels  225 us (97%)
  local copies, waits for them, and re-layouts  5.43 us (2%)
    pallas_call x1, Pallas kernels, backward(): pl.pallas_call(functools.partial(backward_kernel, bits, names), out_shape...  130 us
    pallas_call x1, Pallas kernels, mixer_forward(): pl.pallas_call(functools.partial(forward_kernel, bits), out_shape=[shape_...  57.3 us
    pallas_call x1, Pallas kernels, feed_forward(): pl.pallas_call(functools.partial(feed_forward_kernel, bits, names), out_s...  31.1 us
    pallas_call x1, Pallas kernels, finish(): pl.pallas_call(functools.partial(finish_kernel, cells, names), out_shape=...  6.18 us
    unnamed x1, local copies, waits for them, and re-layouts  5.43 us

profile of v7, /device:TPU:0, one launch (start us, length us, event | category | flops | bytes accessed | tf_op | source)
XLA Modules:
  0.0 230.9 jit_solution(2747042860029215065)
XLA Ops:
  0.6 5.4 %copy.26 = bf16[192,8,2,768]{3,1,2,0:T(8,128)(2,1)} copy(bf16[192,8,2,768]{3,2,1,0:T(2,128)(2,1)} %bitcast.7) | data formatting | bytes 9437184
  6.1 57.3 %mixer_forward.1 = (bf16[256,1536]{1,0:T(8,128)(2,1)}, bf16[2,2,2,192,256]{4,3,2,1,0:T(8,128)(2,1)}, bf16[16,768]{1,0:T(8,128)(2,1)}, f32[256,768]{1,0:T(8,128)}...) custom-call(s32[2]{0:T(128)} %refs_0_.3, ...), custom_call_target="tpu_custom_call" | custom-call | flops 6000000000 | bytes 6000000 | tf_op jit(solution)/shard_map/mixer_forward/pallas_call | solution.py:412
  63.4 31.1 %feed_forward.1 = (bf16[2,2,64,1536]{3,2,1,0:T(8,128)(2,1)}, bf16[2,2,64,1536]{3,2,1,0:T(8,128)(2,1)}, bf16[2,2,192,512]{3,2,1,0:T(8,128)(2,1)}, bf16[512,2048]{...) custom-call(bf16[256,1536]{1,0:T(8,128)(2,1)} %refs_1_.1, ...), custom_call_target="tpu_custom_call" | custom-call | tf_op jit(solution)/shard_map/feed_forward/pallas_call | solution.py:854
  94.4 130.1 %block_backward.1 = (f32[256,1536]{1,0:T(8,128)}, bf16[256,1536]{1,0:T(8,128)(2,1)}, f32[96,256]{1,0:T(8,128)}, f32[8,1536]{1,0:T(8,128)}, f32[128,1536]{1,0:T(8...) custom-call(s32[2]{0:T(128)} %refs_0_.3, ...), custom_call_target="tpu_custom_call" | custom-call | tf_op jit(solution)/shard_map/block_backward/pallas_call | solution.py:1539
  224.6 6.2 %finish.1 = (bf16[256,1536]{1,0:T(8,128)(2,1)}, f32[256,1536]{1,0:T(8,128)}, f32[2,192]{1,0:T(2,128)}, f32[192,2,768]{2,1,0:T(2,128)}, f32[7,96]{1,0:T(8,128)}, ...) custom-call(f32[256,1536]{1,0:T(8,128)} %get-tuple-element.86.refs_0, ...), custom_call_target="tpu_custom_call" | custom-call | tf_op jit(solution)/shard_map/finish/pallas_call | solution.py:1633

commit v8 on v7

--- a/solution.py
+++ b/solution.py
@@ -969,8 +969,14 @@
         )
         for k, refs in enumerate((r.out0, r.out1))
     ]
-    gin = unit(r.left_one, r.right_in, (channels, channels), r.gin, 7, r.gin_out)
     part = channels // 2
+    gins = [
+        unit(
+            r.left_one, r.right_in, (channels + k * part, part), refs, 7 + 4 * k,
+            r.gin_out.at[:, pl.ds(k * part, part)],
+        )
+        for k, refs in enumerate((r.gin0, r.gin1))
+    ]
     cins = [
         unit(
             r.left_one, r.right_in, (k * part, part), refs, 8 + k,
@@ -1197,7 +1203,8 @@
 
     lax.fori_loop(0, chunks, norm_grads, 0)
     copy = sent(r.raw_move.at[0], r.raw_land.at[0], r.raw_sends, r.raw_receives, 0, "ch", across)
-    gin.made(one_own, one_other, gin_other)
+    gins[0].made(one_own, one_other, gin_other)
+    gins[1].made()
     copy.wait()
     r.raw_move[1] = r.raw_move[0] + r.raw_land[0]
     copy = sent(r.raw_move.at[1], r.raw_land.at[1], r.raw_sends, r.raw_receives, 1, "ch", along)
@@ -1240,7 +1247,8 @@
     copy = sent(r.grad_pre.at[pl.ds(0, 8)], r.grad_pre.at[pl.ds(tokens, 8)], r.raw_sends,
                 r.raw_receives, 2, "seq", previous)
     outs[1].go()
-    gin.go()
+    gins[0].go()
+    gins[1].go()
     r.extended[0:16] = r.halo[...].astype(f32)
 
     def extend(index, _):
@@ -1383,11 +1391,12 @@
     small_columns()
     small_sum = small_summed()
     next(small_sum)
+    gins[0].next()
     down_kept.wait()
     down.next()
     late.next()
     next(one_sum)
-    gin.next()
+    gins[1].next()
     gate0.next()
     next(flat_sum)
     gate1.next()
@@ -1413,7 +1422,7 @@
     for waiting in (flat_sum, small_sum):
         for _ in waiting:
             pass
-    pending = [*outs, gin, *cins, down, late, *quarters]
+    pending = [*outs, *gins, *cins, down, late, *quarters]
     for _ in range(len(bits)):
         for item in pending:
             item.next()
@@ -1509,17 +1518,18 @@
         up1=unit(rows_in, hid // 2),
         out0=unit(rows_out, width // 2),
         out1=unit(rows_out, width // 2),
-        gin=unit(rows_in, channels),
+        gin0=unit(rows_in, channels // 2),
+        gin1=unit(rows_in, channels // 2),
         cin0=unit(rows_in, channels // 2),
         cin1=unit(rows_in, channels // 2),
         load_sems=sems(32),
-        write_sems=sems(11),
+        write_sems=sems(12),
         pair_sends=sems(8),
         pair_receives=sems(8),
         shared_sends=sems(4),
         shared_receives=sems(4),
-        unit_sends=sems(11 * n_bits),
-        unit_receives=sems(11 * n_bits),
+        unit_sends=sems(12 * n_bits),
+        unit_receives=sems(12 * n_bits),
         sum_sends=sems(16),
         sum_receives=sems(16),
         raw_sends=sems(3),

time: 231 us -> 231 us (level)
  no operation moved by 1% of the time
where the time goes in v8:
time: 231 us
  Pallas kernels  225 us (97%)
  local copies, waits for them, and re-layouts  5.43 us (2%)
    pallas_call x1, Pallas kernels, backward(): pl.pallas_call(functools.partial(backward_kernel, bits, names), out_shape...  130 us
    pallas_call x1, Pallas kernels, mixer_forward(): pl.pallas_call(functools.partial(forward_kernel, bits), out_shape=[shape_...  57.3 us
    pallas_call x1, Pallas kernels, feed_forward(): pl.pallas_call(functools.partial(feed_forward_kernel, bits, names), out_s...  31.1 us
    pallas_call x1, Pallas kernels, finish(): pl.pallas_call(functools.partial(finish_kernel, cells, names), out_shape=...  6.18 us
    unnamed x1, local copies, waits for them, and re-layouts  5.43 us

profile of v8, /device:TPU:0, one launch (start us, length us, event | category | flops | bytes accessed | tf_op | source)
XLA Modules:
  0.0 231.0 jit_solution(17201700243497509550)
XLA Ops:
  0.6 5.4 %copy.26 = bf16[192,8,2,768]{3,1,2,0:T(8,128)(2,1)} copy(bf16[192,8,2,768]{3,2,1,0:T(2,128)(2,1)} %bitcast.7) | data formatting | bytes 9437184
  6.1 57.3 %mixer_forward.1 = (bf16[256,1536]{1,0:T(8,128)(2,1)}, bf16[2,2,2,192,256]{4,3,2,1,0:T(8,128)(2,1)}, bf16[16,768]{1,0:T(8,128)(2,1)}, f32[256,768]{1,0:T(8,128)}...) custom-call(s32[2]{0:T(128)} %refs_0_.3, ...), custom_call_target="tpu_custom_call" | custom-call | flops 6000000000 | bytes 6000000 | tf_op jit(solution)/shard_map/mixer_forward/pallas_call | solution.py:412
  63.4 31.1 %feed_forward.1 = (bf16[2,2,64,1536]{3,2,1,0:T(8,128)(2,1)}, bf16[2,2,64,1536]{3,2,1,0:T(8,128)(2,1)}, bf16[2,2,192,512]{3,2,1,0:T(8,128)(2,1)}, bf16[512,2048]{...) custom-call(bf16[256,1536]{1,0:T(8,128)(2,1)} %refs_1_.1, ...), custom_call_target="tpu_custom_call" | custom-call | tf_op jit(solution)/shard_map/feed_forward/pallas_call | solution.py:854
  94.4 130.2 %block_backward.1 = (f32[256,1536]{1,0:T(8,128)}, bf16[256,1536]{1,0:T(8,128)(2,1)}, f32[96,256]{1,0:T(8,128)}, f32[8,1536]{1,0:T(8,128)}, f32[128,1536]{1,0:T(8...) custom-call(s32[2]{0:T(128)} %refs_0_.3, ...), custom_call_target="tpu_custom_call" | custom-call | tf_op jit(solution)/shard_map/block_backward/pallas_call | solution.py:1549
  224.6 6.2 %finish.1 = (bf16[256,1536]{1,0:T(8,128)(2,1)}, f32[256,1536]{1,0:T(8,128)}, f32[2,192]{1,0:T(2,128)}, f32[192,2,768]{2,1,0:T(2,128)}, f32[7,96]{1,0:T(8,128)}, ...) custom-call(f32[256,1536]{1,0:T(8,128)} %get-tuple-element.86.refs_0, ...), custom_call_target="tpu_custom_call" | custom-call | tf_op jit(solution)/shard_map/finish/pallas_call | solution.py:1643
